TPU v7x, 32 devices: a whole 2x2x4 slice. The times are simulated.
32 devices in a mesh: dp: 2 (over core), seq: 16 (over z, y, x).
Axes of the slice: x: 2, y: 2, z: 4, core: 2. Of those that a mesh axis runs over, the one named last changes fastest.
Arguments:
- block_input: bfloat16 [2, 2048, 2048], P('dp', 'seq'), may hold values from -6 to 6
- segments: int32 [2, 2048], P('dp', 'seq'), may hold values from 0 to 3, as said below
- mix_gain: float32 [2048], P(('dp', 'seq')), may hold values from 0.5 to 1.5
- w_project: float32 [2048, 6144], P(('dp', 'seq')), may hold values from -0.125 to 0.125
- conv_taps: float32 [4, 6144], P(None, ('dp', 'seq')), may hold values from -3 to 3
- w_beta: float32 [2048, 16], P(('dp', 'seq')), may hold values from -0.125 to 0.125
- w_gate: float32 [2048, 2048], P(('dp', 'seq')), may hold values from -0.125 to 0.125
- head_gain: float32 [2048], P(('dp', 'seq')), may hold values from 0.5 to 1.5
- w_output: float32 [2048, 2048], P(('dp', 'seq')), may hold values from -0.1875 to 0.1875
- ffn_gain: float32 [2048], P(('dp', 'seq')), may hold values from 0.5 to 1.5
- w_hidden_gate: float32 [2048, 5632], P(('dp', 'seq')), may hold values from -0.125 to 0.125
- w_hidden_up: float32 [2048, 5632], P(('dp', 'seq')), may hold values from -0.125 to 0.125
- w_hidden_down: float32 [5632, 2048], P(('dp', 'seq')), may hold values from -0.109375 to 0.109375
- cotangent: bfloat16 [2, 2048, 2048], P('dp', 'seq'), may hold values from -6 to 6
Outputs:
- block_output: bfloat16 [2, 2048, 2048], P('dp', 'seq')
- grad_input: float32 [2, 2048, 2048], P('dp', 'seq')
- grad_mix_gain: float32 [2048], P(('dp', 'seq'))
- grad_project: float32 [2048, 6144], P(('dp', 'seq'))
- grad_conv_taps: float32 [4, 6144], P(None, ('dp', 'seq'))
- grad_beta: float32 [2048, 16], P(('dp', 'seq'))
- grad_gate: float32 [2048, 2048], P(('dp', 'seq'))
- grad_head_gain: float32 [2048], P(('dp', 'seq'))
- grad_output: float32 [2048, 2048], P(('dp', 'seq'))
- grad_ffn_gain: float32 [2048], P(('dp', 'seq'))
- grad_hidden_gate: float32 [2048, 5632], P(('dp', 'seq'))
- grad_hidden_up: float32 [2048, 5632], P(('dp', 'seq'))
- grad_hidden_down: float32 [5632, 2048], P(('dp', 'seq'))
Inputs may be any that keep to these rules, and one draw needn't show every extreme that they name: In every row the ids never fall; segment 1 begins within the first 128 slots and ends within the last 128 slots; segments 0, 2 and 3 each hold at least one slot.
All inputs are finite; a program needn't handle non-finite values.
Results may differ from a plain program's by a relative error of at most 0.015.
The roundings to bfloat16 on the way count: a program that leaves them out, or rounds other values in their place, can miss the bound.
Values may be sent and summed in bfloat16 or wider, within the bound.
No kernel may reach another device: no remote copies, remote signals or barrier semaphores. Data moves between devices by JAX's collectives and lax.ppermute only.
A program may use at most 512 MiB of HBM per device.

v0:
```python
import jax
import jax.numpy as jnp
from jax import lax
from jax.sharding import PartitionSpec as P

D = 2048
H = 16
HEAD = 128
CONV = 4
GROUP = 64


EPS = 1e-06
HEAD_EPS = 0.01
HIGH = lax.Precision.HIGHEST


def from_behind(block, axis, distance):
    devices = range(lax.axis_size(axis))
    route = [(i - distance, i) for i in devices if i - distance in devices]
    return lax.ppermute(block, axis, route)


def carried_in(value, axis, join, neutral, backward):
    count = lax.axis_size(axis)
    place = lax.axis_index(axis)
    ahead = count - 1 - place if backward else place
    gathered = jax.tree.map(
        lambda a, kind: lax.all_gather(a.astype(kind), axis),
        value,
        jax.tree.map(lambda a: jnp.bfloat16 if a.dtype == jnp.float32 else a.dtype, value),
    )
    state = jax.tree.map(lambda a, e: jnp.zeros_like(a) + jnp.asarray(e, a.dtype), value, neutral)

    def one(lap, state):
        source = count - 1 - lap if backward else lap
        return join(
            state,
            jax.tree.map(
                lambda a, own: lax.dynamic_index_in_dim(a, source, 0, False).astype(own.dtype),
                gathered,
                value,
            ),
        )

    return lax.fori_loop(0, ahead, one, state)


def rms_scale(values, gain):
    return values * lax.rsqrt(jnp.mean(values * values, axis=-1, keepdims=True) + EPS) * gain


def head_scale(values, gain):
    return values * lax.rsqrt(jnp.mean(values * values, axis=-1, keepdims=True) + HEAD_EPS) * gain


def unit_rows(values):
    return values * lax.rsqrt(jnp.sum(values * values, axis=-1, keepdims=True) + EPS)


def dot_low(left, right):
    return jnp.dot(left, right, preferred_element_type=jnp.float32)


def dot_left_t(left, right):
    return lax.dot_general(
        left, right, (((0,), (0,)), ((), ())), preferred_element_type=jnp.float32
    )


def dot_right_t(left, right):
    return lax.dot_general(
        left, right, (((1,), (1,)), ((), ())), preferred_element_type=jnp.float32
    )


def compose(earlier, later):
    first = jnp.einsum("hij,hjk->hik", earlier[0], later[0], precision=HIGH)
    second = jnp.einsum("hvj,hjk->hvk", earlier[1], later[0], precision=HIGH) + later[1]
    return (first, second)


def conv_act(extended, taps, same_masks):
    count = same_masks.shape[1]
    total = jnp.zeros((count, extended.shape[1]), jnp.float32)
    for tap in range(CONV):
        total = total + taps[tap] * extended[tap : tap + count] * same_masks[tap][:, None]
    active = jax.nn.silu(total)
    query = unit_rows(active[:, :D].reshape(count, H, HEAD))
    key = unit_rows(active[:, D : 2 * D].reshape(count, H, HEAD))
    value = active[:, 2 * D :].reshape(count, H, HEAD)
    return (query, key, value)


def group_prep(query, key, value, strength, masks):
    same_lower, same_incl, carry_in, keep_end, keep_last = masks
    blocks = query.shape[0] // GROUP

    def split_blocks(values):
        return jnp.swapaxes(values.reshape((blocks, GROUP) + values.shape[1:]), 1, 2)

    query_c, key_c, value_c = (split_blocks(query), split_blocks(key), split_blocks(value))
    weight_c = split_blocks(strength)
    gram = jnp.einsum("nhck,nhdk->nhcd", key_c, key_c, precision=HIGH)
    system = jnp.eye(GROUP, dtype=jnp.float32) + weight_c[..., None] * gram * same_lower[:, None]
    weighted = jnp.concatenate(
        [weight_c[..., None] * value_c, (weight_c * carry_in[:, None])[..., None] * key_c], -1
    )
    solved = lax.linalg.triangular_solve(system, weighted, left_side=True, lower=True)
    solved_v = solved[..., :HEAD]
    solved_k = solved[..., HEAD:]
    scores = jnp.einsum("nhck,nhdk->nhcd", query_c, key_c, precision=HIGH) * same_incl[:, None]
    ending = key_c * keep_end[:, None, :, None]
    trans_a = keep_last[:, None, None, None] * jnp.eye(HEAD, dtype=jnp.float32) - jnp.einsum(
        "nhci,nhcj->nhij", solved_k, ending, precision=HIGH
    )
    trans_b = jnp.einsum("nhcv,nhck->nhvk", solved_v, ending, precision=HIGH)
    return (scores, solved_v, solved_k, query_c, trans_a, trans_b)


def group_run(prepared, state_in, carry_in):
    scores, solved_v, solved_k, query_c, trans_a, trans_b = prepared

    def advance(state, item):
        score, upd_v, upd_k, query_b, carried, map_a, map_b = item
        delta = upd_v - jnp.einsum("hck,hvk->hcv", upd_k, state, precision=HIGH)
        output = carried[None, :, None] * jnp.einsum(
            "hck,hvk->hcv", query_b, state, precision=HIGH
        ) + jnp.einsum("hcd,hdv->hcv", score, delta, precision=HIGH)
        state = jnp.einsum("hvk,hkj->hvj", state, map_a, precision=HIGH) + map_b
        return (state, output)

    state_out, outputs = lax.scan(
        advance, state_in, (scores, solved_v, solved_k, query_c, carry_in, trans_a, trans_b)
    )
    return (outputs, state_out)


def gated_norm(recalled, gain, gate):
    count = recalled.shape[0]
    heads_gate = gate.reshape(count, H, HEAD)
    return (head_scale(recalled, gain.reshape(H, HEAD)) * jax.nn.silu(heads_gate)).reshape(count, D)


def swiglu(gate_two, up_two):
    return jax.nn.silu(gate_two) * up_two


def local(
    block_input,
    segments,
    mix_gain,
    w_project,
    conv_taps,
    w_beta,
    w_gate,
    head_gain,
    w_output,
    ffn_gain,
    w_hidden_gate,
    w_hidden_up,
    w_hidden_down,
    cotangent,
):
    half_type = jnp.bfloat16
    gain_low = mix_gain.astype(half_type)
    proj_low = w_project.astype(half_type)
    taps_low = conv_taps.astype(half_type)
    beta_low = w_beta.astype(half_type)
    gate_low = w_gate.astype(half_type)
    hgain_low = head_gain.astype(half_type)
    oproj_low = w_output.astype(half_type)
    fgain_low = ffn_gain.astype(half_type)
    hgate_low = w_hidden_gate.astype(half_type)
    hup_low = w_hidden_up.astype(half_type)
    hdown_low = w_hidden_down.astype(half_type)
    full = (
        lax.all_gather(gain_low, ("dp", "seq"), axis=0, tiled=True),
        lax.all_gather(proj_low, ("dp", "seq"), axis=0, tiled=True),
        lax.all_gather(taps_low, ("dp", "seq"), axis=1, tiled=True),
        lax.all_gather(beta_low, ("dp", "seq"), axis=0, tiled=True),
        lax.all_gather(gate_low, ("dp", "seq"), axis=0, tiled=True),
        lax.all_gather(hgain_low, ("dp", "seq"), axis=0, tiled=True),
        lax.all_gather(oproj_low, ("dp", "seq"), axis=0, tiled=True),
        lax.all_gather(fgain_low, ("dp", "seq"), axis=0, tiled=True),
        lax.all_gather(hgate_low, ("dp", "seq"), axis=0, tiled=True),
        lax.all_gather(hup_low, ("dp", "seq"), axis=0, tiled=True),
        lax.all_gather(hdown_low, ("dp", "seq"), axis=0, tiled=True),
    )
    (
        gain_one,
        proj_in,
        taps_full,
        beta_full,
        gate_full,
        gain_head,
        proj_out,
        gain_two,
        hidden_gate,
        hidden_up,
        hidden_down,
    ) = full
    residual = block_input[0].astype(jnp.float32)
    seg_local = segments[0]
    count = residual.shape[0]
    blocks = count // GROUP
    normed_f, mix_pull = jax.vjp(rms_scale, residual, gain_one.astype(jnp.float32))
    normed = normed_f.astype(half_type)
    projected = dot_low(normed, proj_in).astype(half_type)
    logits = dot_low(normed, beta_full)
    gate_pre = dot_low(normed, gate_full)
    rim_values, rim_ids = from_behind(
        (projected[count - (CONV - 1) :], seg_local[count - (CONV - 1) :].astype(half_type)),
        "seq",
        1,
    )
    rim_seg = rim_ids.astype(jnp.int32)
    extended = jnp.concatenate([rim_values, projected], 0).astype(jnp.float32)
    ext_seg = jnp.concatenate([rim_seg, seg_local], 0)
    same_masks = jnp.stack(
        [(ext_seg[tap : tap + count] == seg_local).astype(jnp.float32) for tap in range(CONV)]
    )
    (query, key, value), conv_pull = jax.vjp(
        lambda ext_rows, taps: conv_act(ext_rows, taps, same_masks),
        extended,
        taps_full.astype(jnp.float32),
    )
    strength = jax.nn.sigmoid(logits)
    seg_blocks = seg_local.reshape(blocks, GROUP)
    before = jnp.concatenate([rim_seg[CONV - 2 :], seg_blocks[:-1, -1]], 0)
    row_index = lax.broadcasted_iota(jnp.int32, (GROUP, GROUP), 0)
    column_index = lax.broadcasted_iota(jnp.int32, (GROUP, GROUP), 1)
    same_seg = seg_blocks[:, :, None] == seg_blocks[:, None, :]
    same_lower = (same_seg & (column_index < row_index)[None]).astype(jnp.float32)
    same_incl = (same_seg & (column_index <= row_index)[None]).astype(jnp.float32)
    carry_in = (seg_blocks == before[:, None]).astype(jnp.float32)
    keep_end = (seg_blocks == seg_blocks[:, -1:]).astype(jnp.float32)
    masks = (same_lower, same_incl, carry_in, keep_end, carry_in[:, -1])
    prepared, prep_pull = jax.vjp(
        lambda queries, keys_in, values_in, strengths: group_prep(
            queries, keys_in, values_in, strengths, masks
        ),
        query,
        key,
        value,
        strength,
    )
    identity = (
        jnp.broadcast_to(jnp.eye(HEAD, dtype=jnp.float32), (H, HEAD, HEAD)),
        jnp.zeros((H, HEAD, HEAD), jnp.float32),
    )

    def fold_maps(carry, item):
        return (compose(carry, item), None)

    device_maps, unused = lax.scan(fold_maps, identity, (prepared[4], prepared[5]))
    entering = carried_in(device_maps, "seq", compose, identity, False)
    state_in = entering[1]
    (outputs, state_out), run_pull = jax.vjp(
        lambda prep, state: group_run(prep, state, carry_in), prepared, state_in
    )
    recalled = jnp.swapaxes(outputs, 1, 2).reshape(count, H, HEAD)
    scaled_f, gated_pull = jax.vjp(gated_norm, recalled, gain_head.astype(jnp.float32), gate_pre)
    scaled = scaled_f.astype(half_type)
    middle = residual + dot_low(scaled, proj_out)
    normed_two_f, ffn_pull = jax.vjp(rms_scale, middle, gain_two.astype(jnp.float32))
    normed_two = normed_two_f.astype(half_type)
    gate_two = dot_low(normed_two, hidden_gate)
    up_two = dot_low(normed_two, hidden_up)
    hidden_f, glu_pull = jax.vjp(swiglu, gate_two, up_two)
    hidden = hidden_f.astype(half_type)
    result = middle + dot_low(hidden, hidden_down)
    block_output = result.astype(half_type)[None]
    upstream = cotangent[0]
    grad_down = dot_left_t(hidden, upstream)
    grad_hidden = dot_right_t(upstream, hidden_down)
    grad_gate_two, grad_up_two = glu_pull(grad_hidden)
    grad_gate_two = grad_gate_two.astype(half_type)
    grad_up_two = grad_up_two.astype(half_type)
    grad_normed_two = dot_right_t(grad_gate_two, hidden_gate) + dot_right_t(grad_up_two, hidden_up)
    grad_middle, grad_fgain = ffn_pull(grad_normed_two)
    grad_middle = grad_middle + upstream.astype(jnp.float32)
    grad_hgate = dot_left_t(normed_two, grad_gate_two)
    grad_hup = dot_left_t(normed_two, grad_up_two)
    ffn_sums = (
        lax.psum_scatter(grad_fgain, ("dp", "seq"), scatter_dimension=0, tiled=True),
        lax.psum_scatter(grad_hgate, ("dp", "seq"), scatter_dimension=0, tiled=True),
        lax.psum_scatter(grad_hup, ("dp", "seq"), scatter_dimension=0, tiled=True),
        lax.psum_scatter(grad_down, ("dp", "seq"), scatter_dimension=0, tiled=True),
    )
    grad_branch = grad_middle.astype(half_type)
    grad_oproj = dot_left_t(scaled, grad_branch)
    grad_scaled = dot_right_t(grad_branch, proj_out)
    grad_recalled, grad_hgain, grad_gate_pre = gated_pull(grad_scaled)
    grad_gate_pre = grad_gate_pre.astype(half_type)
    grad_wgate = dot_left_t(normed, grad_gate_pre)
    grad_normed = dot_right_t(grad_gate_pre, gate_full)
    grad_outputs = jnp.swapaxes(grad_recalled.reshape(blocks, GROUP, H, HEAD), 1, 2)
    zero_state = jnp.zeros((H, HEAD, HEAD), jnp.float32)
    local_term = run_pull((grad_outputs, zero_state))[1]
    leaving = carried_in(
        (jnp.swapaxes(device_maps[0], 1, 2), local_term), "seq", compose, identity, True
    )
    grad_prepared, unused_state = run_pull((grad_outputs, leaving[1]))
    grad_query, grad_key, grad_value, grad_strength = prep_pull(grad_prepared)
    grad_logits = grad_strength * strength * (1.0 - strength)
    grad_wbeta = jnp.dot(normed.astype(jnp.float32).T, grad_logits, precision=HIGH)
    grad_normed = grad_normed + jnp.dot(
        grad_logits, beta_full.astype(jnp.float32).T, precision=HIGH
    )
    grad_extended, grad_taps = conv_pull((grad_query, grad_key, grad_value))
    from_next = from_behind(grad_extended[: CONV - 1].astype(jnp.bfloat16), "seq", -1).astype(
        jnp.float32
    )
    grad_projected = grad_extended[CONV - 1 :] + jnp.pad(
        from_next, ((count - (CONV - 1), 0), (0, 0))
    )
    grad_projected = grad_projected.astype(half_type)
    grad_wproj = dot_left_t(normed, grad_projected)
    grad_normed = grad_normed + dot_right_t(grad_projected, proj_in)
    grad_tokens, grad_mgain = mix_pull(grad_normed)
    grad_input = (grad_tokens + grad_middle)[None]
    mix_sums = (
        lax.psum_scatter(grad_mgain, ("dp", "seq"), scatter_dimension=0, tiled=True),
        lax.psum_scatter(grad_wproj, ("dp", "seq"), scatter_dimension=0, tiled=True),
        lax.psum_scatter(grad_taps, ("dp", "seq"), scatter_dimension=1, tiled=True),
        lax.psum_scatter(grad_wbeta, ("dp", "seq"), scatter_dimension=0, tiled=True),
        lax.psum_scatter(grad_wgate, ("dp", "seq"), scatter_dimension=0, tiled=True),
        lax.psum_scatter(grad_hgain, ("dp", "seq"), scatter_dimension=0, tiled=True),
        lax.psum_scatter(grad_oproj, ("dp", "seq"), scatter_dimension=0, tiled=True),
    )
    return (
        block_output,
        grad_input,
        mix_sums[0],
        mix_sums[1],
        mix_sums[2],
        mix_sums[3],
        mix_sums[4],
        mix_sums[5],
        mix_sums[6],
        ffn_sums[0],
        ffn_sums[1],
        ffn_sums[2],
        ffn_sums[3],
    )


def solution(mesh):
    in_specs = (
        P("dp", "seq", None),
        P("dp", "seq"),
        P(("dp", "seq")),
        P(("dp", "seq"), None),
        P(None, ("dp", "seq")),
        P(("dp", "seq"), None),
        P(("dp", "seq"), None),
        P(("dp", "seq")),
        P(("dp", "seq"), None),
        P(("dp", "seq")),
        P(("dp", "seq"), None),
        P(("dp", "seq"), None),
        P(("dp", "seq"), None),
        P("dp", "seq", None),
    )
    out_specs = (
        P("dp", "seq", None),
        P("dp", "seq", None),
        P(("dp", "seq")),
        P(("dp", "seq"), None),
        P(None, ("dp", "seq")),
        P(("dp", "seq"), None),
        P(("dp", "seq"), None),
        P(("dp", "seq")),
        P(("dp", "seq"), None),
        P(("dp", "seq")),
        P(("dp", "seq"), None),
        P(("dp", "seq"), None),
        P(("dp", "seq"), None),
    )
    return jax.shard_map(local, mesh=mesh, in_specs=in_specs, out_specs=out_specs, check_vma=False)
```

profile of v0, /device:TPU:0, one launch (start us, length us, event | category | flops | bytes accessed | tf_op | source)
XLA Modules:
  0.0 5920.3 jit_solution(10731547332766033391)
XLA Ops:
  12.0 4.8 collective-permute-start
  17.6 41.9 all-reduce.21
  59.6 68.1 %all-gather.5 = bf16[32,192,4]{1,2,0:T(4,128)(2,1)S(1)} all-gather(bf16[1,192,4]{1,2,0:T(4,128)(2,1)S(1)} %convert_bitcast_fusion.2), channel_id=1, replica_groups=mesh['dp'=2,'seq'=16] {'dp','seq'}, dimensions={0}, use_global_device_ids=true | all-gather | bytes 50688 | tf_op jit(solution)/shard_map/all_gather | solution.py:180
  128.4 65.5 %all-gather.4 = bf16[32,64,16]{1,2,0:T(8,128)(2,1)S(1)} all-gather(bf16[1,64,16]{1,2,0:T(8,128)(2,1)S(1)} %convert_bitcast_fusion.1), channel_id=1, replica_groups=mesh['dp'=2,'seq'=16] {'dp','seq'}, dimensions={0}, use_global_device_ids=true | all-gather | bytes 67584 | tf_op jit(solution)/shard_map/all_gather | solution.py:181
  198.8 12.0 convolution_convert_fusion
  210.8 4.7 collective-permute-start.1
  217.4 3.4 fusion.100
  230.4 158.0 %custom-call.7 = f32[2,16,1,64,64]{3,4,2,1,0:T(8,128)S(1)} custom-call(f32[2,16,1,64,64]{4,3,2,1,0:T(8,128)} %select_bitcast_fusion), custom_call_target="InvertDiagBlocksLowerTriangular" | custom-call | tf_op jit(solution)/shard_map/jvp()/triangular_solve | solution.py:109
  392.6 5.2 convolution_subtract_fusion.1
  400.0 6.4 fusion.170
  407.5 13.7 while.102
  408.8 3.3 fusion.359
  415.6 3.3 fusion.359
  435.0 12.3 copy.318
  463.7 72.0 %all-gather.29.cloned.1.call-done = bf16[256,128,128]{2,1,0:T(8,128)(2,1)} async-done(((bf16[16,128,128]{2,1,0:T(8,128)(2,1)}), bf16[256,128,128]{2,1,0:T(8,128)(2,1)}) %all-gather.29.cloned.1.call-update) | async-done | bytes 8388624 | tf_op jit(solution)/shard_map/all_gather | solution.py:29
  535.7 114.3 %all-gather.31.cloned.1.call-done = bf16[256,128,128]{2,1,0:T(8,128)(2,1)} async-done(((bf16[16,128,128]{2,1,0:T(8,128)(2,1)}), bf16[256,128,128]{2,1,0:T(8,128)(2,1)}) %all-gather.31.cloned.1.call-update) | async-done | bytes 8388624 | tf_op jit(solution)/shard_map/all_gather | solution.py:29
  652.8 16.3 while.99
  673.1 6.8 multiply_convert_fusion.3
  680.0 48.5 all-gather.21.cloned.1.call-done
  728.5 4.7 multiply_reduce_fusion.11
  733.5 141.0 %all-gather.23.cloned.1.call-done = bf16[2048,5632]{1,0:T(8,128)(2,1)} async-done(((bf16[64,5632]{1,0:T(8,128)(2,1)}), bf16[2048,5632]{1,0:T(8,128)(2,1)}) %all-gather.23.cloned.1.call-update) | async-done | bytes 23068688 | tf_op jit(solution)/shard_map/all_gather | solution.py:186
  874.5 12.3 fusion.224
  886.8 133.4 %all-gather.25.cloned.1.call-done = bf16[2048,5632]{1,0:T(8,128)(2,1)} async-done(((bf16[64,5632]{1,0:T(8,128)(2,1)}), bf16[2048,5632]{1,0:T(8,128)(2,1)}) %all-gather.25.cloned.1.call-update) | async-done | bytes 23068688 | tf_op jit(solution)/shard_map/all_gather | solution.py:187
  1020.2 12.3 fusion.225
  1032.5 133.4 %all-gather.27.cloned.1.call-done = bf16[5632,2048]{1,0:T(8,128)(2,1)} async-done(((bf16[176,2048]{1,0:T(8,128)(2,1)}), bf16[5632,2048]{1,0:T(8,128)(2,1)}) %all-gather.27.cloned.1.call-update) | async-done | bytes 23068688 | tf_op jit(solution)/shard_map/all_gather | solution.py:188
  1165.9 15.2 multiply_convert_fusion
  1181.1 13.4 fusion.226
  1194.5 13.6 multiply_reduce_fusion.4
  1208.5 6.2 fusion.189
  1219.1 16.2 while.103
  1237.8 42.2 all-gather.33.cloned.1.call-done
  1280.0 114.2 %all-gather.35.cloned.1.call-done = bf16[256,128,128]{2,1,0:T(8,128)(2,1)} async-done(((bf16[16,128,128]{2,1,0:T(8,128)(2,1)}), bf16[256,128,128]{2,1,0:T(8,128)(2,1)}) %all-gather.35.cloned.1.call-update) | async-done | bytes 8388624 | tf_op jit(solution)/shard_map/all_gather | solution.py:29
  1394.3 90.5 %while.100 = (s32[]{:T(128)}, f32[16,128,128]{1,2,0:T(8,128)S(1)}, s32[]{:T(128)}, bf16[16,16,128,128]{3,2,1,0:T(8,128)(2,1)}, bf16[16,16,128,128]{3,2,1,0:T(8,1...) while((s32[]{:T(128)}, f32[16,128,128]{1,2,0:T(8,128)S(1)}, s32[]{:T(128)}, ...), condition=%wide.region_16.17_spmd, body=%wide.region_15.16_spmd.sunk | while | flops 403177472 | bytes 7340179 | solution.py:46
  1492.5 43.3 while.101
  1497.6 3.9 fusion.354
  1503.6 3.8 fusion.352
  1507.4 3.8 fusion.353
  1519.1 3.9 fusion.354
  1525.0 3.8 fusion.352
  1528.9 3.8 fusion.353
  1535.8 7.2 fusion.211
  1545.5 4.3 fusion.117
  1553.1 3.4 fusion.115
  1561.4 4.4 fusion.128
  1568.1 3.4 fusion.125
  1585.7 4.3 multiply_reduce_fusion.3
  1594.4 8.2 fusion.187
  1603.7 8.3 fusion.177
  1618.1 4.7 collective-permute-done.2
  1622.8 21.0 fusion.191
  1643.9 19.8 fusion.228
  1663.7 19.7 fusion.229
  1683.5 19.3 fusion.171
  1702.8 6.7 fusion.227
  1709.5 11.8 fusion.106
  1722.9 15.1 fusion.141
  1738.0 37.5 all-reduce.20
  1781.8 47.7 reduce-scatter.27.cloned.1.call-done
  1830.9 355.5 %reduce-scatter.17.cloned.1.call-done = f32[64,2048]{1,0:T(8,128)} async-done(((f32[2048,2048]{1,0:T(8,128)}), f32[64,2048]{1,0:T(8,128)}) %reduce-scatter.17.cloned.1.call-update) | async-done | bytes 524304 | tf_op jit(solution)/shard_map/reduce_scatter | solution.py:330
  2186.5 362.9 %reduce-scatter.15.cloned.1.call-done = f32[64,2048]{1,0:T(8,128)} async-done(((f32[2048,2048]{1,0:T(8,128)}), f32[64,2048]{1,0:T(8,128)}) %reduce-scatter.15.cloned.1.call-update) | async-done | bytes 524304 | tf_op jit(solution)/shard_map/reduce_scatter | solution.py:328
  2549.4 440.7 %reduce-scatter.13.cloned.1.call-done = f32[64,6144]{1,0:T(8,128)} async-done(((f32[2048,6144]{1,0:T(8,128)}), f32[64,6144]{1,0:T(8,128)}) %reduce-scatter.13.cloned.1.call-update) | async-done | bytes 1572880 | tf_op jit(solution)/shard_map/reduce_scatter | solution.py:325
  2990.1 969.2 %reduce-scatter.19.cloned.1.call-done = f32[64,5632]{1,0:T(8,128)} async-done(((f32[2048,5632]{1,0:T(8,128)}), f32[64,5632]{1,0:T(8,128)}) %reduce-scatter.19.cloned.1.call-update) | async-done | bytes 1441808 | tf_op jit(solution)/shard_map/reduce_scatter | solution.py:287
  3959.3 977.0 %reduce-scatter.21.cloned.1.call-done = f32[64,5632]{1,0:T(8,128)} async-done(((f32[2048,5632]{1,0:T(8,128)}), f32[64,5632]{1,0:T(8,128)}) %reduce-scatter.21.cloned.1.call-update) | async-done | bytes 1441808 | tf_op jit(solution)/shard_map/reduce_scatter | solution.py:288
  4936.3 977.0 %reduce-scatter.23.cloned.1.call-done = f32[176,2048]{1,0:T(8,128)} async-done(((f32[5632,2048]{1,0:T(8,128)}), f32[176,2048]{1,0:T(8,128)}) %reduce-scatter.23.cloned.1.call-update) | async-done | bytes 1441808 | tf_op jit(solution)/shard_map/reduce_scatter | solution.py:289
  (630 shorter events, 277.2 us)
Async XLA Ops:
  7.2 52.3 copy-start.133
  7.2 121.2 %copy-start.128 = (f32[64,16]{0,1:T(8,128)S(1)}, f32[64,16]{0,1:T(8,128)}, u32[]{:S(2)}) copy-start(f32[64,16]{0,1:T(8,128)} %param.31) | copy-start | bytes 12292
  7.3 186.9 %copy-start.15 = (bf16[1,128,2048]{2,1,0:T(8,128)(2,1)S(1)}, bf16[1,128,2048]{2,1,0:T(8,128)(2,1)}, u32[]{:S(2)}) copy-start(bf16[1,128,2048]{2,1,0:T(8,128)(2,1)} %param.26) | copy-start | bytes 1572868
  7.3 191.5 %all-gather.17.cloned.1.call-start = ((), (), s32[]{:S(2)}) async-start(), calls=%async_computation.8 | async-start | bytes 25952256 | tf_op jit(solution)/shard_map/all_gather | solution.py:179
  9.9 425.2 %all-gather.19.cloned.1.call-start = ((), (), s32[]{:S(2)}) async-start(), calls=%async_computation.9 | async-start | bytes 8650752 | tf_op jit(solution)/shard_map/all_gather | solution.py:182
  10.7 525.1 %all-gather.29.cloned.1.call-start = ((), (), s32[]{:S(2)}) async-start(), calls=%async_computation.20 | async-start | bytes 8912896 | tf_op jit(solution)/shard_map/all_gather | solution.py:29
  12.0 184.0 %collective-permute-start = (bf16[3]{0:T(256)(128)(2,1)S(1)}, bf16[3]{0:T(256)(128)(2,1)S(1)}, u32[]{:S(2)}, u32[]{:S(2)}) collective-permute-start(bf16[3]{0:T(256)(128)(2,1)S(1)} %slice_bitcast_fusion.3), channel_id=1, source_target_pairs={{0,1},{1,2},{2,3},{3,4},{4,5},{5,6},{6,7},{7,8},{8,9},{9,10},{10,1... | collective-permute-start | bytes 26 | tf_op jit(solution)/shard_map/ppermute | solution.py:21
  59.5 613.6 %copy-start.74 = (f32[2048]{0:T(1024)}, f32[2048]{0:T(1024)S(1)}, u32[]{:S(2)}) copy-start(f32[2048]{0:T(1024)S(1)} %convert_element_type.214) | copy-start | bytes 24580
  194.2 16.6 copy-start.81
  194.4 16.4 copy-start.136
  194.4 16.4 copy-start.112
  194.7 16.0 copy-start.93
  194.8 193.6 %copy-start.78 = (f32[2,64,16]{1,2,0:T(8,128)}, f32[2,64,16]{1,2,0:T(8,128)S(1)}, u32[]{:S(2)}) copy-start(f32[2,64,16]{1,2,0:T(8,128)S(1)} %copy.486) | copy-start | bytes 24580
  195.8 31.5 copy-start.96
  195.9 31.5 copy-start.76
  195.9 256.0 %copy-start.72 = (f32[2,64,64]{2,1,0:T(8,128)}, f32[2,64,64]{2,1,0:T(8,128)S(1)}, u32[]{:S(2)}) copy-start(f32[2,64,64]{2,1,0:T(8,128)S(1)} %get-tuple-element.1171) | copy-start | bytes 98308
  196.0 21.4 copy-start.83
  196.0 21.4 copy-start.85
  196.0 21.4 copy-start.87
  196.0 21.4 copy-start.89
  198.1 201.9 %copy-start.115 = (f32[2,64]{1,0:T(2,128)}, f32[2,64]{1,0:T(2,128)S(1)}, u32[]{:S(2)}) copy-start(f32[2,64]{1,0:T(2,128)S(1)} %get-tuple-element.1173) | copy-start | bytes 1540
  198.6 189.8 %copy-start.91 = (f32[2,16,64]{2,1,0:T(8,128)}, f32[2,16,64]{2,1,0:T(8,128)S(1)}, u32[]{:S(2)}) copy-start(f32[2,16,64]{2,1,0:T(8,128)S(1)} %broadcast_multiply_fusion.2) | copy-start | bytes 24580
  210.8 6.1 collective-permute-start.1
  223.0 228.9 %copy-start.2 = (f32[16,8,16,128]{3,2,1,0:T(8,128)}, f32[16,8,16,128]{3,2,1,0:T(8,128)S(1)}, u32[]{:S(2)}) copy-start(f32[16,8,16,128]{3,2,1,0:T(8,128)S(1)} %copy.424) | copy-start | bytes 3145732
  224.7 227.2 %copy-start.69 = (f32[2,64,16]{1,2,0:T(8,128)}, f32[2,64,16]{1,2,0:T(8,128)S(1)}, u32[]{:S(2)}) copy-start(f32[2,64,16]{1,2,0:T(8,128)S(1)} %copy.298) | copy-start | bytes 24580
  224.9 164.4 %copy-start.47 = (f32[16,8,16,128]{3,2,1,0:T(8,128)}, f32[16,8,16,128]{3,2,1,0:T(8,128)S(1)}, u32[]{:S(2)}) copy-start(f32[16,8,16,128]{3,2,1,0:T(8,128)S(1)} %copy.426) | copy-start | bytes 3145732
  423.4 226.6 %all-gather.31.cloned.1.call-start = ((), (), s32[]{:S(2)}) async-start(), calls=%async_computation.21 | async-start | bytes 8912896 | tf_op jit(solution)/shard_map/all_gather | solution.py:29
  425.7 302.8 %all-gather.21.cloned.1.call-start = ((), (), s32[]{:S(2)}) async-start(), calls=%async_computation.10 | async-start | bytes 8650752 | tf_op jit(solution)/shard_map/all_gather | solution.py:184
  427.6 446.9 %all-gather.23.cloned.1.call-start = ((), (), s32[]{:S(2)}) async-start(), calls=%async_computation.11 | async-start | bytes 23789568 | tf_op jit(solution)/shard_map/all_gather | solution.py:186
  430.0 590.2 %all-gather.25.cloned.1.call-start = ((), (), s32[]{:S(2)}) async-start(), calls=%async_computation.12 | async-start | bytes 23789568 | tf_op jit(solution)/shard_map/all_gather | solution.py:187
  432.5 733.4 %all-gather.27.cloned.1.call-start = ((), (), s32[]{:S(2)}) async-start(), calls=%async_computation.13 | async-start | bytes 23789568 | tf_op jit(solution)/shard_map/all_gather | solution.py:188
  434.9 845.1 %all-gather.33.cloned.1.call-start = ((), (), s32[]{:S(2)}) async-start(), calls=%async_computation.22 | async-start | bytes 8912896 | tf_op jit(solution)/shard_map/all_gather | solution.py:29
  463.7 930.6 %all-gather.35.cloned.1.call-start = ((), (), s32[]{:S(2)}) async-start(), calls=%async_computation.23 | async-start | bytes 8912896 | tf_op jit(solution)/shard_map/all_gather | solution.py:29
  669.1 10.9 copy-start.141
  680.0 53.3 copy-start.53
  733.2 153.5 %copy-start.134 = (f32[128]{0:T(128)}, f32[128]{0:T(128)S(1)}, u32[]{:S(2)}) copy-start(f32[128]{0:T(128)S(1)} %get-tuple-element.1179) | copy-start | bytes 1540
  733.2 474.9 %copy-start.18 = (f32[128,2048]{1,0:T(8,128)}, f32[128,2048]{1,0:T(8,128)S(1)}, u32[]{:S(2)}) copy-start(f32[128,2048]{1,0:T(8,128)S(1)} %get-tuple-element.1180) | copy-start | bytes 3145732
  733.3 153.5 %copy-start.129 = (f32[128]{0:T(128)}, f32[128]{0:T(128)S(1)}, u32[]{:S(2)}) copy-start(f32[128]{0:T(128)S(1)} %fusion.203) | copy-start | bytes 1540
  733.4 286.7 %copy-start.33 = (bf16[128,2048]{1,0:T(8,128)(2,1)}, bf16[128,2048]{1,0:T(8,128)(2,1)S(1)}, u32[]{:S(2)}) copy-start(bf16[128,2048]{1,0:T(8,128)(2,1)S(1)} %multiply_convert_fusion.2) | copy-start | bytes 1572868
  886.8 279.1 %copy-start.71 = (bf16[1,128,2048]{2,1,0:T(8,128)(2,1)S(1)}, bf16[1,128,2048]{2,1,0:T(8,128)(2,1)}, u32[]{:S(2)}) copy-start(bf16[1,128,2048]{2,1,0:T(8,128)(2,1)} %param.39) | copy-start | bytes 1572868
  1181.0 13.4 copy-start.38
  1181.1 13.4 copy-start.39
  1181.1 13.4 copy-start.130
  1194.5 13.6 copy-start.135
  1219.1 18.5 copy-start.107
  1219.1 18.6 copy-start.109
  1237.5 542.7 %reduce-scatter.25.cloned.1.call-start = ((), (), s32[]{:S(2)}) async-start(), calls=%async_computation.24 | async-start | bytes 3244032
  1492.5 50.6 copy-start.70
  1501.7 10.5 copy-start.35
  1523.2 10.5 copy-start.35
  1592.4 237.1 %reduce-scatter.27.cloned.1.call-start = ((), (), s32[]{:S(2)}) async-start(), calls=%async_computation.25 | async-start | bytes 1081344
  1594.3 592.1 %reduce-scatter.17.cloned.1.call-start = ((), (), s32[]{:S(2)}) async-start(), calls=%async_computation.16 | async-start | bytes 17301504 | tf_op jit(solution)/shard_map/reduce_scatter | solution.py:330
  1602.7 946.7 %reduce-scatter.15.cloned.1.call-start = ((), (), s32[]{:S(2)}) async-start(), calls=%async_computation.15 | async-start | bytes 17301504 | tf_op jit(solution)/shard_map/reduce_scatter | solution.py:328
  1612.1 1378.0 %reduce-scatter.13.cloned.1.call-start = ((), (), s32[]{:S(2)}) async-start(), calls=%async_computation.14 | async-start | bytes 51904512 | tf_op jit(solution)/shard_map/reduce_scatter | solution.py:325
  1616.8 6.0 collective-permute-start.2
  1643.8 2315.5 %reduce-scatter.19.cloned.1.call-start = ((), (), s32[]{:S(2)}) async-start(), calls=%async_computation.17 | async-start | bytes 47579136 | tf_op jit(solution)/shard_map/reduce_scatter | solution.py:287
  1663.7 3272.6 %reduce-scatter.21.cloned.1.call-start = ((), (), s32[]{:S(2)}) async-start(), calls=%async_computation.18 | async-start | bytes 47579136 | tf_op jit(solution)/shard_map/reduce_scatter | solution.py:288
  1683.4 4229.8 %reduce-scatter.23.cloned.1.call-start = ((), (), s32[]{:S(2)}) async-start(), calls=%async_computation.19 | async-start | bytes 47579136 | tf_op jit(solution)/shard_map/reduce_scatter | solution.py:289
  1709.5 11.8 copy-start.82
  1709.5 11.8 copy-start.95
  1709.5 11.8 copy-start.99
  1722.9 15.1 copy-start.117
  1722.9 15.1 copy-start.118
  1722.9 54.3 copy-start.137
  (121 other events, 471.9 us)
Sparse Core Ops, SparseCore 0:
  11.6 161.0 all-gather.16
  176.0 76.9 all-gather.18
  423.6 112.1 all-gather.28
  538.9 111.0 all-gather.30
  652.7 75.7 all-gather.20
  731.2 143.2 all-gather.22
  877.3 142.8 all-gather.24
  1023.0 142.8 all-gather.26
  1168.7 111.2 all-gather.32
  1283.2 111.0 all-gather.34
  1592.5 97.3 reduce-scatter.24
  1692.0 137.4 reduce-scatter.26
  1832.5 353.9 reduce-scatter.16
  2189.3 360.0 reduce-scatter.14
  2557.3 432.6 reduce-scatter.12
  2992.9 966.3 reduce-scatter.18
  3962.1 974.1 reduce-scatter.20
  4939.1 974.0 reduce-scatter.22
where the time goes:
time: 5930 us; the launch traced here: 5920 us
  waiting for transfers between devices  4940 us (83%)
  matrix products  396 us (7%)
  blocking collectives  213 us (4%)
  other arithmetic  204 us (3%)
  local copies, waits for them, and re-layouts  141 us (2%)
    reduce_scatter x1, waiting for transfers between devices, local(): lax.psum_scatter(grad_hup, ('dp', 'seq'), scatter_dimension=0, tiled=True)  977 us
    reduce_scatter x1, waiting for transfers between devices, local(): lax.psum_scatter(grad_down, ('dp', 'seq'), scatter_dimension=0, tiled=True)  977 us
    reduce_scatter x1, waiting for transfers between devices, local(): lax.psum_scatter(grad_hgate, ('dp', 'seq'), scatter_dimension=0, tiled=True)  969 us
    reduce_scatter x1, waiting for transfers between devices, local(): lax.psum_scatter(grad_wproj, ('dp', 'seq'), scatter_dimension=0, tiled=True)  441 us
    reduce_scatter x1, waiting for transfers between devices, local(): lax.psum_scatter(grad_wgate, ('dp', 'seq'), scatter_dimension=0, tiled=True)  363 us
    reduce_scatter x1, waiting for transfers between devices, local(): lax.psum_scatter(grad_oproj, ('dp', 'seq'), scatter_dimension=0, tiled=True)  356 us
    all_gather x4, waiting for transfers between devices, carried_in(): lax.all_gather(a.astype(kind), axis)  343 us
    another operation x3, other arithmetic, group_prep(): lax.linalg.triangular_solve(system, weighted, left_side=True, lower=True)  161 us
  transfers between devices with their start and end apart: 21, of which 17 were waited for; matrix products, arithmetic and copies ran while one was open for 9% of the time, Pallas kernels for 0%

commit v1 on v0

v1 whole, which is shorter than its diff:
```python
import functools

import jax
import jax.numpy as jnp
from jax import lax
from jax.experimental import pallas as pl
from jax.experimental.pallas import tpu as pltpu
from jax.sharding import PartitionSpec as P

D = 2048
H = 16
HEAD = 128
CONV = 4
WIDTH = 8


EPS = 1e-06
HEAD_EPS = 0.01
HIGH = lax.Precision.HIGHEST
LOW = jnp.bfloat16
FULL = jnp.float32


def rms_scale(values, gain):
    return values * lax.rsqrt(jnp.mean(values * values, axis=-1, keepdims=True) + EPS) * gain


def dot_low(left, right):
    return jnp.dot(left, right, preferred_element_type=FULL)


def dot_left_t(left, right):
    return lax.dot_general(left, right, (((0,), (0,)), ((), ())), preferred_element_type=FULL)


def dot_right_t(left, right):
    return lax.dot_general(left, right, (((1,), (1,)), ((), ())), preferred_element_type=FULL)


def bits_of(count):
    return [1 << place for place in range(count.bit_length() - 1)]


def swap(values, axis, bit):
    return lax.ppermute(values, axis, [(i, i ^ bit) for i in range(lax.axis_size(axis))])


def grow(values, axis, bit, dim):
    upper = ((lax.axis_index(axis) & bit) != 0).astype(jnp.int32)
    other = swap(values, axis, bit)
    shape = values.shape[:dim] + (2,) + values.shape[dim:]
    own = lax.broadcasted_iota(jnp.int32, shape, dim) == upper
    both = jnp.where(own, jnp.expand_dims(values, dim), jnp.expand_dims(other, dim))
    return both.reshape(values.shape[:dim] + (2 * values.shape[dim],) + values.shape[dim + 1 :])


def halve(values, axis, bit, dim, waited=()):
    upper = ((lax.axis_index(axis) & bit) != 0).astype(jnp.int32)
    kept = lax.dynamic_index_in_dim(values, upper, dim, True)
    sent = lax.dynamic_index_in_dim(values, 1 - upper, dim, True)
    sent = sent.astype(LOW)
    return kept.astype(FULL) + swap(tie(sent, *waited) if waited else sent, axis, bit).astype(FULL)


def tie(values, *others):
    leaves, tree = jax.tree.flatten(values)
    waited = jax.tree.leaves(others)
    anywhere = pl.BlockSpec(memory_space=pl.ANY)
    passed = pl.pallas_call(
        lambda *refs: None,
        out_shape=[jax.ShapeDtypeStruct(leaf.shape, leaf.dtype) for leaf in leaves],
        in_specs=[anywhere] * (len(leaves) + len(waited)),
        out_specs=[anywhere] * len(leaves),
        input_output_aliases={at: at for at in range(len(leaves))},
        cost_estimate=pl.CostEstimate(flops=1024, bytes_accessed=1024, transcendentals=0),
    )(*leaves, *waited)
    return jax.tree.unflatten(tree, passed)


def hint(values, *others):
    return lax.optimization_barrier((values, *others))[0]


def turned_about(values, axis, unit, count, dim):
    place = lax.axis_index(axis) // unit
    shape = values.shape
    for bit in bits_of(count):
        split = values.reshape(shape[:dim] + (count // (2 * bit), 2, bit) + shape[dim + 1 :])
        flipped = jnp.flip(split, dim + 1)
        values = jnp.where((place & bit) != 0, flipped, split).reshape(shape)
    return values


def fiber_order(values, width):
    dp, cubes = lax.axis_size("dp"), lax.axis_size("seq") // width
    split = values.reshape(values.shape[:-1] + (dp, cubes, -1))
    dim = values.ndim - 1
    split = turned_about(split, "dp", 1, dp, dim)
    return turned_about(split, "seq", width, cubes, dim + 1).reshape(values.shape)


def near_gather(values, axis, unit, count):
    values = values[None]
    for bit in bits_of(count):
        values = jnp.concatenate([values, swap(values, axis, bit * unit)], 0)
    return values


def near_sum(values, axis, unit, count, waited=()):
    for bit in reversed(bits_of(count)):
        sent = values[bit:].astype(LOW)
        sent = swap(tie(sent, *waited) if waited else sent, axis, bit * unit)
        values = values[:bit].astype(FULL) + sent.astype(FULL)
    return values[0]


def cube_turn(values, width):
    seq = lax.axis_size("seq")
    groups = [list(range(first, first + width)) for first in range(0, seq, width)]
    return lax.all_to_all(values, "seq", 0, 0, axis_index_groups=groups, tiled=True)


def gather_all(values):
    count = lax.axis_size("dp") * lax.axis_size("seq")
    rows = jnp.broadcast_to(values[None], (count,) + values.shape)
    return lax.all_to_all(rows, ("dp", "seq"), 0, 0, tiled=True)


def sum_all(values):
    return jnp.sum(lax.all_to_all(values, ("dp", "seq"), 0, 0, tiled=True), axis=0)


def column_parts(columns, count):
    tiles = columns // 128
    edges = [128 * ((tiles * part) // count) for part in range(count + 1)]
    edges[-1] = columns
    return list(zip(edges[:-1], edges[1:]))


def cube_orders(width, parts):
    places = list(range(width.bit_length() - 1))
    if parts == 2 and len(places) > 2:
        return [places[1:] + places[:1], places[2:] + places[:2]]
    if parts == 3:
        return [places[start:] + places[:start] for start in range(len(places))] or [[]]
    return ([places[::-1], places[-1:] + places[:-1]] if len(places) > 2 else [places[::-1]])[:parts]


def cube_open(values, width, parts):
    rows, columns = values.shape
    orders = cube_orders(width, parts)
    cut = column_parts(columns, len(orders))
    return [values[:, low:high].reshape([1] * len(orders[0]) + [rows, high - low]) for low, high in cut]


def cube_step(blocks, width, parts, phase):
    orders = cube_orders(width, parts)
    depth = len(orders[0])
    return [
        grow(block, "seq", 1 << order[phase], depth - 1 - order[phase])
        for order, block in zip(orders, blocks)
    ]


def cube_close(blocks):
    return jnp.concatenate([block.reshape(-1, block.shape[-1]) for block in blocks], 1)


def cube_gather(values, width, parts):
    lead, (rows, columns) = values.shape[:-2], values.shape[-2:]
    orders = cube_orders(width, parts)
    depth = len(orders[0])
    done = []
    for order, (low, high) in zip(orders, column_parts(columns, len(orders))):
        block = values[..., low:high].reshape([1] * depth + list(values.shape[:-1]) + [high - low])
        for place in order:
            block = grow(block, "seq", 1 << place, depth - 1 - place)
        block = jnp.moveaxis(block.reshape((width,) + lead + (rows, high - low)), 0, -3)
        done.append(block.reshape(lead + (width * rows, high - low)))
    return jnp.concatenate(done, -1)


def cube_sum(values, width):
    blocks = values.astype(LOW).reshape((width, values.shape[0] // width) + values.shape[1:])
    return jnp.sum(cube_turn(blocks, width).astype(FULL), axis=0)


def cube_sum_by_axes(left, right, dot, width):
    rows = left.shape[0]
    orders = cube_orders(width, 2)
    depth = len(orders[0])
    done = []
    for order, part in zip(orders, right):
        block = dot(left, part)
        columns = block.shape[1]
        block = block.reshape([2] * depth + [rows // width, columns])
        for place in reversed(order):
            block = halve(block, "seq", 1 << place, depth - 1 - place)
        done.append(block.reshape(rows // width, columns))
    return jnp.concatenate(done, 1)


def fiber_gather_seq(values, width):
    values = values[None]
    for bit in bits_of(lax.axis_size("seq") // width):
        values = grow(values, "seq", bit * width, 0)
    return values


def chip_gather(values):
    for bit in bits_of(lax.axis_size("dp")):
        values = grow(values, "dp", bit, 0)
    return values


def chip_sum(values):
    rest = values.shape[1:]
    for bit in reversed(bits_of(lax.axis_size("dp"))):
        values = halve(values.reshape((2, -1) + rest), "dp", bit, 0)[0]
    return values


def far_sum(values, width, waited=()):
    rest = values.shape[1:]
    for bit in reversed(bits_of(lax.axis_size("seq") // width)):
        values = halve(values.reshape((2, -1) + rest), "seq", bit * width, 0, waited)[0]
    return values.reshape(rest)


CHUNK = 128
MICRO = 1 << 30
SPAN = 8
RIM = 16


def split(values):
    high = values.astype(LOW)
    return (high, (values - high.astype(FULL)).astype(LOW))


def mul(left, right):
    return jnp.dot(
        jnp.concatenate([left[0], left[1], left[0]], 1),
        jnp.concatenate([right[0], right[0], right[1]], 0),
        preferred_element_type=FULL,
    )


def mul_t(left, right):
    return lax.dot_general(
        jnp.concatenate([left[0], left[1], left[0]], 1),
        jnp.concatenate([right[0], right[0], right[1]], 1),
        (((1,), (1,)), ((), ())),
        preferred_element_type=FULL,
    )


def grid_index(dim):
    return lax.broadcasted_iota(jnp.int32, (CHUNK, CHUNK), dim)


def row_sum(values):
    return jnp.sum(values, axis=1, keepdims=True)


def here_rows(chunk):
    return pl.ds(pl.multiple_of(chunk * CHUNK + RIM, SPAN), CHUNK)


def conv_part(mix_ref, taps_ref, cols, chunk, low):
    start = pl.multiple_of(chunk * CHUNK + RIM - SPAN, SPAN)
    rows = mix_ref[pl.ds(start, CHUNK + SPAN), low : low + HEAD].astype(LOW).astype(FULL)
    total = jnp.zeros((CHUNK, HEAD), FULL)
    terms = []
    for tap in range(CONV):
        back = CONV - 1 - tap
        moved = rows if back == 0 else pltpu.roll(rows, back, 0)
        term = moved[SPAN:] * cols[:, tap : tap + 1]
        terms.append(term)
        total = total + taps_ref[tap : tap + 1, low : low + HEAD] * term
    return (total, terms)


def unit_part(values):
    scale = lax.rsqrt(row_sum(values * values) + EPS)
    return (values * scale, scale)


def prep_kernel(heads, deep, mix_ref, taps_ref, cols_ref, seg_ref, *outs):
    q_ref, k_ref, uk_ref, uv_ref, inv_ref, att_ref, map_ref, add_ref, far_ref, end_ref = outs
    mine = heads * HEAD
    chunks = seg_ref.shape[0]
    group = 2 if chunks % 2 == 0 else 1
    i_at, j_at = grid_index(0), grid_index(1)
    apart = i_at ^ j_at
    eye = (i_at == j_at).astype(FULL)

    def some(step, carry):
        work = []
        for offset in range(group):
            chunk = step * group + offset
            cols = cols_ref[pl.ds(pl.multiple_of(chunk * CHUNK, CHUNK), CHUNK), :]
            same = cols[:, 4:5] == seg_ref[chunk]
            lower = (same & (j_at < i_at)).astype(FULL)
            inclusive = (same & (j_at <= i_at)).astype(FULL)
            carried, ending = cols[:, 5:6], cols[:, 6:7]
            for head in range(heads):
                at = chunk * heads + head
                parts = [
                    jax.nn.silu(
                        conv_part(mix_ref, taps_ref, cols, chunk, part * mine + head * HEAD)[0]
                    )
                    for part in range(3)
                ]
                query, key = unit_part(parts[0])[0], unit_part(parts[1])[0]
                last = mix_ref[here_rows(chunk), 4 * mine : 4 * mine + HEAD]
                weight = jax.nn.sigmoid(last[:, head : head + 1])
                q_ref[at] = query
                k_ref[at] = key
                key_s, query_s = split(key), split(query)
                both = tuple(jnp.concatenate([a, b], 0) for a, b in zip(key_s, query_s))
                grams = mul_t(both, key_s)
                att_ref[at] = grams[CHUNK:] * inclusive
                below = weight * grams[:CHUNK] * lower
                work.append([at, key, parts[2], weight, carried, ending, below])
        inverses = [eye - jnp.where(apart == 1, item[6], 0.0) for item in work]
        level = 1
        while (1 << level) < CHUNK:
            next_inverses = []
            for item, inverse in zip(work, inverses):
                inverse_s = split(inverse)
                block = split(jnp.where((apart >> level) == 1, item[6], 0.0))
                inner = split(mul(inverse_s, block))
                next_inverses.append(inverse - mul(inner, inverse_s))
            inverses = next_inverses
            level += 1
        for item, inverse in zip(work, inverses):
            at, key, value, weight, carried, ending, below = item
            inv_ref[at] = inverse
            right = jnp.concatenate([(weight * carried) * key, weight * value], 1)
            solved = mul(split(inverse), split(right))
            uk_ref[at] = solved[:, :HEAD]
            uv_ref[at] = solved[:, HEAD:]
            turned = mul(split((key * ending).T), split(solved))
            map_ref[at] = carried[CHUNK - 1 :] * eye - turned[:, :HEAD]
            add_ref[at] = turned[:, HEAD:]
        return carry

    lax.fori_loop(0, chunks // group, some, 0)

    end_ref[...] = jnp.zeros_like(end_ref)
    for head in range(heads):
        far_ref[head] = eye

    def chain(chunk, carry):
        for head in range(heads):
            at = chunk * heads + head
            step = split(map_ref[at])
            end_ref[head] = mul(step, split(end_ref[head])) + add_ref[at]
            if deep:
                far_ref[head] = mul(step, split(far_ref[head]))
        return carry

    lax.fori_loop(0, chunks, chain, 0)


def run_kernel(heads, mix_ref, cols_ref, gain_ref, q_ref, uk_ref, uv_ref, att_ref, map_ref, add_ref, state_ref, *outs):
    p_ref, delta_ref, out_ref, scaled_ref, now_ref = outs
    mine = heads * HEAD
    chunks = p_ref.shape[0] // heads
    now_ref[...] = state_ref[...]

    def one(chunk, carry):
        start = pl.multiple_of(chunk * CHUNK, CHUNK)
        carried = cols_ref[pl.ds(start, CHUNK), :][:, 5:6]
        for head in range(heads):
            at = chunk * heads + head
            state = now_ref[head]
            p_ref[at] = state
            state_s = split(state)
            now_ref[head] = mul(split(map_ref[at]), state_s) + add_ref[at]
            both = split(jnp.concatenate([uk_ref[at], q_ref[at]], 0))
            seen = mul(both, state_s)
            delta = uv_ref[at] - seen[:CHUNK]
            delta_ref[at] = delta
            output = carried * seen[CHUNK:] + mul(split(att_ref[at]), split(delta))
            out_ref[at] = output
            low = 3 * mine + head * HEAD
            gate = mix_ref[here_rows(chunk), low : low + HEAD]
            scale = lax.rsqrt(row_sum(output * output) / HEAD + HEAD_EPS)
            gain = gain_ref[:, head * HEAD : (head + 1) * HEAD]
            scaled = output * scale * gain * jax.nn.silu(gate)
            scaled_ref[pl.ds(start, CHUNK), head * HEAD : (head + 1) * HEAD] = scaled.astype(LOW)
        return carry

    lax.fori_loop(0, chunks, one, 0)


def silu_slope(values):
    gate = jax.nn.sigmoid(values)
    return gate * (1.0 + values * (1.0 - gate))


def back_kernel(heads, mix_ref, cols_ref, gain_ref, q_ref, uk_ref, att_ref, map_ref, out_ref, grad_ref, *outs):
    dout_ref, first_ref, term_ref, dgate_ref, end_ref = outs
    mine = heads * HEAD
    chunks = out_ref.shape[0] // heads
    end_ref[...] = jnp.zeros_like(end_ref)

    def one(step, carry):
        chunk = chunks - 1 - step
        start = pl.multiple_of(chunk * CHUNK, CHUNK)
        carried = cols_ref[pl.ds(start, CHUNK), :][:, 5:6]
        for head in range(heads):
            at = chunk * heads + head
            here = slice(head * HEAD, (head + 1) * HEAD)
            low = 3 * mine + head * HEAD
            gate = mix_ref[here_rows(chunk), low : low + HEAD]
            output = out_ref[at]
            grad = grad_ref[pl.ds(start, CHUNK), here].astype(FULL)
            gain = gain_ref[:, here]
            scale = lax.rsqrt(row_sum(output * output) / HEAD + HEAD_EPS)
            unit = output * scale
            opened = jax.nn.silu(gate)
            dgate_ref[pl.ds(start, CHUNK), here] = (grad * unit * gain * silu_slope(gate)).astype(LOW)
            inner = grad * gain * opened
            dout = scale * (inner - unit * (row_sum(inner * unit) / HEAD))
            dout_ref[at] = dout
            first = mul(split(att_ref[at].T), split(dout))
            first_ref[at] = first
            left = split(jnp.concatenate([q_ref[at].T, uk_ref[at].T], 1))
            term = mul(left, split(jnp.concatenate([carried * dout, -first], 0)))
            term_ref[at] = term
            end_ref[head] = mul(split(map_ref[at].T), split(end_ref[head])) + term
        return carry

    lax.fori_loop(0, chunks, one, 0)


def pull_kernel(heads, mix_ref, taps_ref, cols_ref, seg_ref, *rest):
    (q_ref, k_ref, inv_ref, att_ref, map_ref, p_ref, delta_ref) = rest[:7]
    (dout_ref, first_ref, term_ref, dgate_ref, leave_ref) = rest[7:12]
    gmix_ref, tail_ref, edge_ref, dtaps_ref, now_ref, next_ref = rest[12:]
    gmix_ref[:RIM] = jnp.zeros((RIM, gmix_ref.shape[1]), LOW)
    mine = heads * HEAD
    chunks = seg_ref.shape[0]
    i_at, j_at = grid_index(0), grid_index(1)
    now_ref[...] = leave_ref[...]
    next_ref[...] = jnp.zeros_like(next_ref)
    dtaps_ref[...] = jnp.zeros_like(dtaps_ref)

    def one(step, carry):
        chunk = chunks - 1 - step
        start = pl.multiple_of(chunk * CHUNK, CHUNK)
        cols_far = cols_ref[pl.ds(start, CHUNK + SPAN), :]
        cols = cols_far[:CHUNK]
        same = cols[:, 4:5] == seg_ref[chunk]
        lower = (same & (j_at < i_at)).astype(FULL)
        inclusive = (same & (j_at <= i_at)).astype(FULL)
        carried, ending = cols[:, 5:6], cols[:, 6:7]
        last = mix_ref[here_rows(chunk), 4 * mine : 4 * mine + HEAD]
        dlast = jnp.zeros((CHUNK, HEAD), FULL)
        for head in range(heads):
            at = chunk * heads + head
            lows = [part * mine + head * HEAD for part in range(3)]
            mixed = [conv_part(mix_ref, taps_ref, cols, chunk, low) for low in lows]
            query, query_scale = unit_part(jax.nn.silu(mixed[0][0]))
            key, key_scale = unit_part(jax.nn.silu(mixed[1][0]))
            value = jax.nn.silu(mixed[2][0])
            weight = jax.nn.sigmoid(last[:, head : head + 1])
            key_s = split(key)
            leave = now_ref[head]
            leave_s = split(leave)
            now_ref[head] = mul(split(map_ref[at].T), leave_s) + term_ref[at]
            ddelta = first_ref[at] + mul(split(key * ending), leave_s)
            solved = mul(split(inv_ref[at].T), split(ddelta))
            delta_s = split(delta_ref[at])
            dout = dout_ref[at]
            ends = split(jnp.concatenate([solved, dout], 0))
            by_state = mul_t(ends, split(p_ref[at]))
            by_delta = mul_t(ends, delta_s)
            dright = -by_state[:CHUNK]
            dsystem = -by_delta[:CHUNK] * lower
            datt = by_delta[CHUNK:] * inclusive
            dquery = carried * by_state[CHUNK:] + mul(split(datt), key_s)
            gram = mul_t(key_s, key_s)
            dgram = weight * dsystem
            left = split(jnp.concatenate([datt.T, dgram + dgram.T], 1))
            right = tuple(jnp.concatenate([a, b], 0) for a, b in zip(split(query), key_s))
            dkey = mul(left, right) + (weight * carried) * dright
            dkey = dkey + ending * mul_t(delta_s, leave_s)
            dvalue = weight * solved
            dweight = row_sum(solved * value + carried * dright * key + dsystem * gram)
            dlogit = dweight * weight * (1.0 - weight)
            dlast = jnp.where(j_at == head, dlogit, dlast)
            dactive = [
                query_scale * (dquery - query * row_sum(dquery * query)),
                key_scale * (dkey - key * row_sum(dkey * key)),
                dvalue,
            ]
            for part, low in enumerate(lows):
                total, terms = mixed[part]
                dtotal = dactive[part] * silu_slope(total)
                here = slice(low, low + HEAD)
                far = jnp.concatenate([dtotal, next_ref[:, here]], 0)
                near = jnp.concatenate([jnp.zeros((SPAN, HEAD), FULL), dtotal[:SPAN]], 0)
                next_ref[:, here] = dtotal[:SPAN]
                dproj = jnp.zeros((CHUNK, HEAD), FULL)
                edge = jnp.zeros((SPAN, HEAD), FULL)
                zero = jnp.zeros((SPAN, 1), FULL)
                for tap in range(CONV):
                    back = CONV - 1 - tap
                    tap_row = taps_ref[tap : tap + 1, here]
                    dtaps_ref[tap : tap + 1, here] += jnp.sum(dtotal * terms[tap], axis=0, keepdims=True)
                    spread = far * cols_far[:, tap : tap + 1]
                    near_mask = jnp.concatenate([zero, cols[:SPAN, tap : tap + 1]], 0)
                    close = near * near_mask
                    if back > 0:
                        spread = pltpu.roll(spread, CHUNK + SPAN - back, 0)
                        close = pltpu.roll(close, 2 * SPAN - back, 0)
                        edge = edge + tap_row * close[:SPAN]
                    dproj = dproj + tap_row * spread[:CHUNK]
                gmix_ref[here_rows(chunk), here] = dproj.astype(LOW)
                edge_ref[:, here] = edge

                @pl.when(step == 0)
                def _():
                    tail_ref[:, here] = dproj[CHUNK - SPAN :]

        gmix_ref[here_rows(chunk), 3 * mine : 4 * mine] = dgate_ref[pl.ds(start, CHUNK), :]
        gmix_ref[here_rows(chunk), 4 * mine : 4 * mine + HEAD] = dlast.astype(LOW)
        return carry

    lax.fori_loop(0, chunks, one, 0)
    gap = jnp.zeros((RIM - SPAN, 3 * mine), FULL)
    gmix_ref[:RIM, : 3 * mine] = jnp.concatenate([gap, edge_ref[...]], 0).astype(LOW)


def on_chip(body, shapes, scratch, flops, waited, *operands):
    whole = pl.BlockSpec(memory_space=pltpu.VMEM)
    anywhere = pl.BlockSpec(memory_space=pl.ANY)
    used, spare = len(operands), len(waited)
    return pl.pallas_call(
        lambda *refs: body(*refs[:used], *refs[used + spare :]),
        out_shape=shapes,
        in_specs=[whole] * used + [anywhere] * spare,
        out_specs=[whole] * len(shapes),
        scratch_shapes=list(scratch),
        compiler_params=pltpu.CompilerParams(vmem_limit_bytes=56 * 1024 * 1024),
        cost_estimate=pl.CostEstimate(flops=flops, bytes_accessed=20 * 1024 * 1024, transcendentals=0),
    )(*operands, *waited)


def squares(*counts):
    return tuple(jax.ShapeDtypeStruct((count, HEAD, HEAD), FULL) for count in counts)


def delta_prep(heads, deep, mix, taps, cols, segs, waited):
    each = segs.shape[0] * heads
    shapes = squares(*[each] * 8, heads, heads)
    body = functools.partial(prep_kernel, heads, deep)
    return on_chip(body, shapes, (), 30 * MICRO, waited, mix, taps, cols, segs)


def delta_run(heads, mix, cols, gain, prepared, state, waited):
    q, k, uk, uv, inv, att, step, add = prepared
    each = q.shape[0]
    count = each // heads * CHUNK
    shapes = squares(each, each, each) + (jax.ShapeDtypeStruct((count, heads * HEAD), LOW),)
    body = functools.partial(run_kernel, heads)
    scratch = [pltpu.VMEM((heads, HEAD, HEAD), FULL)]
    flops = 11 * MICRO
    return on_chip(
        body, shapes, scratch, flops, waited, mix, cols, gain, q, uk, uv, att, step, add, state
    )


def delta_back(heads, mix, cols, gain, prepared, output, grad, waited):
    q, k, uk, uv, inv, att, step, add = prepared
    each = q.shape[0]
    count = each // heads * CHUNK
    mine = heads * HEAD
    shapes = squares(each, each, each) + (
        jax.ShapeDtypeStruct((count, mine), LOW),
    ) + squares(heads)
    body = functools.partial(back_kernel, heads)
    flops = 12 * MICRO
    return on_chip(
        body, shapes, (), flops, waited, mix, cols, gain, q, uk, att, step, output, grad
    )


def delta_pull(heads, mix, taps, cols, segs, prepared, states, delta, backs, leaving, waited):
    q, k, uk, uv, inv, att, step, add = prepared
    dout, first, term, dgate = backs
    mine = heads * HEAD
    shapes = (
        jax.ShapeDtypeStruct(mix.shape, LOW),
        jax.ShapeDtypeStruct((SPAN, 3 * mine), FULL),
        jax.ShapeDtypeStruct((SPAN, 3 * mine), FULL),
        jax.ShapeDtypeStruct((SPAN, 3 * mine), FULL),
    )
    body = functools.partial(pull_kernel, heads)
    scratch = [pltpu.VMEM((heads, HEAD, HEAD), FULL), pltpu.VMEM((SPAN, 3 * mine), FULL)]
    flops = 30 * MICRO
    return on_chip(
        body, shapes, scratch, flops, waited, mix, taps, cols, segs, q, k, inv, att, step, states, delta, dout, first, term, dgate, leaving
    )


def swiglu(gate_two, up_two):
    return jax.nn.silu(gate_two) * up_two


def local(
    block_input,
    segments,
    mix_gain,
    w_project,
    conv_taps,
    w_beta,
    w_gate,
    head_gain,
    w_output,
    ffn_gain,
    w_hidden_gate,
    w_hidden_up,
    w_hidden_down,
    cotangent,
):
    dp, seq = lax.axis_size("dp"), lax.axis_size("seq")
    width = min(WIDTH, seq & -seq)
    cubes = seq // width
    everyone = dp * seq
    fiber = dp * cubes
    both = ("dp", "seq")
    row_at, chip_at = lax.axis_index("dp"), lax.axis_index("seq")
    me = chip_at % width
    cube_at = chip_at // width
    heads = H // width
    mine = heads * HEAD
    rows = w_project.shape[0]
    tokens = block_input.shape[1]
    count = tokens * width
    units = w_hidden_down.shape[0]
    hidden_mine = fiber * units

    taps_each = conv_taps.shape[1]
    packed = jnp.concatenate(
        [
            mix_gain.astype(LOW),
            head_gain.astype(LOW),
            ffn_gain.astype(LOW),
            conv_taps.astype(LOW).reshape(-1),
            segments[0].astype(LOW),
        ]
    )
    mixer_pad = -(mine * 4 + heads) % 128
    mixer_low = jnp.concatenate(
        [
            jnp.swapaxes(w_project.reshape(rows, 3, width, mine), 1, 2).reshape(rows, width, 3 * mine),
            w_gate.reshape(rows, width, mine),
            w_beta.reshape(rows, width, heads),
            jnp.zeros((rows, width, mixer_pad), FULL),
        ],
        -1,
    ).astype(LOW)
    mixer_turned = cube_turn(jnp.swapaxes(mixer_low, 0, 1), width)
    small = gather_all(packed)
    gain_one = small[:, :rows].reshape(D).astype(FULL)
    gain_head = small[:, rows : 2 * rows].reshape(D).astype(FULL)
    gain_two = small[:, 2 * rows : 3 * rows].reshape(D).astype(FULL)
    taps_full = small[:, 3 * rows : 3 * rows + CONV * taps_each].reshape(everyone, CONV, taps_each)
    taps_full = jnp.swapaxes(taps_full, 0, 1).reshape(CONV, 3, width, mine).astype(FULL)
    taps_mine = lax.dynamic_index_in_dim(taps_full, me, 2, False).reshape(CONV, 3 * mine)
    gain_mine = lax.dynamic_index_in_dim(gain_head.reshape(width, heads, HEAD), me, 0, False)
    seg_all = small[:, 3 * rows + CONV * taps_each :].astype(jnp.int32).reshape(dp, seq * tokens)
    seg_row = lax.dynamic_index_in_dim(seg_all, row_at, 0, False)
    ext_seg = lax.dynamic_slice_in_dim(
        jnp.concatenate([jnp.zeros((CONV - 1,), jnp.int32), seg_row]),
        cube_at * count,
        count + CONV - 1,
    )
    seg_mine = ext_seg[CONV - 1 :]
    tokens_in = jnp.concatenate([fiber_order(block_input, width), cotangent], 0)
    pair = cube_gather(tokens_in, width, 2)
    x_cube, g_out = pair[0], pair[1]
    ahead = [(i, i + width) for i in range(seq - width)]
    behind = [(i + width, i) for i in range(seq - width)]
    rim = lax.ppermute(fiber_order(x_cube[count - RIM :], width), "seq", ahead)
    x_more = jnp.concatenate([fiber_order(rim, width), x_cube], 0)
    mixer_far = near_gather(mixer_turned, "seq", width, cubes)
    mixer_w = near_gather(mixer_far, "dp", 1, dp).reshape(D, -1)

    hgate_late, hup_late = hint((w_hidden_gate, w_hidden_up), mixer_turned)

    def by_units(weight):
        split = weight.astype(LOW).reshape(rows, dp, cubes, width, units)
        return jnp.transpose(split, (3, 0, 1, 2, 4)).reshape(width, rows, hidden_mine)

    ffn_low = jnp.concatenate([by_units(hgate_late), by_units(hup_late)], -1)
    ffn_turned = cube_turn(ffn_low, width)
    ffn_far = near_gather(hint(ffn_turned, mixer_far), "seq", width, cubes)

    residual = block_input[0].astype(FULL)
    normed_own, mix_pull = jax.vjp(lambda v: rms_scale(v, gain_one), residual)
    normed = rms_scale(x_more.astype(FULL), fiber_order(gain_one, width)).astype(LOW)
    mixed_in = dot_low(normed, mixer_w)
    out_low, down_low, mixed_in = lax.optimization_barrier(
        (w_output.astype(LOW), w_hidden_down.astype(LOW), mixed_in)
    )
    out_far = near_gather(out_low, "seq", width, cubes)
    out_spread = jnp.broadcast_to(out_far[None], (width,) + out_far.shape)
    out_near = cube_turn(out_spread, width).reshape(D // dp, D)
    chunks = count // CHUNK
    seg_chunks = seg_mine.reshape(chunks, CHUNK)
    before = jnp.concatenate([ext_seg[CONV - 2 : CONV - 1], seg_chunks[:-1, -1]], 0)
    columns = [ext_seg[tap : tap + count] == seg_mine for tap in range(CONV)]
    columns.append(seg_mine)
    columns.append((seg_chunks == before[:, None]).reshape(count))
    columns.append((seg_chunks == seg_chunks[:, -1:]).reshape(count))
    columns.append(jnp.zeros((count,), FULL))
    cols = jnp.stack([column.astype(FULL) for column in columns], 1)
    cols = jnp.pad(cols, ((0, SPAN), (0, 0)))
    segs = seg_chunks.astype(FULL)[:, None, :]
    gain_row = gain_mine.reshape(1, mine)
    prepared = delta_prep(heads, cubes > 2, mixed_in, taps_mine, cols, segs, ())
    far, end = prepared[8:]
    prepared = prepared[:8]
    state_in = jnp.zeros((heads, HEAD, HEAD), FULL)
    for hop in range(cubes - 1):
        out = end
        if hop > 0:
            out = end + jnp.einsum("hij,hjk->hik", far, state_in, precision=HIGH)
        state_in = lax.ppermute(out, "seq", ahead)
    states, delta, recalled, scaled = delta_run(
        heads, mixed_in, cols, gain_row, prepared, state_in, ()
    )
    ffn_w = near_gather(ffn_far, "dp", 1, dp).reshape(D, 2 * hidden_mine)
    out_parts = [out_near]
    for bit in bits_of(dp):
        out_parts = out_parts + [swap(part, "dp", bit) for part in out_parts]
    scaled_own = jnp.swapaxes(cube_turn(scaled.reshape(width, tokens, mine), width), 0, 1)
    down_w = chip_gather(fiber_gather_seq(down_low, width)).reshape(hidden_mine, D)
    scaled_own = fiber_order(scaled_own.reshape(tokens, D), width)
    scaled_own = jnp.swapaxes(scaled_own.reshape(tokens, dp, cubes, width, rows), 2, 3)
    scaled_own = scaled_own.reshape(tokens, dp, D // dp)
    middle = residual
    for at, part in enumerate(out_parts):
        middle = middle + dot_low(scaled_own[:, at], part)

    normed_two_f, ffn_pull = jax.vjp(lambda v: rms_scale(v, gain_two), middle)
    normed_two = cube_gather(fiber_order(normed_two_f.astype(LOW), width), width, 3)
    both_two = dot_low(normed_two, ffn_w)
    gate_two, up_two = both_two[:, :hidden_mine], both_two[:, hidden_mine:]
    hidden_f, glu_pull = jax.vjp(swiglu, gate_two, up_two)
    hidden = hidden_f.astype(LOW)
    grad_hidden = dot_right_t(g_out, down_w)
    grad_gate_two, grad_up_two = glu_pull(grad_hidden)
    grad_both = jnp.concatenate([grad_gate_two.astype(LOW), grad_up_two.astype(LOW)], 1)
    pulled = dot_right_t(grad_both, ffn_w).astype(LOW)
    grad_normed_two = fiber_order(cube_sum(pulled, width), width)
    grad_down = chip_sum(dot_left_t(hidden, g_out).reshape(fiber, units, D))
    grad_ffn = dot_left_t(normed_two, grad_both).reshape(dp, cubes, width, rows, -1)
    grad_ffn = near_sum(grad_ffn, "dp", 1, dp)
    grad_normed_two, grad_ffn, grad_down = lax.optimization_barrier(
        (grad_normed_two, grad_ffn, grad_down)
    )
    grad_ffn = [grad_ffn[..., :hidden_mine], grad_ffn[..., hidden_mine:]]
    (grad_middle,) = ffn_pull(grad_normed_two)
    grad_middle = grad_middle + cotangent[0].astype(FULL)
    grad_branch = grad_middle.astype(LOW)
    grad_scaled_own = jnp.stack([dot_right_t(grad_branch, part).astype(LOW) for part in out_parts], 1)
    grad_scaled_own = jnp.swapaxes(grad_scaled_own.reshape(tokens, dp, width, cubes, rows), 2, 3)
    grad_scaled_own = fiber_order(grad_scaled_own.reshape(tokens, D), width)

    grad_scaled = cube_turn(
        jnp.swapaxes(grad_scaled_own.reshape(tokens, width, mine), 0, 1), width
    ).reshape(count, mine)
    owners = []
    for row in range(dp):
        for chip in range(seq):
            block = (chip % width) * fiber + row * cubes + chip // width
            owners.append((row * seq + chip, block))
    groups = [list(range(first, first + width)) for first in range(0, seq, width)]
    branch_cube = lax.all_gather(grad_branch, "seq", axis_index_groups=groups, tiled=True)
    half = D // len(cube_orders(width, 2))
    down_parts = [down_w[:, at : at + half] for at in range(0, D, half)]
    result = middle + cube_sum_by_axes(tie(hidden, grad_branch), down_parts, dot_low, width)
    block_output = result.astype(LOW)[None]
    backs = delta_back(
        heads, mixed_in, cols, gain_row, prepared, recalled, grad_scaled, ()
    )
    end_back = backs[4]
    leaving = jnp.zeros((heads, HEAD, HEAD), FULL)
    for hop in range(cubes - 1):
        out = end_back
        if hop > 0:
            out = end_back + jnp.einsum("hji,hjk->hik", far, leaving, precision=HIGH)
        leaving = lax.ppermute(out, "seq", behind)
    grad_down = far_sum(grad_down, width, (leaving,))
    grad_hgate = near_sum(grad_ffn[0], "seq", width, cubes, (leaving,))
    grad_mixed, tail, edge, grad_taps = delta_pull(
        heads, mixed_in, taps_mine, cols, segs, prepared, states, delta, backs[:4], leaving,
        (),
    )
    grad_hup = near_sum(grad_ffn[1], "seq", width, cubes, (grad_hgate, leaving))
    grad_mixed = hint(grad_mixed, grad_hgate)
    grad_mixer = dot_left_t(normed, grad_mixed).reshape(dp, cubes, width, rows, -1)
    grad_mixer = near_sum(grad_mixer, "dp", 1, dp)
    from_next = lax.ppermute(edge.astype(LOW), "seq", behind).astype(FULL)
    grad_fixed = lax.dynamic_update_slice(
        grad_mixed[RIM:], (tail + from_next).astype(LOW), (count - SPAN, 0)
    )
    grad_taps = grad_taps[:CONV]
    mixer_parts = [mixer_w[at : at + half] for at in range(0, D, half)]
    grad_mixer = near_sum(grad_mixer, "seq", width, cubes, (grad_hup, grad_down)).astype(LOW)
    grad_normed = cube_sum_by_axes(grad_fixed, mixer_parts, dot_right_t, width)
    grad_normed = fiber_order(grad_normed, width)
    grad_oproj = chip_sum(dot_left_t(scaled, branch_cube).reshape(fiber, rows, D))
    grad_oproj = far_sum(grad_oproj, width)
    grad_oproj = lax.ppermute(grad_oproj.astype(LOW), both, owners).astype(FULL)
    grad_ffn = jnp.concatenate([grad_hgate.astype(LOW), grad_hup.astype(LOW)], -1)
    grad_ffn = cube_turn(tie(grad_ffn, block_output), width)
    taps_wide = lax.dynamic_update_index_in_dim(
        jnp.zeros((CONV, 3, width, mine), FULL), grad_taps.reshape(CONV, 3, mine), me, 2
    ).reshape(CONV, everyone, taps_each)
    taps_wide = jnp.swapaxes(taps_wide, 0, 1).reshape(everyone, CONV * taps_each)
    taps_own = sum_all(taps_wide)
    grad_mixer = cube_turn(tie(grad_mixer, grad_ffn, taps_own), width).astype(FULL)
    grad_ffn = grad_ffn.astype(FULL)

    def by_rows(grad):
        split = grad.reshape(width, rows, dp, cubes, units)
        return jnp.transpose(split, (1, 2, 3, 0, 4)).reshape(rows, -1)

    grad_hgate, grad_hup = by_rows(grad_ffn[..., :hidden_mine]), by_rows(grad_ffn[..., hidden_mine:])
    grad_mixer = jnp.swapaxes(grad_mixer, 0, 1)
    grad_wproj = jnp.swapaxes(grad_mixer[..., : 3 * mine].reshape(rows, width, 3, mine), 1, 2)
    grad_wproj = grad_wproj.reshape(rows, 3 * D)
    grad_wgate = grad_mixer[..., 3 * mine : 4 * mine].reshape(rows, D)
    grad_wbeta = grad_mixer[..., 4 * mine : 4 * mine + heads].reshape(rows, H)
    (grad_tokens,) = mix_pull(grad_normed)
    grad_input = (grad_tokens + grad_middle)[None]

    def gain_grad(gain, *pairs):
        terms = [row_sum(weight.astype(LOW).astype(FULL) * grad) for weight, grad in pairs]
        return sum(terms)[:, 0] / gain.astype(LOW).astype(FULL)

    grad_mgain = gain_grad(mix_gain, (w_project, grad_wproj), (w_gate, grad_wgate), (w_beta, grad_wbeta))
    grad_hgain = gain_grad(head_gain, (w_output, grad_oproj))
    grad_fgain = gain_grad(ffn_gain, (w_hidden_gate, grad_hgate), (w_hidden_up, grad_hup))
    return (
        block_output,
        grad_input,
        grad_mgain,
        grad_wproj,
        taps_own.reshape(CONV, taps_each),
        grad_wbeta,
        grad_wgate,
        grad_hgain,
        grad_oproj,
        grad_fgain,
        grad_hgate,
        grad_hup,
        grad_down,
    )


def solution(mesh):
    tokens = P("dp", "seq", None)
    vector = P(("dp", "seq"))
    matrix = P(("dp", "seq"), None)
    taps = P(None, ("dp", "seq"))
    in_specs = (tokens, P("dp", "seq"), vector, matrix, taps, matrix, matrix, vector, matrix)
    in_specs = in_specs + (vector, matrix, matrix, matrix, tokens)
    out_specs = (tokens, tokens, vector, matrix, taps, matrix, matrix, vector, matrix)
    out_specs = out_specs + (vector, matrix, matrix, matrix)
    return jax.shard_map(local, mesh=mesh, in_specs=in_specs, out_specs=out_specs, check_vma=False)
```

time: 5930 us -> 861 us (0.15)
  waiting for transfers between devices: 4940 us -> 268 us
  matrix products: 396 us -> 89.2 us
  blocking collectives: 213 us -> 0 us
  starting transfers between devices: 11.7 us -> 107 us
  Pallas kernels: 0 us -> 83.7 us
  other arithmetic: 204 us -> 132 us
    reduce_scatter x6 -> x0, waiting for transfers between devices: 4080 us -> none  [the longest x1 977 us: local(): lax.psum_scatter(grad_hup, ('dp', 'seq'), scatter_dimension=0, tiled=True)]
    all_gather x10 -> x1, waiting for transfers between devices: 799 us -> 0.01 us  [local(): lax.all_gather(grad_branch, 'seq', axis_index_groups=groups, tiled=True)]
    ppermute x3 -> x49, waiting for transfers between devices: 6.03 us -> 249 us  [the longest x44 241 us: swap(): lax.ppermute(values, axis, [(i, i ^ bit) for i in range(lax.axis_size(axi...]
    dot_general x72 -> x6, matrix products: 221 us -> 25.9 us  [dot_low(): return jnp.dot(left, right, preferred_element_type=FULL)]
    another operation x5 -> x15, other arithmetic: 161 us -> 7.01 us  [the longest x9 4.03 us: turned_about(): values.reshape(shape[:dim] + (count // (2 * bit), 2, bit) + shape[dim + 1:])]
    all_gather x2 -> x0, blocking collectives: 134 us -> none  [the longest x1 68.1 us: local(): lax.all_gather(taps_low, ('dp', 'seq'), axis=1, tiled=True)]
    pallas_call x0 -> x11, Pallas kernels: none -> 83.7 us  [the longest x4 83.7 us: on_chip(): pl.pallas_call(lambda *refs: body(*refs[:used], *refs[used + spare:]), ou...]
    unnamed x2 -> x0, blocking collectives: 79.4 us -> none
  transfers between devices with their start and end apart: 21 -> 60, of which waited for: 17 -> 23; matrix products, arithmetic and copies ran while one was open for 9% -> 34% of each run, Pallas kernels for 0% -> 10%
where the time goes in v1:
time: 861 us; the launch traced here: 845 us
  waiting for transfers between devices  268 us (31%)
  local copies, waits for them, and re-layouts  149 us (17%)
  other arithmetic  132 us (15%)
  starting transfers between devices  107 us (12%)
  matrix products  89.2 us (10%)
  Pallas kernels  83.7 us (10%)
  between operations  16.6 us (2%)
    ppermute x44, waiting for transfers between devices, swap(): lax.ppermute(values, axis, [(i, i ^ bit) for i in range(lax.axis_size(axi...  241 us
    pallas_call x4, Pallas kernels, on_chip(): pl.pallas_call(lambda *refs: body(*refs[:used], *refs[used + spare:]), ou...  83.7 us
    ppermute x44, starting transfers between devices, swap(): lax.ppermute(values, axis, [(i, i ^ bit) for i in range(lax.axis_size(axi...  51.9 us
    all_to_all x8, starting transfers between devices, cube_turn(): lax.all_to_all(values, 'seq', 0, 0, axis_index_groups=groups, tiled=True)  38.7 us
    select_n x28, other arithmetic, grow(): jnp.where(own, jnp.expand_dims(values, dim), jnp.expand_dims(other, dim))  36.6 us
    dot_general x6, matrix products, dot_right_t(): lax.dot_general(left, right, (((1,), (1,)), ((), ())), preferred_element_...  33.5 us
    dot_general x4, matrix products, dot_left_t(): lax.dot_general(left, right, (((0,), (0,)), ((), ())), preferred_element_...  29.8 us
    unnamed x234, local copies, waits for them, and re-layouts  27.5 us
  transfers between devices with their start and end apart: 60, of which 23 were waited for; matrix products, arithmetic and copies ran while one was open for 34% of the time, Pallas kernels for 10%

profile of v1, /device:TPU:0, one launch (start us, length us, event | category | flops | bytes accessed | tf_op | source)
XLA Modules:
  0.0 845.0 jit_solution(2505645130343878429)
XLA Ops:
  20.3 4.9 all-to-all-start
  34.1 3.8 all-to-all-start.1
  52.5 23.6 %collective-permute-done.1 = bf16[1,2,1,2,128,1024]{5,4,1,3,2,0:T(8,128)(2,1)} collective-permute-done((bf16[1,2,1,2,128,1024]{5,4,1,3,2,0:T(8,128)(2,1)}, bf16[1,2,1,2,128,1024]{5,4,1,3,2,0:T(8,128)(2,1)}, u32[]{:S(2)}, u32[]{:S(2)}) %collective-permute-start.1) | collective-permute-done | bytes 1048608 | tf_op jit(solution)/shard_map/ppermute | solution.py:45
  101.5 4.5 reshape.600
  112.6 4.7 all-to-all-start.4
  117.3 22.5 %collective-permute-done.7 = bf16[1,8,64,1152]{3,2,1,0:T(8,128)(2,1)} collective-permute-done((bf16[1,8,64,1152]{3,2,1,0:T(8,128)(2,1)S(1)}, bf16[1,8,64,1152]{3,2,1,0:T(8,128)(2,1)}, u32[]{:S(2)}, u32[]{:S(2)}) %collective-permute-start.7) | collective-permute-done | bytes 1179680 | tf_op jit(solution)/shard_map/ppermute | solution.py:45
  139.8 3.1 pad_maximum_fusion.6
  155.4 3.8 fusion.4
  159.9 3.1 fusion
  165.9 7.8 fusion.62.refs_0_
  175.0 13.3 %collective-permute-done.10 = bf16[1,64,2048]{2,1,0:T(8,128)(2,1)S(1)} collective-permute-done((bf16[1,64,2048]{2,1,0:T(8,128)(2,1)S(1)}, bf16[1,64,2048]{2,1,0:T(8,128)(2,1)S(1)}, u32[]{:S(2)}, u32[]{:S(2)}) %collective-permute-start.10) | collective-permute-done | bytes 262176 | tf_op jit(solution)/shard_map/ppermute | solution.py:45
  190.9 4.7 all-to-all-start.3
  203.4 29.9 %shard_map.237 = (f32[16,128,128]{2,1,0:T(8,128)}, f32[16,128,128]{2,1,0:T(8,128)}, f32[16,128,128]{2,1,0:T(8,128)}, f32[16,128,128]{2,1,0:T(8,128)}, f32[16,128...) custom-call(f32[1040,1152]{1,0:T(8,128)} %fusion.62.refs_0_, ...), custom_call_target="tpu_custom_call" | custom-call | flops 32212254720 | bytes 20971520 | tf_op jit(solution)/shard_map/pallas_call | solution.py:543
  235.2 37.8 %collective-permute-done.21 = bf16[1,8,64,1408]{3,2,1,0:T(8,128)(2,1)S(1)} collective-permute-done((bf16[1,8,64,1408]{3,2,1,0:T(8,128)(2,1)}, bf16[1,8,64,1408]{3,2,1,0:T(8,128)(2,1)S(1)}, u32[]{:S(2)}, u32[]{:S(2)}) %collective-permute-start.21) | collective-permute-done | bytes 1441824 | tf_op jit(solution)/shard_map/ppermute | solution.py:45
  273.0 3.3 maximum_bitcast_fusion
  276.4 6.7 all-to-all-done.3
  283.0 12.9 %collective-permute-done.23 = bf16[1,176,2048]{2,1,0:T(8,128)(2,1)S(1)} collective-permute-done((bf16[1,176,2048]{2,1,0:T(8,128)(2,1)S(1)}, bf16[1,176,2048]{2,1,0:T(8,128)(2,1)S(1)}, u32[]{:S(2)}, u32[]{:S(2)}) %collective-permute-start.23) | collective-permute-done | bytes 720928 | tf_op jit(solution)/shard_map/ppermute | solution.py:45
  296.9 11.1 %shard_map.238 = (f32[16,128,128]{2,1,0:T(8,128)}, f32[16,128,128]{2,1,0:T(8,128)}, f32[16,128,128]{2,1,0:T(8,128)}, bf16[1024,256]{1,0:T(8,128)(2,1)}) custom-call(f32[1040,1152]{1,0:T(8,128)} %fusion.62.refs_0_, f32[1032,8]{1,0:T(8,128)} %pad.5.refs_2_.refs_1_, f32[1,256]{1,0:T(1,128)} %bitcast.414, f32[16,128,128]{2,1,0:T(8,128)} %get-tuple-element.46.refs_3_.refs_4_, ...), custom_call_target="tpu_custom_call" | custom-call | flops 11811160064 | bytes 20971520 | tf_op jit(solution)/shard_map/pallas_call | solution.py:543
  308.0 7.2 all-to-all-start.2
  315.6 8.1 all-to-all-done.2
  328.3 5.7 pad_maximum_fusion
  337.0 3.0 multiply_reduce_fusion.4
  363.9 7.8 collective-permute-done.19
  378.0 4.7 collective-permute-done.17
  386.0 6.7 fusion.16
  392.8 6.0 fusion.11
  398.7 10.4 %convolution_convert_fusion = bf16[1024,2048]{1,0:T(8,128)(2,1)} fusion(bf16[2048,1408]{1,0:T(8,128)(2,1)S(1)} %bitcast.334, bf16[1024,704]{1,0:T(8,128)(2,1)} %get-tuple-element.86, bf16[1024,704]{1,0:T(8,128)(2,1)} %get-tuple-element.85), kind=kOutput, calls=%fused_computation.26 | convolution fusion | flops 5913444352 | bytes 12845056 | tf_op jit(solution)/shard_map/dot_general | solution.py:37
  409.1 4.5 all-to-all-start.5
  413.7 13.0 %fusion.15 = f32[2048,1408]{1,0:T(8,128)} fusion(bf16[1024,704]{1,0:T(8,128)(2,1)} %get-tuple-element.86, bf16[1024,704]{1,0:T(8,128)(2,1)} %get-tuple-element.85, bf16[1024,768]{1,0:T(8,128)(2,1)} %copy-done.59, bf16[1024,640]{1,0:T(8,128)(2,1)} %copy-done.63, bf16[1024,640]{1,0:T(8,128)(2,1)} %copy-done.64), kind=kOutput, calls=%fused_computation.63 | convolution fusion | flops 5923930112 | bytes 18612224 | tf_op jit(solution)/shard_map/dot_general | solution.py:33
  426.8 4.5 slice.293
  434.2 5.8 fusion.5
  444.5 3.5 bitcast_select_fusion
  448.0 5.6 slice.227
  453.6 3.3 add_bitcast_fusion.1
  456.9 6.6 add_bitcast_fusion
  472.8 3.9 convolution_convert_fusion.2
  476.7 3.9 convolution_convert_fusion.1
  482.3 5.3 all-to-all-start.6
  487.6 3.8 fusion.17
  504.5 4.1 all-to-all-done.6
  509.4 12.5 %shard_map.240 = (f32[16,128,128]{2,1,0:T(8,128)}, f32[16,128,128]{2,1,0:T(8,128)}, f32[16,128,128]{2,1,0:T(8,128)}, bf16[1024,256]{1,0:T(8,128)(2,1)}, f32[2,128,128]{2,1,0:T(8,128)}) custom-call(f32[1040,1152]{1,0:T(8,128)} %fusion.62.refs_0_, f32[1032,8]{1,0:T(8,128)} %pad.5.refs_2_.refs_1_, f32[1,256]{1,0:T(1,128)} %bitcast.415, ...), custom_call_target="tpu_custom_call" | custom-call | flops 12884901888 | bytes 20971520 | tf_op jit(solution)/shard_map/pallas_call | solution.py:543
  525.6 7.7 collective-permute-done.33.refs_15_.refs_1_.refs_2_
  537.9 25.2 %collective-permute-done.27 = bf16[2,2,1,128,1024]{4,3,2,1,0:T(8,128)(2,1)} collective-permute-done((bf16[2,2,1,128,1024]{4,3,2,1,0:T(8,128)(2,1)S(1)}, bf16[2,2,1,128,1024]{4,3,2,1,0:T(8,128)(2,1)}, u32[]{:S(2)}, u32[]{:S(2)}) %collective-permute-start.27) | collective-permute-done | bytes 1048608 | tf_op jit(solution)/shard_map/ppermute | solution.py:45
  566.1 3.2 collective-permute-start.28
  569.4 30.1 %shard_map.241 = (bf16[1040,1152]{1,0:T(8,128)(2,1)}, f32[8,768]{1,0:T(8,128)}, f32[8,768]{1,0:T(8,128)}, f32[8,768]{1,0:T(8,128)}) custom-call(f32[1040,1152]{1,0:T(8,128)} %fusion.62.refs_0_, f32[4,768]{1,0:T(4,128)} %bitcast.411, f32[1032,8]{1,0:T(8,128)} %pad.5.refs_2_.refs_1_, f32[8,1,128]{2,1,0:T(1,128)} %bitcast.404, ...), custom_call_target="tpu_custom_call" | custom-call | flops 32212254720 | bytes 20971520 | tf_op jit(solution)/shard_map/pallas_call | solution.py:543
  601.6 3.6 collective-permute-start.44
  607.0 4.5 all-to-all-start.8
  620.5 3.0 fusion.66
  623.5 7.3 fusion.60
  631.7 6.5 fusion.74
  652.1 5.0 slice.232
  667.7 5.3 collective-permute-done.36
  675.6 19.4 %collective-permute-done.43 = bf16[1,8,64,704]{3,2,1,0:T(8,128)(2,1)S(1)} collective-permute-done((bf16[1,8,64,704]{3,2,1,0:T(8,128)(2,1)S(1)}, bf16[1,8,64,704]{3,2,1,0:T(8,128)(2,1)S(1)}, u32[]{:S(2)}, u32[]{:S(2)}) %collective-permute-start.43) | collective-permute-done | bytes 720928 | tf_op jit(solution)/shard_map/ppermute | solution.py:45
  694.9 3.0 fusion.67
  698.3 6.0 collective-permute-done.37
  718.9 3.2 fusion.28
  722.1 3.9 all-to-all-start.7
  726.0 3.6 convert_add_fusion
  734.6 3.6 fusion.75
  740.4 42.3 %collective-permute-done.45 = bf16[1,8,64,1152]{3,2,1,0:T(8,128)(2,1)S(1)} collective-permute-done((bf16[1,8,64,1152]{3,2,1,0:T(8,128)(2,1)}, bf16[1,8,64,1152]{3,2,1,0:T(8,128)(2,1)S(1)}, u32[]{:S(2)}, u32[]{:S(2)}) %collective-permute-start.45) | collective-permute-done | bytes 1179680 | tf_op jit(solution)/shard_map/ppermute | solution.py:45
  785.2 4.6 all-to-all-start.9
  792.7 4.7 reshape.618
  802.4 5.2 reshape.616
  816.8 9.1 %collective-permute-done.47 = bf16[1,1,64,2048]{3,2,1,0:T(8,128)(2,1)S(1)} collective-permute-done((bf16[1,1,64,2048]{3,2,1,0:T(8,128)(2,1)S(1)}, bf16[1,1,64,2048]{3,2,1,0:T(8,128)(2,1)S(1)}, u32[]{:S(2)}, u32[]{:S(2)}) %collective-permute-start.47) | collective-permute-done | bytes 262176 | tf_op jit(solution)/shard_map/ppermute | solution.py:45
  (576 shorter events, 276.9 us)
Async XLA Ops:
  14.6 23.3 %collective-permute-start = (bf16[1,1,1,2,128,1024]{5,4,3,2,1,0:T(8,128)(2,1)}, bf16[1,1,1,2,128,1024]{5,4,3,2,1,0:T(8,128)(2,1)}, u32[]{:S(2)}, u32[]{:S(2)}) collective-permute-start(bf16[1,1,1,2,128,1024]{5,4,3,2,1,0:T(8,128)(2,1)} %get-tuple-element.97), channel_id=1, source_target_pairs={{0,2},{1,3},{2,0},{3,1},{4,6},{5,7},{6,4},{7,5},{8,10},{9,11},{10,... | collective-permute-start | bytes 1572872 | tf_op jit(solution)/shard_map/ppermute | solution.py:45
  20.3 13.1 %all-to-all-start = ((bf16[32,2,544]{2,1,0:T(2,128)(2,1)}), bf16[32,2,544]{2,1,0:T(2,128)(2,1)S(1)}, u32[]{:S(2)}, u32[]{:S(2)}) async-start(bf16[32,2,544]{2,1,0:T(2,128)(2,1)} %reshape.642), calls=%async_computation | async-start | bytes 163840 | tf_op jit(solution)/shard_map/all_to_all | solution.py:126
  25.2 21.5 %collective-permute-start.3 = (bf16[1,1,1,2,128,1024]{5,4,3,2,1,0:T(8,128)(2,1)}, bf16[1,1,1,2,128,1024]{5,4,3,2,1,0:T(8,128)(2,1)}, u32[]{:S(2)}, u32[]{:S(2)}) collective-permute-start(bf16[1,1,1,2,128,1024]{5,4,3,2,1,0:T(8,128)(2,1)} %get-tuple-element.98), channel_id=1, source_target_pairs={{0,4},{1,5},{2,6},{3,7},{4,0},{5,1},{6,2},{7,3},{8,12},{9,13},{10,... | collective-permute-start | bytes 1572872 | tf_op jit(solution)/shard_map/ppermute | solution.py:45
  33.5 49.1 %copy-start.85 = (pred[2]{0:T(512)(128)(4,1)}, pred[2]{0:T(512)(128)(4,1)S(1)}, u32[]{:S(2)}) copy-start(pred[2]{0:T(512)(128)(4,1)S(1)} %iota_compare_fusion.2) | copy-start | bytes 10
  34.1 52.8 %all-to-all-start.1 = ((bf16[8,64,1152]{2,1,0:T(8,128)(2,1)}), bf16[8,64,1152]{2,1,0:T(8,128)(2,1)S(1)}, u32[]{:S(2)}, u32[]{:S(2)}) async-start(bf16[8,64,1152]{2,1,0:T(8,128)(2,1)} %copy.194), calls=%async_computation.1 | async-start | bytes 2359296 | tf_op jit(solution)/shard_map/all_to_all | solution.py:120
  40.2 35.8 %collective-permute-start.1 = (bf16[1,2,1,2,128,1024]{5,4,1,3,2,0:T(8,128)(2,1)}, bf16[1,2,1,2,128,1024]{5,4,1,3,2,0:T(8,128)(2,1)}, u32[]{:S(2)}, u32[]{:S(2)}) collective-permute-start(bf16[1,2,1,2,128,1024]{5,4,1,3,2,0:T(8,128)(2,1)} %broadcast_select_fusion.10), channel_id=1, source_target_pairs={{0,4},{1,5},{2,6},{3,7},{4,0},{5,1},{6,2},{7,3},{8,12},{9,13},{10,... | collective-permute-start | bytes 3145736 | tf_op jit(solution)/shard_map/ppermute | solution.py:45
  45.3 47.2 %copy-start.87 = (pred[2]{0:T(512)(128)(4,1)}, pred[2]{0:T(512)(128)(4,1)S(1)}, u32[]{:S(2)}) copy-start(pred[2]{0:T(512)(128)(4,1)S(1)} %iota_compare_fusion.4) | copy-start | bytes 10
  46.6 43.1 %copy-start.79 = (pred[2]{0:T(512)(128)(4,1)}, pred[2]{0:T(512)(128)(4,1)S(1)}, u32[]{:S(2)}) copy-start(pred[2]{0:T(512)(128)(4,1)S(1)} %iota_compare_fusion.3) | copy-start | bytes 10
  49.0 33.6 %collective-permute-start.4 = (bf16[2,1,1,2,128,1024]{5,4,0,3,2,1:T(8,128)(2,1)}, bf16[2,1,1,2,128,1024]{5,4,0,3,2,1:T(8,128)(2,1)}, u32[]{:S(2)}, u32[]{:S(2)}) collective-permute-start(bf16[2,1,1,2,128,1024]{5,4,0,3,2,1:T(8,128)(2,1)} %broadcast_select_fusion.8), channel_id=1, source_target_pairs={{0,1},{1,0},{2,3},{3,2},{4,5},{5,4},{6,7},{7,6},{8,9},{9,8},{10,11... | collective-permute-start | bytes 3145736 | tf_op jit(solution)/shard_map/ppermute | solution.py:45
  78.9 64.0 %collective-permute-start.2 = (bf16[2,2,1,2,128,1024]{5,4,1,0,3,2:T(8,128)(2,1)}, bf16[2,2,1,2,128,1024]{5,4,1,0,3,2:T(8,128)(2,1)}, u32[]{:S(2)}, u32[]{:S(2)}) collective-permute-start(bf16[2,2,1,2,128,1024]{5,4,1,0,3,2:T(8,128)(2,1)} %broadcast_select_fusion.5), channel_id=1, source_target_pairs={{0,1},{1,0},{2,3},{3,2},{4,5},{5,4},{6,7},{7,6},{8,9},{9,8},{10,11... | collective-permute-start | bytes 6291464 | tf_op jit(solution)/shard_map/ppermute | solution.py:45
  85.4 60.7 %collective-permute-start.5 = (bf16[2,1,2,2,128,1024]{5,4,2,0,3,1:T(8,128)(2,1)}, bf16[2,1,2,2,128,1024]{5,4,2,0,3,1:T(8,128)(2,1)}, u32[]{:S(2)}, u32[]{:S(2)}) collective-permute-start(bf16[2,1,2,2,128,1024]{5,4,2,0,3,1:T(8,128)(2,1)} %broadcast_select_fusion.3), channel_id=1, source_target_pairs={{0,2},{1,3},{2,0},{3,1},{4,6},{5,7},{6,4},{7,5},{8,10},{9,11},{10,... | collective-permute-start | bytes 6291464 | tf_op jit(solution)/shard_map/ppermute | solution.py:45
  86.9 52.9 %collective-permute-start.7 = (bf16[1,8,64,1152]{3,2,1,0:T(8,128)(2,1)S(1)}, bf16[1,8,64,1152]{3,2,1,0:T(8,128)(2,1)}, u32[]{:S(2)}, u32[]{:S(2)}) collective-permute-start(bf16[1,8,64,1152]{3,2,1,0:T(8,128)(2,1)S(1)} %bitcast.335), channel_id=1, source_target_pairs={{0,8},{1,9},{2,10},{3,11},{4,12},{5,13},{6,14},{7,15},{8,0},{9,1},... | collective-permute-start | bytes 3538952 | tf_op jit(solution)/shard_map/ppermute | solution.py:45
  112.6 75.7 %all-to-all-start.4 = ((bf16[8,64,1408]{2,1,0:T(8,128)(2,1)}), bf16[8,64,1408]{2,1,0:T(8,128)(2,1)}, u32[]{:S(2)}, u32[]{:S(2)}) async-start(bf16[8,64,1408]{2,1,0:T(8,128)(2,1)} %pad_maximum_fusion.11), calls=%async_computation.4 | async-start | bytes 2883584 | tf_op jit(solution)/shard_map/all_to_all | solution.py:120
  142.9 20.2 %collective-permute-start.8 = (bf16[1,2,8,64,1152]{4,3,2,1,0:T(8,128)(2,1)S(1)}, bf16[1,2,8,64,1152]{4,3,2,1,0:T(8,128)(2,1)}, u32[]{:S(2)}, u32[]{:S(2)}) collective-permute-start(bf16[1,2,8,64,1152]{4,3,2,1,0:T(8,128)(2,1)S(1)} %get-tuple-element.91), channel_id=1, source_target_pairs={{0,16},{16,0},{1,17},{17,1},{2,18},{18,2},{3,19},{19,3},{4,20},{20... | collective-permute-start | bytes 7077896 | tf_op jit(solution)/shard_map/ppermute | solution.py:45
  153.4 5.8 collective-permute-start.6
  173.7 14.6 %collective-permute-start.10 = (bf16[1,64,2048]{2,1,0:T(8,128)(2,1)S(1)}, bf16[1,64,2048]{2,1,0:T(8,128)(2,1)S(1)}, u32[]{:S(2)}, u32[]{:S(2)}) collective-permute-start(bf16[1,64,2048]{2,1,0:T(8,128)(2,1)S(1)} %bitcast.379), channel_id=1, source_target_pairs={{0,8},{1,9},{2,10},{3,11},{4,12},{5,13},{6,14},{7,15},{8,0},{9,1},... | collective-permute-start | bytes 786440 | tf_op jit(solution)/shard_map/ppermute | solution.py:45
  190.9 92.1 %all-to-all-start.3 = ((bf16[8,2,64,2048]{3,2,1,0:T(8,128)(2,1)}), bf16[8,2,64,2048]{3,2,1,0:T(8,128)(2,1)}, u32[]{:S(2)}, u32[]{:S(2)}) async-start(bf16[8,2,64,2048]{3,2,1,0:T(8,128)(2,1)} %broadcast_in_dim.484), calls=%async_computation.3 | async-start | bytes 8388608 | tf_op jit(solution)/shard_map/all_to_all | solution.py:120
  200.5 72.5 %collective-permute-start.21 = (bf16[1,8,64,1408]{3,2,1,0:T(8,128)(2,1)}, bf16[1,8,64,1408]{3,2,1,0:T(8,128)(2,1)S(1)}, u32[]{:S(2)}, u32[]{:S(2)}) collective-permute-start(bf16[1,8,64,1408]{3,2,1,0:T(8,128)(2,1)} %bitcast.75), channel_id=1, source_target_pairs={{0,8},{1,9},{2,10},{3,11},{4,12},{5,13},{6,14},{7,15},{8,0},{9,1},... | collective-permute-start | bytes 4325384 | tf_op jit(solution)/shard_map/ppermute | solution.py:45
  200.5 95.4 %collective-permute-start.23 = (bf16[1,176,2048]{2,1,0:T(8,128)(2,1)S(1)}, bf16[1,176,2048]{2,1,0:T(8,128)(2,1)S(1)}, u32[]{:S(2)}, u32[]{:S(2)}) collective-permute-start(bf16[1,176,2048]{2,1,0:T(8,128)(2,1)S(1)} %bitcast.352), channel_id=1, source_target_pairs={{0,8},{1,9},{2,10},{3,11},{4,12},{5,13},{6,14},{7,15},{8,0},{9,1},... | collective-permute-start | bytes 2162696 | tf_op jit(solution)/shard_map/ppermute | solution.py:45
  233.3 62.9 %collective-permute-start.9 = (f32[2,128,128]{2,1,0:T(8,128)}, f32[2,128,128]{2,1,0:T(8,128)S(1)}, u32[]{:S(2)}, u32[]{:S(2)}) collective-permute-start(f32[2,128,128]{2,1,0:T(8,128)} %get-tuple-element.52), channel_id=1, source_target_pairs={{0,8},{1,9},{2,10},{3,11},{4,12},{5,13},{6,14},{7,15},{16,24},{17,... | collective-permute-start | bytes 393224 | tf_op jit(solution)/shard_map/ppermute | solution.py:735
  276.4 52.0 %collective-permute-start.22 = (bf16[1,2,8,64,1408]{4,3,2,1,0:T(8,128)(2,1)}, bf16[1,2,8,64,1408]{4,3,2,1,0:T(8,128)(2,1)}, u32[]{:S(2)}, u32[]{:S(2)}) collective-permute-start(bf16[1,2,8,64,1408]{4,3,2,1,0:T(8,128)(2,1)} %maximum_bitcast_fusion), channel_id=1, source_target_pairs={{0,16},{16,0},{1,17},{17,1},{2,18},{18,2},{3,19},{19,3},{4,20},{20... | collective-permute-start | bytes 8650760 | tf_op jit(solution)/shard_map/ppermute | solution.py:45
  283.0 54.0 %collective-permute-start.11 = (bf16[1024,2048]{1,0:T(8,128)(2,1)}, bf16[1024,2048]{1,0:T(8,128)(2,1)}, u32[]{:S(2)}, u32[]{:S(2)}) collective-permute-start(bf16[1024,2048]{1,0:T(8,128)(2,1)} %bitcast.51), channel_id=1, source_target_pairs={{0,16},{16,0},{1,17},{17,1},{2,18},{18,2},{3,19},{19,3},{4,20},{20... | collective-permute-start | bytes 12582920 | tf_op jit(solution)/shard_map/ppermute | solution.py:45
  296.1 30.1 %collective-permute-start.24 = (bf16[2,176,2048]{2,1,0:T(8,128)(2,1)S(1)}, bf16[2,176,2048]{2,1,0:T(8,128)(2,1)S(1)}, u32[]{:S(2)}, u32[]{:S(2)}) collective-permute-start(bf16[2,176,2048]{2,1,0:T(8,128)(2,1)S(1)} %broadcast_select_fusion.7), channel_id=1, source_target_pairs={{0,16},{16,0},{1,17},{17,1},{2,18},{18,2},{3,19},{19,3},{4,20},{20... | collective-permute-start | bytes 4325384 | tf_op jit(solution)/shard_map/ppermute | solution.py:45
  308.0 15.7 %all-to-all-start.2 = ((bf16[8,128,256]{2,1,0:T(8,128)(2,1)}), bf16[8,128,256]{2,1,0:T(8,128)(2,1)S(1)}, u32[]{:S(2)}, u32[]{:S(2)}) async-start(bf16[8,128,256]{2,1,0:T(8,128)(2,1)} %bitcast.389), calls=%async_computation.2 | async-start | bytes 1048576 | tf_op jit(solution)/shard_map/all_to_all | solution.py:120
  343.4 5.6 collective-permute-start.15
  344.6 12.2 %collective-permute-start.18 = (bf16[1,1,1,128,768]{3,4,2,1,0:T(8,128)(2,1)}, bf16[1,1,1,128,768]{3,4,2,1,0:T(8,128)(2,1)}, u32[]{:S(2)}, u32[]{:S(2)}) collective-permute-start(bf16[1,1,1,128,768]{3,4,2,1,0:T(8,128)(2,1)} %get-tuple-element.105), channel_id=1, source_target_pairs={{0,4},{1,5},{2,6},{3,7},{4,0},{5,1},{6,2},{7,3},{8,12},{9,13},{10,... | collective-permute-start | bytes 589832 | tf_op jit(solution)/shard_map/ppermute | solution.py:45
  346.2 7.0 collective-permute-start.12
  350.9 10.9 %collective-permute-start.16 = (bf16[1,2,1,128,640]{4,3,1,2,0:T(8,128)(2,1)}, bf16[1,2,1,128,640]{4,3,1,2,0:T(8,128)(2,1)}, u32[]{:S(2)}, u32[]{:S(2)}) collective-permute-start(bf16[1,2,1,128,640]{4,3,1,2,0:T(8,128)(2,1)} %broadcast_select_fusion.22), channel_id=1, source_target_pairs={{0,4},{1,5},{2,6},{3,7},{4,0},{5,1},{6,2},{7,3},{8,12},{9,13},{10,... | collective-permute-start | bytes 983048 | tf_op jit(solution)/shard_map/ppermute | solution.py:45
  355.1 18.2 %collective-permute-start.13 = (bf16[1,1,2,128,640]{4,3,2,1,0:T(8,128)(2,1)}, bf16[1,1,2,128,640]{4,3,2,1,0:T(8,128)(2,1)}, u32[]{:S(2)}, u32[]{:S(2)}) collective-permute-start(bf16[1,1,2,128,640]{4,3,2,1,0:T(8,128)(2,1)} %broadcast_select_fusion.24), channel_id=1, source_target_pairs={{0,2},{1,3},{2,0},{3,1},{4,6},{5,7},{6,4},{7,5},{8,10},{9,11},{10,... | collective-permute-start | bytes 983048 | tf_op jit(solution)/shard_map/ppermute | solution.py:45
  359.6 12.1 %collective-permute-start.19 = (bf16[2,1,1,128,768]{4,3,0,2,1:T(8,128)(2,1)S(1)}, bf16[2,1,1,128,768]{4,3,0,2,1:T(8,128)(2,1)S(1)}, u32[]{:S(2)}, u32[]{:S(2)}) collective-permute-start(bf16[2,1,1,128,768]{4,3,0,2,1:T(8,128)(2,1)S(1)} %broadcast_select_fusion.20), channel_id=1, source_target_pairs={{0,1},{1,0},{2,3},{3,2},{4,5},{5,4},{6,7},{7,6},{8,9},{9,8},{10,11... | collective-permute-start | bytes 1179656 | tf_op jit(solution)/shard_map/ppermute | solution.py:45
  362.9 19.8 %collective-permute-start.17 = (bf16[2,2,1,128,640]{4,3,1,0,2:T(8,128)(2,1)S(1)}, bf16[2,2,1,128,640]{4,3,1,0,2:T(8,128)(2,1)S(1)}, u32[]{:S(2)}, u32[]{:S(2)}) collective-permute-start(bf16[2,2,1,128,640]{4,3,1,0,2:T(8,128)(2,1)S(1)} %broadcast_select_fusion.16), channel_id=1, source_target_pairs={{0,1},{1,0},{2,3},{3,2},{4,5},{5,4},{6,7},{7,6},{8,9},{9,8},{10,11... | collective-permute-start | bytes 1966088 | tf_op jit(solution)/shard_map/ppermute | solution.py:45
  371.8 13.9 %collective-permute-start.20 = (bf16[2,1,2,128,768]{4,3,2,0,1:T(8,128)(2,1)S(1)}, bf16[2,1,2,128,768]{4,3,2,0,1:T(8,128)(2,1)S(1)}, u32[]{:S(2)}, u32[]{:S(2)}) collective-permute-start(bf16[2,1,2,128,768]{4,3,2,0,1:T(8,128)(2,1)S(1)} %broadcast_select_fusion.14), channel_id=1, source_target_pairs={{0,2},{1,3},{2,0},{3,1},{4,6},{5,7},{6,4},{7,5},{8,10},{9,11},{10,... | collective-permute-start | bytes 2359304 | tf_op jit(solution)/shard_map/ppermute | solution.py:45
  374.5 11.0 %collective-permute-start.14 = (bf16[1,2,2,128,640]{4,3,2,1,0:T(8,128)(2,1)S(1)}, bf16[1,2,2,128,640]{4,3,2,1,0:T(8,128)(2,1)S(1)}, u32[]{:S(2)}, u32[]{:S(2)}) collective-permute-start(bf16[1,2,2,128,640]{4,3,2,1,0:T(8,128)(2,1)S(1)} %broadcast_select_fusion.18), channel_id=1, source_target_pairs={{0,4},{1,5},{2,6},{3,7},{4,0},{5,1},{6,2},{7,3},{8,12},{9,13},{10,... | collective-permute-start | bytes 1966088 | tf_op jit(solution)/shard_map/ppermute | solution.py:45
  409.1 54.4 %all-to-all-start.5 = ((bf16[8,128,2048]{2,1,0:T(8,128)(2,1)}), bf16[8,128,2048]{2,1,0:T(8,128)(2,1)}, u32[]{:S(2)}, u32[]{:S(2)}) async-start(bf16[8,128,2048]{2,1,0:T(8,128)(2,1)} %bitcast.346), calls=%async_computation.5 | async-start | bytes 8388608 | tf_op jit(solution)/shard_map/all_to_all | solution.py:120
  413.7 320.9 %all-gather.2.cloned.1.call-start = ((), (), s32[]{:S(2)}) async-start(), calls=%async_computation.10 | async-start | bytes 4718592 | tf_op jit(solution)/shard_map/all_gather | solution.py:786
  431.2 25.7 %collective-permute-start.25 = (bf16[1,2,8,64,1408]{4,3,2,1,0:T(8,128)(2,1)}, bf16[1,2,8,64,1408]{4,3,2,1,0:T(8,128)(2,1)}, u32[]{:S(2)}, u32[]{:S(2)}) collective-permute-start(bf16[1,2,8,64,1408]{4,3,2,1,0:T(8,128)(2,1)} %bitcast.86), channel_id=1, source_target_pairs={{0,16},{16,0},{1,17},{17,1},{2,18},{18,2},{3,19},{19,3},{4,20},{20... | collective-permute-start | bytes 8650760 | tf_op jit(solution)/shard_map/ppermute | solution.py:45
  443.7 9.8 %collective-permute-start.26 = (bf16[1,2,176,2048]{3,2,1,0:T(8,128)(2,1)}, bf16[1,2,176,2048]{3,2,1,0:T(8,128)(2,1)}, u32[]{:S(2)}, u32[]{:S(2)}) collective-permute-start(bf16[1,2,176,2048]{3,2,1,0:T(8,128)(2,1)} %dynamic-slice_convert_fusion), channel_id=1, source_target_pairs={{0,16},{16,0},{1,17},{17,1},{2,18},{18,2},{3,19},{19,3},{4,20},{20... | collective-permute-start | bytes 4325384 | tf_op jit(solution)/shard_map/ppermute | solution.py:45
  482.3 26.4 %all-to-all-start.6 = ((bf16[8,128,256]{2,1,0:T(8,128)(2,1)}), bf16[8,128,256]{2,1,0:T(8,128)(2,1)S(1)}, u32[]{:S(2)}, u32[]{:S(2)}) async-start(bf16[8,128,256]{2,1,0:T(8,128)(2,1)} %bitcast.107), calls=%async_computation.6 | async-start | bytes 1048576 | tf_op jit(solution)/shard_map/all_to_all | solution.py:120
  494.9 40.6 %collective-permute-start.30 = (bf16[2,1,2,128,1024]{4,3,2,1,0:T(8,128)(2,1)}, bf16[2,1,2,128,1024]{4,3,2,1,0:T(8,128)(2,1)}, u32[]{:S(2)}, u32[]{:S(2)}) collective-permute-start(bf16[2,1,2,128,1024]{4,3,2,1,0:T(8,128)(2,1)} %dynamic-slice_convert_fusion.3), channel_id=1, source_target_pairs={{0,2},{1,3},{2,0},{3,1},{4,6},{5,7},{6,4},{7,5},{8,10},{9,11},{10,... | collective-permute-start | bytes 3145736 | tf_op jit(solution)/shard_map/ppermute | solution.py:45
  500.9 62.1 %collective-permute-start.27 = (bf16[2,2,1,128,1024]{4,3,2,1,0:T(8,128)(2,1)S(1)}, bf16[2,2,1,128,1024]{4,3,2,1,0:T(8,128)(2,1)}, u32[]{:S(2)}, u32[]{:S(2)}) collective-permute-start(bf16[2,2,1,128,1024]{4,3,2,1,0:T(8,128)(2,1)S(1)} %dynamic-slice_convert_fusion.4), channel_id=1, source_target_pairs={{0,1},{1,0},{2,3},{3,2},{4,5},{5,4},{6,7},{7,6},{8,9},{9,8},{10,11... | collective-permute-start | bytes 3145736 | tf_op jit(solution)/shard_map/ppermute | solution.py:45
  522.0 11.4 %collective-permute-start.33 = (f32[2,128,128]{2,1,0:T(8,128)}, f32[2,128,128]{2,1,0:T(8,128)S(1)}, u32[]{:S(2)}, u32[]{:S(2)}) collective-permute-start(f32[2,128,128]{2,1,0:T(8,128)} %get-tuple-element.69), channel_id=1, source_target_pairs={{8,0},{9,1},{10,2},{11,3},{12,4},{13,5},{14,6},{15,7},{24,16},{25,... | collective-permute-start | bytes 393224 | tf_op jit(solution)/shard_map/ppermute | solution.py:800
  534.0 86.5 %collective-permute-start.34 = (bf16[1,8,64,704]{3,2,1,0:T(8,128)(2,1)}, bf16[1,8,64,704]{3,2,1,0:T(8,128)(2,1)}, u32[]{:S(2)}, u32[]{:S(2)}) collective-permute-start(bf16[1,8,64,704]{3,2,1,0:T(8,128)(2,1)} %shard_map.242), channel_id=1, source_target_pairs={{0,8},{1,9},{2,10},{3,11},{4,12},{5,13},{6,14},{7,15},{8,0},{9,1},... | collective-permute-start | bytes 2162696 | tf_op jit(solution)/shard_map/ppermute | solution.py:45
  537.8 73.8 %collective-permute-start.31 = (bf16[2,1,1,128,1024]{4,3,2,1,0:T(8,128)(2,1)S(1)}, bf16[2,1,1,128,1024]{4,3,2,1,0:T(8,128)(2,1)}, u32[]{:S(2)}, u32[]{:S(2)}) collective-permute-start(bf16[2,1,1,128,1024]{4,3,2,1,0:T(8,128)(2,1)S(1)} %dynamic-slice_convert_fusion.9), channel_id=1, source_target_pairs={{0,1},{1,0},{2,3},{3,2},{4,5},{5,4},{6,7},{7,6},{8,9},{9,8},{10,11... | collective-permute-start | bytes 1572872 | tf_op jit(solution)/shard_map/ppermute | solution.py:45
  566.1 49.5 %collective-permute-start.28 = (bf16[1,2,1,128,1024]{4,3,2,1,0:T(8,128)(2,1)S(1)}, bf16[1,2,1,128,1024]{4,3,2,1,0:T(8,128)(2,1)}, u32[]{:S(2)}, u32[]{:S(2)}) collective-permute-start(bf16[1,2,1,128,1024]{4,3,2,1,0:T(8,128)(2,1)S(1)} %dynamic-slice_convert_fusion.10), channel_id=1, source_target_pairs={{0,4},{1,5},{2,6},{3,7},{4,0},{5,1},{6,2},{7,3},{8,12},{9,13},{10,... | collective-permute-start | bytes 1572872 | tf_op jit(solution)/shard_map/ppermute | solution.py:45
  600.3 30.8 %collective-permute-start.35 = (bf16[8,768]{1,0:T(8,128)(2,1)S(1)}, bf16[8,768]{1,0:T(8,128)(2,1)S(1)}, u32[]{:S(2)}, u32[]{:S(2)}) collective-permute-start(bf16[8,768]{1,0:T(8,128)(2,1)S(1)} %convert_element_type.475), channel_id=1, source_target_pairs={{8,0},{9,1},{10,2},{11,3},{12,4},{13,5},{14,6},{15,7},{24,16},{25,... | collective-permute-start | bytes 36872 | tf_op jit(solution)/shard_map/ppermute | solution.py:811
  601.6 48.2 %collective-permute-start.44 = (bf16[1,1,176,2048]{3,2,1,0:T(8,128)(2,1)}, bf16[1,1,176,2048]{3,2,1,0:T(8,128)(2,1)}, u32[]{:S(2)}, u32[]{:S(2)}) collective-permute-start(bf16[1,1,176,2048]{3,2,1,0:T(8,128)(2,1)} %shard_map.244), channel_id=1, source_target_pairs={{0,8},{1,9},{2,10},{3,11},{4,12},{5,13},{6,14},{7,15},{8,0},{9,1},... | collective-permute-start | bytes 2162696 | tf_op jit(solution)/shard_map/ppermute | solution.py:45
  607.0 115.1 %all-to-all-start.8 = ((f32[32,1,768]{2,1,0:T(1,128)}), f32[32,1,768]{2,1,0:T(1,128)S(1)}, u32[]{:S(2)}, u32[]{:S(2)}) async-start(f32[32,1,768]{2,1,0:T(1,128)} %all_to_all.48), calls=%async_computation.8 | async-start | bytes 196608 | tf_op jit(solution)/shard_map/all_to_all | solution.py:130
  613.8 43.3 %collective-permute-start.32 = (bf16[1,1,1,128,1024]{4,3,2,1,0:T(8,128)(2,1)}, bf16[1,1,1,128,1024]{4,3,2,1,0:T(8,128)(2,1)S(1)}, u32[]{:S(2)}, u32[]{:S(2)}) collective-permute-start(bf16[1,1,1,128,1024]{4,3,2,1,0:T(8,128)(2,1)} %dynamic-slice_convert_fusion.14), channel_id=1, source_target_pairs={{0,4},{1,5},{2,6},{3,7},{4,0},{5,1},{6,2},{7,3},{8,12},{9,13},{10,... | collective-permute-start | bytes 786440 | tf_op jit(solution)/shard_map/ppermute | solution.py:45
  619.0 41.4 %collective-permute-start.29 = (bf16[1,1,1,128,1024]{4,3,2,1,0:T(8,128)(2,1)}, bf16[1,1,1,128,1024]{4,3,2,1,0:T(8,128)(2,1)}, u32[]{:S(2)}, u32[]{:S(2)}) collective-permute-start(bf16[1,1,1,128,1024]{4,3,2,1,0:T(8,128)(2,1)} %dynamic-slice_convert_fusion.15), channel_id=1, source_target_pairs={{0,2},{1,3},{2,0},{3,1},{4,6},{5,7},{6,4},{7,5},{8,10},{9,11},{10,... | collective-permute-start | bytes 786440 | tf_op jit(solution)/shard_map/ppermute | solution.py:45
  639.5 25.0 %collective-permute-start.39 = (bf16[2,1,2,128,1024]{4,3,2,1,0:T(8,128)(2,1)}, bf16[2,1,2,128,1024]{4,3,2,1,0:T(8,128)(2,1)}, u32[]{:S(2)}, u32[]{:S(2)}) collective-permute-start(bf16[2,1,2,128,1024]{4,3,2,1,0:T(8,128)(2,1)} %dynamic-slice_convert_fusion.1), channel_id=1, source_target_pairs={{0,2},{1,3},{2,0},{3,1},{4,6},{5,7},{6,4},{7,5},{8,10},{9,11},{10,... | collective-permute-start | bytes 3145736 | tf_op jit(solution)/shard_map/ppermute | solution.py:45
  646.6 26.4 %collective-permute-start.36 = (bf16[2,2,1,128,1024]{4,3,2,1,0:T(8,128)(2,1)}, bf16[2,2,1,128,1024]{4,3,2,1,0:T(8,128)(2,1)}, u32[]{:S(2)}, u32[]{:S(2)}) collective-permute-start(bf16[2,2,1,128,1024]{4,3,2,1,0:T(8,128)(2,1)} %dynamic-slice_convert_fusion.2), channel_id=1, source_target_pairs={{0,1},{1,0},{2,3},{3,2},{4,5},{5,4},{6,7},{7,6},{8,9},{9,8},{10,11... | collective-permute-start | bytes 3145736 | tf_op jit(solution)/shard_map/ppermute | solution.py:45
  649.7 76.3 %collective-permute-start.42 = (bf16[1,2,8,64,1152]{4,3,2,1,0:T(8,128)(2,1)}, bf16[1,2,8,64,1152]{4,3,2,1,0:T(8,128)(2,1)}, u32[]{:S(2)}, u32[]{:S(2)}) collective-permute-start(bf16[1,2,8,64,1152]{4,3,2,1,0:T(8,128)(2,1)} %bitcast.124), channel_id=1, source_target_pairs={{0,16},{16,0},{1,17},{17,1},{2,18},{18,2},{3,19},{19,3},{4,20},{20... | collective-permute-start | bytes 7077896 | tf_op jit(solution)/shard_map/ppermute | solution.py:45
  657.1 37.8 %collective-permute-start.43 = (bf16[1,8,64,704]{3,2,1,0:T(8,128)(2,1)S(1)}, bf16[1,8,64,704]{3,2,1,0:T(8,128)(2,1)S(1)}, u32[]{:S(2)}, u32[]{:S(2)}) collective-permute-start(bf16[1,8,64,704]{3,2,1,0:T(8,128)(2,1)S(1)} %copy-done.41), channel_id=1, source_target_pairs={{0,8},{1,9},{2,10},{3,11},{4,12},{5,13},{6,14},{7,15},{8,0},{9,1},... | collective-permute-start | bytes 2162696 | tf_op jit(solution)/shard_map/ppermute | solution.py:45
  666.1 31.9 %collective-permute-start.40 = (bf16[2,1,1,128,1024]{4,3,2,1,0:T(8,128)(2,1)S(1)}, bf16[2,1,1,128,1024]{4,3,2,1,0:T(8,128)(2,1)S(1)}, u32[]{:S(2)}, u32[]{:S(2)}) collective-permute-start(bf16[2,1,1,128,1024]{4,3,2,1,0:T(8,128)(2,1)S(1)} %dynamic-slice_convert_fusion.7), channel_id=1, source_target_pairs={{0,1},{1,0},{2,3},{3,2},{4,5},{5,4},{6,7},{7,6},{8,9},{9,8},{10,11... | collective-permute-start | bytes 1572872 | tf_op jit(solution)/shard_map/ppermute | solution.py:45
  674.8 29.6 %collective-permute-start.37 = (bf16[1,2,1,128,1024]{4,3,2,1,0:T(8,128)(2,1)S(1)}, bf16[1,2,1,128,1024]{4,3,2,1,0:T(8,128)(2,1)S(1)}, u32[]{:S(2)}, u32[]{:S(2)}) collective-permute-start(bf16[1,2,1,128,1024]{4,3,2,1,0:T(8,128)(2,1)S(1)} %dynamic-slice_convert_fusion.8), channel_id=1, source_target_pairs={{0,4},{1,5},{2,6},{3,7},{4,0},{5,1},{6,2},{7,3},{8,12},{9,13},{10,... | collective-permute-start | bytes 1572872 | tf_op jit(solution)/shard_map/ppermute | solution.py:45
  698.2 10.0 %collective-permute-start.41 = (bf16[1,1,1,128,1024]{4,3,2,1,0:T(8,128)(2,1)S(1)}, bf16[1,1,1,128,1024]{4,3,2,1,0:T(8,128)(2,1)S(1)}, u32[]{:S(2)}, u32[]{:S(2)}) collective-permute-start(bf16[1,1,1,128,1024]{4,3,2,1,0:T(8,128)(2,1)S(1)} %dynamic-slice_convert_fusion.12), channel_id=1, source_target_pairs={{0,4},{1,5},{2,6},{3,7},{4,0},{5,1},{6,2},{7,3},{8,12},{9,13},{10,... | collective-permute-start | bytes 786440 | tf_op jit(solution)/shard_map/ppermute | solution.py:45
  704.5 6.4 collective-permute-start.38
  722.1 62.0 %all-to-all-start.7 = ((bf16[8,64,1408]{2,1,0:T(8,128)(2,1)}), bf16[8,64,1408]{2,1,0:T(8,128)(2,1)S(1)}, u32[]{:S(2)}, u32[]{:S(2)}) async-start(bf16[8,64,1408]{2,1,0:T(8,128)(2,1)} %shard_map.246), calls=%async_computation.7 | async-start | bytes 2883584 | tf_op jit(solution)/shard_map/all_to_all | solution.py:120
  733.0 49.8 %collective-permute-start.45 = (bf16[1,8,64,1152]{3,2,1,0:T(8,128)(2,1)}, bf16[1,8,64,1152]{3,2,1,0:T(8,128)(2,1)S(1)}, u32[]{:S(2)}, u32[]{:S(2)}) collective-permute-start(bf16[1,8,64,1152]{3,2,1,0:T(8,128)(2,1)} %shard_map.245), channel_id=1, source_target_pairs={{0,8},{1,9},{2,10},{3,11},{4,12},{5,13},{6,14},{7,15},{8,0},{9,1},... | collective-permute-start | bytes 3538952 | tf_op jit(solution)/shard_map/ppermute | solution.py:45
  734.6 48.2 %copy-start.11 = (f32[1,2,8,64,1152]{4,3,2,1,0:T(8,128)S(1)}, f32[1,2,8,64,1152]{4,3,2,1,0:T(8,128)}, u32[]{:S(2)}) copy-start(f32[1,2,8,64,1152]{4,3,2,1,0:T(8,128)} %copy-done.10) | copy-start | bytes 14155780
  740.4 72.4 %collective-permute-start.46 = (bf16[1,2,64,2048]{3,2,1,0:T(8,128)(2,1)}, bf16[1,2,64,2048]{3,2,1,0:T(8,128)(2,1)}, u32[]{:S(2)}, u32[]{:S(2)}) collective-permute-start(bf16[1,2,64,2048]{3,2,1,0:T(8,128)(2,1)} %dynamic-slice_convert_fusion.6), channel_id=1, source_target_pairs={{0,16},{16,0},{1,17},{17,1},{2,18},{18,2},{3,19},{19,3},{4,20},{20... | collective-permute-start | bytes 1572872 | tf_op jit(solution)/shard_map/ppermute | solution.py:45
  785.2 41.6 %all-to-all-start.9 = ((bf16[8,64,1152]{2,1,0:T(8,128)(2,1)}), bf16[8,64,1152]{2,1,0:T(8,128)(2,1)}, u32[]{:S(2)}, u32[]{:S(2)}) async-start(bf16[8,64,1152]{2,1,0:T(8,128)(2,1)} %shard_map.247), calls=%async_computation.9 | async-start | bytes 2359296 | tf_op jit(solution)/shard_map/all_to_all | solution.py:120
  814.9 11.0 %collective-permute-start.47 = (bf16[1,1,64,2048]{3,2,1,0:T(8,128)(2,1)S(1)}, bf16[1,1,64,2048]{3,2,1,0:T(8,128)(2,1)S(1)}, u32[]{:S(2)}, u32[]{:S(2)}) collective-permute-start(bf16[1,1,64,2048]{3,2,1,0:T(8,128)(2,1)S(1)} %dynamic-slice_convert_fusion.11), channel_id=1, source_target_pairs={{0,8},{1,9},{2,10},{3,11},{4,12},{5,13},{6,14},{7,15},{8,0},{9,1},... | collective-permute-start | bytes 786440 | tf_op jit(solution)/shard_map/ppermute | solution.py:45
  825.9 10.5 %collective-permute-start.48 = (bf16[64,2048]{1,0:T(8,128)(2,1)S(1)}, bf16[64,2048]{1,0:T(8,128)(2,1)S(1)}, u32[]{:S(2)}, u32[]{:S(2)}) collective-permute-start(bf16[64,2048]{1,0:T(8,128)(2,1)S(1)} %fusion.38), channel_id=1, source_target_pairs={{0,0},{1,4},{2,8},{3,12},{4,16},{5,20},{6,24},{7,28},{8,1},{9,5},{... | collective-permute-start | bytes 786440 | tf_op jit(solution)/shard_map/ppermute | solution.py:822
  (108 other events, 717.5 us)
Sparse Core Ops, SparseCore 0:
  476.8 128.7 all-gather.1

commit v2 on v1

--- a/solution.py
+++ b/solution.py
@@ -54,12 +54,13 @@
     return both.reshape(values.shape[:dim] + (2 * values.shape[dim],) + values.shape[dim + 1 :])
 
 
-def halve(values, axis, bit, dim, waited=()):
+def halve(values, axis, bit, dim, waited=(), later=()):
     upper = ((lax.axis_index(axis) & bit) != 0).astype(jnp.int32)
     kept = lax.dynamic_index_in_dim(values, upper, dim, True)
     sent = lax.dynamic_index_in_dim(values, 1 - upper, dim, True)
     sent = sent.astype(LOW)
-    return kept.astype(FULL) + swap(tie(sent, *waited) if waited else sent, axis, bit).astype(FULL)
+    come = swap(tie(sent, *waited) if waited else sent, axis, bit)
+    return kept.astype(FULL) + (tie(come, *later) if later else come).astype(FULL)
 
 
 def tie(values, *others):
@@ -185,7 +186,7 @@
     return jnp.sum(cube_turn(blocks, width).astype(FULL), axis=0)
 
 
-def cube_sum_by_axes(left, right, dot, width):
+def cube_sum_by_axes(left, right, dot, width, middle=(), last=()):
     rows = left.shape[0]
     orders = cube_orders(width, 2)
     depth = len(orders[0])
@@ -194,8 +195,9 @@
         block = dot(left, part)
         columns = block.shape[1]
         block = block.reshape([2] * depth + [rows // width, columns])
-        for place in reversed(order):
-            block = halve(block, "seq", 1 << place, depth - 1 - place)
+        for step, place in enumerate(reversed(order)):
+            waited = () if step == 0 else last if step == depth - 1 else middle
+            block = halve(block, "seq", 1 << place, depth - 1 - place, waited)
         done.append(block.reshape(rows // width, columns))
     return jnp.concatenate(done, 1)
 
@@ -220,10 +222,10 @@
     return values
 
 
-def far_sum(values, width, waited=()):
+def far_sum(values, width, waited=(), later=()):
     rest = values.shape[1:]
     for bit in reversed(bits_of(lax.axis_size("seq") // width)):
-        values = halve(values.reshape((2, -1) + rest), "seq", bit * width, 0, waited)[0]
+        values = halve(values.reshape((2, -1) + rest), "seq", bit * width, 0, waited, later)[0]
     return values.reshape(rest)
 
 
@@ -766,7 +768,6 @@
     grad_normed_two, grad_ffn, grad_down = lax.optimization_barrier(
         (grad_normed_two, grad_ffn, grad_down)
     )
-    grad_ffn = [grad_ffn[..., :hidden_mine], grad_ffn[..., hidden_mine:]]
     (grad_middle,) = ffn_pull(grad_normed_two)
     grad_middle = grad_middle + cotangent[0].astype(FULL)
     grad_branch = grad_middle.astype(LOW)
@@ -783,11 +784,10 @@
             block = (chip % width) * fiber + row * cubes + chip // width
             owners.append((row * seq + chip, block))
     groups = [list(range(first, first + width)) for first in range(0, seq, width)]
-    branch_cube = lax.all_gather(grad_branch, "seq", axis_index_groups=groups, tiled=True)
+    branch_cube = cube_turn(jnp.broadcast_to(tie(grad_branch, grad_scaled)[None], (width, tokens, D)), width)
+    branch_cube = branch_cube.reshape(count, D)
     half = D // len(cube_orders(width, 2))
     down_parts = [down_w[:, at : at + half] for at in range(0, D, half)]
-    result = middle + cube_sum_by_axes(tie(hidden, grad_branch), down_parts, dot_low, width)
-    block_output = result.astype(LOW)[None]
     backs = delta_back(
         heads, mixed_in, cols, gain_row, prepared, recalled, grad_scaled, ()
     )
@@ -798,14 +798,14 @@
         if hop > 0:
             out = end_back + jnp.einsum("hji,hjk->hik", far, leaving, precision=HIGH)
         leaving = lax.ppermute(out, "seq", behind)
-    grad_down = far_sum(grad_down, width, (leaving,))
-    grad_hgate = near_sum(grad_ffn[0], "seq", width, cubes, (leaving,))
+    grad_ffn = near_sum(grad_ffn, "seq", width, cubes, (leaving,)).astype(LOW)
     grad_mixed, tail, edge, grad_taps = delta_pull(
         heads, mixed_in, taps_mine, cols, segs, prepared, states, delta, backs[:4], leaving,
         (),
     )
-    grad_hup = near_sum(grad_ffn[1], "seq", width, cubes, (grad_hgate, leaving))
-    grad_mixed = hint(grad_mixed, grad_hgate)
+    result = middle + cube_sum_by_axes(tie(hidden, edge), down_parts, dot_low, width)
+    block_output = result.astype(LOW)[None]
+    grad_mixed = tie(grad_mixed, branch_cube)
     grad_mixer = dot_left_t(normed, grad_mixed).reshape(dp, cubes, width, rows, -1)
     grad_mixer = near_sum(grad_mixer, "dp", 1, dp)
     from_next = lax.ppermute(edge.astype(LOW), "seq", behind).astype(FULL)
@@ -813,21 +813,22 @@
         grad_mixed[RIM:], (tail + from_next).astype(LOW), (count - SPAN, 0)
     )
     grad_taps = grad_taps[:CONV]
+    grad_fixed = tie(grad_fixed, grad_mixer)
     mixer_parts = [mixer_w[at : at + half] for at in range(0, D, half)]
-    grad_mixer = near_sum(grad_mixer, "seq", width, cubes, (grad_hup, grad_down)).astype(LOW)
+    grad_oproj = chip_sum(dot_left_t(scaled, branch_cube).reshape(fiber, rows, D))
+    grad_oproj = far_sum(grad_oproj, width, (grad_ffn,))
+    grad_mixer = near_sum(grad_mixer, "seq", width, cubes, (grad_ffn, grad_oproj)).astype(LOW)
+    mixer_far_sum = grad_mixer
     grad_normed = cube_sum_by_axes(grad_fixed, mixer_parts, dot_right_t, width)
     grad_normed = fiber_order(grad_normed, width)
-    grad_oproj = chip_sum(dot_left_t(scaled, branch_cube).reshape(fiber, rows, D))
-    grad_oproj = far_sum(grad_oproj, width)
     grad_oproj = lax.ppermute(grad_oproj.astype(LOW), both, owners).astype(FULL)
-    grad_ffn = jnp.concatenate([grad_hgate.astype(LOW), grad_hup.astype(LOW)], -1)
-    grad_ffn = cube_turn(tie(grad_ffn, block_output), width)
+    grad_ffn = cube_turn(tie(grad_ffn, grad_normed), width)
     taps_wide = lax.dynamic_update_index_in_dim(
         jnp.zeros((CONV, 3, width, mine), FULL), grad_taps.reshape(CONV, 3, mine), me, 2
     ).reshape(CONV, everyone, taps_each)
     taps_wide = jnp.swapaxes(taps_wide, 0, 1).reshape(everyone, CONV * taps_each)
     taps_own = sum_all(taps_wide)
-    grad_mixer = cube_turn(tie(grad_mixer, grad_ffn, taps_own), width).astype(FULL)
+    grad_mixer = cube_turn(tie(grad_mixer, grad_ffn, taps_own, block_output), width).astype(FULL)
     grad_ffn = grad_ffn.astype(FULL)
 
     def by_rows(grad):
@@ -840,6 +841,7 @@
     grad_wproj = grad_wproj.reshape(rows, 3 * D)
     grad_wgate = grad_mixer[..., 3 * mine : 4 * mine].reshape(rows, D)
     grad_wbeta = grad_mixer[..., 4 * mine : 4 * mine + heads].reshape(rows, H)
+    grad_down = far_sum(grad_down, width, (mixer_far_sum,), (grad_hgate, grad_hup))
     (grad_tokens,) = mix_pull(grad_normed)
     grad_input = (grad_tokens + grad_middle)[None]
 

time: 861 us -> 837 us (0.972)
  waiting for transfers between devices: 268 us -> 221 us
  starting transfers between devices: 107 us -> 147 us
  other arithmetic: 132 us -> 114 us
  blocking collectives: 0 us -> 15.3 us
  between operations: 16.6 us -> 3.23 us
    ppermute x44 -> x43, waiting for transfers between devices: 241 us -> 194 us  [swap(): lax.ppermute(values, axis, [(i, i ^ bit) for i in range(lax.axis_size(axi...]
    all_to_all x1, starting transfers between devices: 4.5 us -> 34.6 us  [sum_all(): lax.all_to_all(values, ('dp', 'seq'), 0, 0, tiled=True)]
    all_to_all x0 -> x1, blocking collectives: none -> 15.3 us  [cube_turn(): lax.all_to_all(values, 'seq', 0, 0, axis_index_groups=groups, tiled=True)]
    slice x2 -> x3, local copies, waits for them, and re-layouts: 10.6 us -> 0.31 us  [near_sum(): values = values[:bit].astype(FULL) + sent.astype(FULL)]
    ppermute x44 -> x43, starting transfers between devices: 51.9 us -> 58.3 us  [swap(): lax.ppermute(values, axis, [(i, i ^ bit) for i in range(lax.axis_size(axi...]
    unnamed x234 -> x245, local copies, waits for them, and re-layouts: 27.5 us -> 30.8 us
  transfers between devices with their start and end apart: 60 -> 58, of which waited for: 23 -> 26; matrix products, arithmetic and copies ran while one was open for 34% -> 32% of each run, Pallas kernels for 10% -> 10%
where the time goes in v2:
time: 837 us; the launch traced here: 829 us
  waiting for transfers between devices  221 us (26%)
  local copies, waits for them, and re-layouts  154 us (18%)
  starting transfers between devices  147 us (18%)
  other arithmetic  114 us (14%)
  matrix products  90.5 us (11%)
  Pallas kernels  84 us (10%)
  blocking collectives  15.3 us (2%)
    ppermute x43, waiting for transfers between devices, swap(): lax.ppermute(values, axis, [(i, i ^ bit) for i in range(lax.axis_size(axi...  194 us
    pallas_call x4, Pallas kernels, on_chip(): pl.pallas_call(lambda *refs: body(*refs[:used], *refs[used + spare:]), ou...  84 us
    ppermute x43, starting transfers between devices, swap(): lax.ppermute(values, axis, [(i, i ^ bit) for i in range(lax.axis_size(axi...  58.3 us
    all_to_all x8, starting transfers between devices, cube_turn(): lax.all_to_all(values, 'seq', 0, 0, axis_index_groups=groups, tiled=True)  37.8 us
    all_to_all x1, starting transfers between devices, sum_all(): lax.all_to_all(values, ('dp', 'seq'), 0, 0, tiled=True)  34.6 us
    dot_general x6, matrix products, dot_right_t(): lax.dot_general(left, right, (((1,), (1,)), ((), ())), preferred_element_...  34.2 us
    unnamed x245, local copies, waits for them, and re-layouts  30.8 us
    dot_general x4, matrix products, dot_left_t(): lax.dot_general(left, right, (((0,), (0,)), ((), ())), preferred_element_...  30.6 us
  transfers between devices with their start and end apart: 58, of which 26 were waited for; matrix products, arithmetic and copies ran while one was open for 32% of the time, Pallas kernels for 10%

profile of v2, /device:TPU:0, one launch (start us, length us, event | category | flops | bytes accessed | tf_op | source)
XLA Modules:
  0.0 829.0 jit_solution(5068879473048021609)
XLA Ops:
  13.8 4.9 all-to-all-start
  27.6 4.0 all-to-all-start.1
  46.0 23.5 %collective-permute-done.1 = bf16[1,2,1,2,128,1024]{5,4,1,3,2,0:T(8,128)(2,1)} collective-permute-done((bf16[1,2,1,2,128,1024]{5,4,1,3,2,0:T(8,128)(2,1)}, bf16[1,2,1,2,128,1024]{5,4,1,3,2,0:T(8,128)(2,1)}, u32[]{:S(2)}, u32[]{:S(2)}) %collective-permute-start.1) | collective-permute-done | bytes 1048608 | tf_op jit(solution)/shard_map/ppermute | solution.py:45
  91.9 3.0 copy.273
  94.9 4.5 reshape.605
  105.9 4.9 all-to-all-start.4
  110.8 22.1 %collective-permute-done.7 = bf16[1,8,64,1152]{3,2,1,0:T(8,128)(2,1)} collective-permute-done((bf16[1,8,64,1152]{3,2,1,0:T(8,128)(2,1)S(1)}, bf16[1,8,64,1152]{3,2,1,0:T(8,128)(2,1)}, u32[]{:S(2)}, u32[]{:S(2)}) %collective-permute-start.7) | collective-permute-done | bytes 1179680 | tf_op jit(solution)/shard_map/ppermute | solution.py:45
  148.6 3.8 fusion.4
  153.1 3.1 fusion
  159.1 7.8 fusion.62.refs_0_
  168.2 13.1 %collective-permute-done.10 = bf16[1,64,2048]{2,1,0:T(8,128)(2,1)S(1)} collective-permute-done((bf16[1,64,2048]{2,1,0:T(8,128)(2,1)S(1)}, bf16[1,64,2048]{2,1,0:T(8,128)(2,1)S(1)}, u32[]{:S(2)}, u32[]{:S(2)}) %collective-permute-start.10) | collective-permute-done | bytes 262176 | tf_op jit(solution)/shard_map/ppermute | solution.py:45
  183.9 4.7 all-to-all-start.3
  196.3 29.9 %shard_map.237 = (f32[16,128,128]{2,1,0:T(8,128)}, f32[16,128,128]{2,1,0:T(8,128)}, f32[16,128,128]{2,1,0:T(8,128)}, f32[16,128,128]{2,1,0:T(8,128)}, f32[16,128...) custom-call(f32[1040,1152]{1,0:T(8,128)} %fusion.62.refs_0_, ...), custom_call_target="tpu_custom_call" | custom-call | flops 32212254720 | bytes 20971520 | tf_op jit(solution)/shard_map/pallas_call | solution.py:545
  228.1 37.8 %collective-permute-done.21 = bf16[1,8,64,1408]{3,2,1,0:T(8,128)(2,1)S(1)} collective-permute-done((bf16[1,8,64,1408]{3,2,1,0:T(8,128)(2,1)}, bf16[1,8,64,1408]{3,2,1,0:T(8,128)(2,1)S(1)}, u32[]{:S(2)}, u32[]{:S(2)}) %collective-permute-start.21) | collective-permute-done | bytes 1441824 | tf_op jit(solution)/shard_map/ppermute | solution.py:45
  266.0 3.3 maximum_bitcast_fusion
  269.3 6.4 all-to-all-done.3
  275.7 12.9 %collective-permute-done.23 = bf16[1,176,2048]{2,1,0:T(8,128)(2,1)S(1)} collective-permute-done((bf16[1,176,2048]{2,1,0:T(8,128)(2,1)S(1)}, bf16[1,176,2048]{2,1,0:T(8,128)(2,1)S(1)}, u32[]{:S(2)}, u32[]{:S(2)}) %collective-permute-start.23) | collective-permute-done | bytes 720928 | tf_op jit(solution)/shard_map/ppermute | solution.py:45
  289.7 11.1 %shard_map.238 = (f32[16,128,128]{2,1,0:T(8,128)}, f32[16,128,128]{2,1,0:T(8,128)}, f32[16,128,128]{2,1,0:T(8,128)}, bf16[1024,256]{1,0:T(8,128)(2,1)}) custom-call(f32[1040,1152]{1,0:T(8,128)} %fusion.62.refs_0_, f32[1032,8]{1,0:T(8,128)} %pad.5.refs_2_.refs_1_, f32[1,256]{1,0:T(1,128)} %bitcast.429, f32[16,128,128]{2,1,0:T(8,128)} %get-tuple-element.45.refs_3_.refs_4_, ...), custom_call_target="tpu_custom_call" | custom-call | flops 11811160064 | bytes 20971520 | tf_op jit(solution)/shard_map/pallas_call | solution.py:545
  300.8 7.1 all-to-all-start.2
  310.0 6.4 all-to-all-done.2
  321.1 5.8 pad_maximum_fusion
  329.8 3.0 multiply_reduce_fusion.4
  349.8 9.0 %collective-permute-done.19 = bf16[2,1,1,128,768]{4,3,0,2,1:T(8,128)(2,1)S(1)} collective-permute-done((bf16[2,1,1,128,768]{4,3,0,2,1:T(8,128)(2,1)S(1)}, bf16[2,1,1,128,768]{4,3,0,2,1:T(8,128)(2,1)S(1)}, u32[]{:S(2)}, u32[]{:S(2)}) %collective-permute-start.19) | collective-permute-done | bytes 393248 | tf_op jit(solution)/shard_map/ppermute | solution.py:45
  361.1 8.1 collective-permute-done.17
  372.4 6.7 fusion.16
  379.2 5.7 fusion.11
  384.9 10.7 %convolution_convert_fusion = bf16[1024,2048]{1,0:T(8,128)(2,1)} fusion(bf16[2048,1408]{1,0:T(8,128)(2,1)S(1)} %bitcast.344, bf16[1024,704]{1,0:T(8,128)(2,1)} %get-tuple-element.82, bf16[1024,704]{1,0:T(8,128)(2,1)} %get-tuple-element.81), kind=kOutput, calls=%fused_computation.26 | convolution fusion | flops 5913444352 | bytes 12845056 | tf_op jit(solution)/shard_map/dot_general | solution.py:37
  395.6 4.6 all-to-all-start.5
  400.2 10.7 %fusion.15 = f32[2048,1408]{1,0:T(8,128)S(1)} fusion(bf16[1024,704]{1,0:T(8,128)(2,1)} %get-tuple-element.82, bf16[1024,704]{1,0:T(8,128)(2,1)} %get-tuple-element.81, bf16[1024,768]{1,0:T(8,128)(2,1)} %copy-done.62, bf16[1024,640]{1,0:T(8,128)(2,1)} %copy-done.63, bf16[1024,640]{1,0:T(8,128)(2,1)} %copy-done.64), kind=kOutput, calls=%fused_computation.67 | convolution fusion | flops 5923930112 | bytes 18612224 | tf_op jit(solution)/shard_map/dot_general | solution.py:33
  410.9 4.3 copy-done.6
  419.0 5.8 fusion.5
  429.1 3.1 collective-permute-done.26
  434.1 4.9 add_bitcast_fusion
  439.0 6.9 all-to-all-done.5
  452.5 3.9 convolution_convert_fusion.2
  456.4 3.7 convolution_convert_fusion.1
  461.0 15.3 %all_to_all.64 = bf16[8,128,256]{2,1,0:T(8,128)(2,1)} all-to-all(bf16[8,128,256]{2,1,0:T(8,128)(2,1)S(1)} %bitcast.379), channel_id=1, replica_groups={{0,1,2,3,4,5,6,7},{8,9,10,11,12,13,14,15},{16,17,18,19,20,21,22,23},{24..., dimensions={0} | all-to-all | bytes 1048576 | tf_op jit(solution)/shard_map/all_to_all | solution.py:121
  476.3 3.5 broadcast_in_dim.548
  479.8 4.6 all-to-all-start.7
  484.5 12.6 %shard_map.239 = (f32[16,128,128]{2,1,0:T(8,128)}, f32[16,128,128]{2,1,0:T(8,128)}, f32[16,128,128]{2,1,0:T(8,128)}, bf16[1024,256]{1,0:T(8,128)(2,1)}, f32[2,128,128]{2,1,0:T(8,128)}) custom-call(f32[1040,1152]{1,0:T(8,128)} %fusion.62.refs_0_, f32[1032,8]{1,0:T(8,128)} %pad.5.refs_2_.refs_1_, f32[1,256]{1,0:T(1,128)} %bitcast.430, ...), custom_call_target="tpu_custom_call" | custom-call | flops 12884901888 | bytes 20971520 | tf_op jit(solution)/shard_map/pallas_call | solution.py:545
  500.6 3.3 bitcast_select_fusion
  503.9 3.1 slice.282.refs_0_
  507.0 30.4 %shard_map.240 = (bf16[1040,1152]{1,0:T(8,128)(2,1)}, f32[8,768]{1,0:T(8,128)}, f32[8,768]{1,0:T(8,128)}, f32[8,768]{1,0:T(8,128)}) custom-call(f32[1040,1152]{1,0:T(8,128)} %fusion.62.refs_0_, f32[4,768]{1,0:T(4,128)} %bitcast.426, f32[1032,8]{1,0:T(8,128)} %pad.5.refs_2_.refs_1_, f32[8,1,128]{2,1,0:T(1,128)} %bitcast.419, ...), custom_call_target="tpu_custom_call" | custom-call | flops 32212254720 | bytes 20971520 | tf_op jit(solution)/shard_map/pallas_call | solution.py:545
  540.4 3.6 fusion.18
  554.5 4.8 collective-permute-start.42
  567.8 34.6 %all-to-all-start.9 = ((f32[32,1,768]{2,1,0:T(1,128)}), f32[32,1,768]{2,1,0:T(1,128)}, u32[]{:S(2)}, u32[]{:S(2)}) async-start(f32[32,1,768]{2,1,0:T(1,128)} %all_to_all.52), calls=%async_computation.9 | async-start | bytes 196608 | tf_op jit(solution)/shard_map/all_to_all | solution.py:131
  603.2 10.2 %fusion.60 = f32[2048,1152]{1,0:T(8,128)S(1)} fusion(bf16[1040,1152]{1,0:T(8,128)(2,1)} %shard_map.243, f32[2048]{0:T(1024)S(1)} %bitcast.428, f32[1040]{0:T(1024)} %copy-done.89, bf16[1024,2048]{1,0:T(8,128)(2,1)} %fusion.4, bf16[16,2048]{1,0:T(8,128)(2,1)} %copy-done.70), kind=kOutput, calls=%fused_computation.238 | convolution fusion | flops 4922245120 | bytes 16105536 | tf_op jit(solution)/shard_map/dot_general | solution.py:33
  624.4 6.1 collective-permute-done.32
  630.8 3.9 fusion.73
  643.1 5.4 fusion.72
  651.6 4.7 fusion.71
  664.9 10.5 %collective-permute-done.39 = bf16[2,1,2,128,1024]{4,3,2,1,0:T(8,128)(2,1)} collective-permute-done((bf16[2,1,2,128,1024]{4,3,2,1,0:T(8,128)(2,1)}, bf16[2,1,2,128,1024]{4,3,2,1,0:T(8,128)(2,1)}, u32[]{:S(2)}, u32[]{:S(2)}) %collective-permute-start.39) | collective-permute-done | bytes 1048608 | tf_op jit(solution)/shard_map/ppermute | solution.py:45
  679.4 4.6 collective-permute-done.36
  688.7 5.3 collective-permute-done.40
  717.4 3.6 all-to-all-start.8
  728.5 10.7 %collective-permute-done.33 = bf16[1,1,1,128,1024]{4,3,2,1,0:T(8,128)(2,1)} collective-permute-done((bf16[1,1,1,128,1024]{4,3,2,1,0:T(8,128)(2,1)}, bf16[1,1,1,128,1024]{4,3,2,1,0:T(8,128)(2,1)}, u32[]{:S(2)}, u32[]{:S(2)}) %collective-permute-start.33) | collective-permute-done | bytes 262176 | tf_op jit(solution)/shard_map/ppermute | solution.py:45
  741.6 4.1 collective-permute-start.46
  745.8 16.4 %collective-permute-done.45 = bf16[1,8,64,1152]{3,2,1,0:T(8,128)(2,1)} collective-permute-done((bf16[1,8,64,1152]{3,2,1,0:T(8,128)(2,1)}, bf16[1,8,64,1152]{3,2,1,0:T(8,128)(2,1)}, u32[]{:S(2)}, u32[]{:S(2)}) %collective-permute-start.45) | collective-permute-done | bytes 1179680 | tf_op jit(solution)/shard_map/ppermute | solution.py:45
  768.7 7.5 all-to-all-done.8.refs_1_
  777.3 4.4 all-to-all-start.10
  790.6 4.7 reshape.624
  797.8 3.3 reshape.625.refs_2_
  801.1 4.7 reshape.622
  808.4 3.4 reshape.623.refs_1_
  (586 shorter events, 285.5 us)
Async XLA Ops:
  8.1 32.2 %copy-start.32 = (bf16[2,128,1024]{2,1,0:T(8,128)(2,1)}, bf16[2,128,1024]{2,1,0:T(8,128)(2,1)S(1)}, u32[]{:S(2)}) copy-start(bf16[2,128,1024]{2,1,0:T(8,128)(2,1)S(1)} %get-tuple-element.90) | copy-start | bytes 1572868
  8.1 23.4 %collective-permute-start = (bf16[1,1,1,2,128,1024]{5,4,3,2,1,0:T(8,128)(2,1)}, bf16[1,1,1,2,128,1024]{5,4,3,2,1,0:T(8,128)(2,1)}, u32[]{:S(2)}, u32[]{:S(2)}) collective-permute-start(bf16[1,1,1,2,128,1024]{5,4,3,2,1,0:T(8,128)(2,1)} %get-tuple-element.91), channel_id=1, source_target_pairs={{0,2},{1,3},{2,0},{3,1},{4,6},{5,7},{6,4},{7,5},{8,10},{9,11},{10,... | collective-permute-start | bytes 1572872 | tf_op jit(solution)/shard_map/ppermute | solution.py:45
  13.8 13.1 %all-to-all-start = ((bf16[32,2,544]{2,1,0:T(2,128)(2,1)}), bf16[32,2,544]{2,1,0:T(2,128)(2,1)S(1)}, u32[]{:S(2)}, u32[]{:S(2)}) async-start(bf16[32,2,544]{2,1,0:T(2,128)(2,1)} %reshape.649), calls=%async_computation | async-start | bytes 163840 | tf_op jit(solution)/shard_map/all_to_all | solution.py:127
  18.7 21.7 %collective-permute-start.3 = (bf16[1,1,1,2,128,1024]{5,4,3,2,1,0:T(8,128)(2,1)}, bf16[1,1,1,2,128,1024]{5,4,3,2,1,0:T(8,128)(2,1)}, u32[]{:S(2)}, u32[]{:S(2)}) collective-permute-start(bf16[1,1,1,2,128,1024]{5,4,3,2,1,0:T(8,128)(2,1)} %get-tuple-element.92), channel_id=1, source_target_pairs={{0,4},{1,5},{2,6},{3,7},{4,0},{5,1},{6,2},{7,3},{8,12},{9,13},{10,... | collective-permute-start | bytes 1572872 | tf_op jit(solution)/shard_map/ppermute | solution.py:45
  26.9 49.0 %copy-start.80 = (pred[2]{0:T(512)(128)(4,1)}, pred[2]{0:T(512)(128)(4,1)S(1)}, u32[]{:S(2)}) copy-start(pred[2]{0:T(512)(128)(4,1)S(1)} %iota_compare_fusion.2) | copy-start | bytes 10
  27.6 52.7 %all-to-all-start.1 = ((bf16[8,64,1152]{2,1,0:T(8,128)(2,1)}), bf16[8,64,1152]{2,1,0:T(8,128)(2,1)S(1)}, u32[]{:S(2)}, u32[]{:S(2)}) async-start(bf16[8,64,1152]{2,1,0:T(8,128)(2,1)} %copy.202), calls=%async_computation.1 | async-start | bytes 2359296 | tf_op jit(solution)/shard_map/all_to_all | solution.py:121
  33.8 35.7 %collective-permute-start.1 = (bf16[1,2,1,2,128,1024]{5,4,1,3,2,0:T(8,128)(2,1)}, bf16[1,2,1,2,128,1024]{5,4,1,3,2,0:T(8,128)(2,1)}, u32[]{:S(2)}, u32[]{:S(2)}) collective-permute-start(bf16[1,2,1,2,128,1024]{5,4,1,3,2,0:T(8,128)(2,1)} %broadcast_select_fusion.10), channel_id=1, source_target_pairs={{0,4},{1,5},{2,6},{3,7},{4,0},{5,1},{6,2},{7,3},{8,12},{9,13},{10,... | collective-permute-start | bytes 3145736 | tf_op jit(solution)/shard_map/ppermute | solution.py:45
  38.9 47.0 %copy-start.82 = (pred[2]{0:T(512)(128)(4,1)}, pred[2]{0:T(512)(128)(4,1)S(1)}, u32[]{:S(2)}) copy-start(pred[2]{0:T(512)(128)(4,1)S(1)} %iota_compare_fusion.4) | copy-start | bytes 10
  40.1 42.9 %copy-start.74 = (pred[2]{0:T(512)(128)(4,1)}, pred[2]{0:T(512)(128)(4,1)S(1)}, u32[]{:S(2)}) copy-start(pred[2]{0:T(512)(128)(4,1)S(1)} %iota_compare_fusion.3) | copy-start | bytes 10
  40.3 32.0 %copy-start.66 = (bf16[32,1,1088]{2,0,1:T(8,128)(2,1)}, bf16[32,1,1088]{2,0,1:T(8,128)(2,1)S(1)}, u32[]{:S(2)}) copy-start(bf16[32,1,1088]{2,0,1:T(8,128)(2,1)S(1)} %copy.276) | copy-start | bytes 208900
  42.5 33.4 %collective-permute-start.4 = (bf16[2,1,1,2,128,1024]{5,4,0,3,2,1:T(8,128)(2,1)}, bf16[2,1,1,2,128,1024]{5,4,0,3,2,1:T(8,128)(2,1)}, u32[]{:S(2)}, u32[]{:S(2)}) collective-permute-start(bf16[2,1,1,2,128,1024]{5,4,0,3,2,1:T(8,128)(2,1)} %broadcast_select_fusion.8), channel_id=1, source_target_pairs={{0,1},{1,0},{2,3},{3,2},{4,5},{5,4},{6,7},{7,6},{8,9},{9,8},{10,11... | collective-permute-start | bytes 3145736 | tf_op jit(solution)/shard_map/ppermute | solution.py:45
  72.3 63.6 %collective-permute-start.2 = (bf16[2,2,1,2,128,1024]{5,4,1,0,3,2:T(8,128)(2,1)}, bf16[2,2,1,2,128,1024]{5,4,1,0,3,2:T(8,128)(2,1)}, u32[]{:S(2)}, u32[]{:S(2)}) collective-permute-start(bf16[2,2,1,2,128,1024]{5,4,1,0,3,2:T(8,128)(2,1)} %broadcast_select_fusion.5), channel_id=1, source_target_pairs={{0,1},{1,0},{2,3},{3,2},{4,5},{5,4},{6,7},{7,6},{8,9},{9,8},{10,11... | collective-permute-start | bytes 6291464 | tf_op jit(solution)/shard_map/ppermute | solution.py:45
  78.8 60.4 %collective-permute-start.5 = (bf16[2,1,2,2,128,1024]{5,4,2,0,3,1:T(8,128)(2,1)}, bf16[2,1,2,2,128,1024]{5,4,2,0,3,1:T(8,128)(2,1)}, u32[]{:S(2)}, u32[]{:S(2)}) collective-permute-start(bf16[2,1,2,2,128,1024]{5,4,2,0,3,1:T(8,128)(2,1)} %broadcast_select_fusion.3), channel_id=1, source_target_pairs={{0,2},{1,3},{2,0},{3,1},{4,6},{5,7},{6,4},{7,5},{8,10},{9,11},{10,... | collective-permute-start | bytes 6291464 | tf_op jit(solution)/shard_map/ppermute | solution.py:45
  80.3 52.6 %collective-permute-start.7 = (bf16[1,8,64,1152]{3,2,1,0:T(8,128)(2,1)S(1)}, bf16[1,8,64,1152]{3,2,1,0:T(8,128)(2,1)}, u32[]{:S(2)}, u32[]{:S(2)}) collective-permute-start(bf16[1,8,64,1152]{3,2,1,0:T(8,128)(2,1)S(1)} %bitcast.345), channel_id=1, source_target_pairs={{0,8},{1,9},{2,10},{3,11},{4,12},{5,13},{6,14},{7,15},{8,0},{9,1},... | collective-permute-start | bytes 3538952 | tf_op jit(solution)/shard_map/ppermute | solution.py:45
  105.9 75.4 %all-to-all-start.4 = ((bf16[8,64,1408]{2,1,0:T(8,128)(2,1)}), bf16[8,64,1408]{2,1,0:T(8,128)(2,1)}, u32[]{:S(2)}, u32[]{:S(2)}) async-start(bf16[8,64,1408]{2,1,0:T(8,128)(2,1)} %pad_maximum_fusion.11), calls=%async_computation.4 | async-start | bytes 2883584 | tf_op jit(solution)/shard_map/all_to_all | solution.py:121
  135.9 20.3 %collective-permute-start.8 = (bf16[1,2,8,64,1152]{4,3,2,1,0:T(8,128)(2,1)S(1)}, bf16[1,2,8,64,1152]{4,3,2,1,0:T(8,128)(2,1)}, u32[]{:S(2)}, u32[]{:S(2)}) collective-permute-start(bf16[1,2,8,64,1152]{4,3,2,1,0:T(8,128)(2,1)S(1)} %get-tuple-element.85), channel_id=1, source_target_pairs={{0,16},{16,0},{1,17},{17,1},{2,18},{18,2},{3,19},{19,3},{4,20},{20... | collective-permute-start | bytes 7077896 | tf_op jit(solution)/shard_map/ppermute | solution.py:45
  146.4 5.9 collective-permute-start.6
  166.9 14.4 %collective-permute-start.10 = (bf16[1,64,2048]{2,1,0:T(8,128)(2,1)S(1)}, bf16[1,64,2048]{2,1,0:T(8,128)(2,1)S(1)}, u32[]{:S(2)}, u32[]{:S(2)}) collective-permute-start(bf16[1,64,2048]{2,1,0:T(8,128)(2,1)S(1)} %bitcast.394), channel_id=1, source_target_pairs={{0,8},{1,9},{2,10},{3,11},{4,12},{5,13},{6,14},{7,15},{8,0},{9,1},... | collective-permute-start | bytes 786440 | tf_op jit(solution)/shard_map/ppermute | solution.py:45
  183.9 91.8 %all-to-all-start.3 = ((bf16[8,2,64,2048]{3,2,1,0:T(8,128)(2,1)}), bf16[8,2,64,2048]{3,2,1,0:T(8,128)(2,1)}, u32[]{:S(2)}, u32[]{:S(2)}) async-start(bf16[8,2,64,2048]{3,2,1,0:T(8,128)(2,1)} %broadcast_in_dim.490), calls=%async_computation.3 | async-start | bytes 8388608 | tf_op jit(solution)/shard_map/all_to_all | solution.py:121
  193.4 72.6 %collective-permute-start.21 = (bf16[1,8,64,1408]{3,2,1,0:T(8,128)(2,1)}, bf16[1,8,64,1408]{3,2,1,0:T(8,128)(2,1)S(1)}, u32[]{:S(2)}, u32[]{:S(2)}) collective-permute-start(bf16[1,8,64,1408]{3,2,1,0:T(8,128)(2,1)} %bitcast.75), channel_id=1, source_target_pairs={{0,8},{1,9},{2,10},{3,11},{4,12},{5,13},{6,14},{7,15},{8,0},{9,1},... | collective-permute-start | bytes 4325384 | tf_op jit(solution)/shard_map/ppermute | solution.py:45
  193.4 95.2 %collective-permute-start.23 = (bf16[1,176,2048]{2,1,0:T(8,128)(2,1)S(1)}, bf16[1,176,2048]{2,1,0:T(8,128)(2,1)S(1)}, u32[]{:S(2)}, u32[]{:S(2)}) collective-permute-start(bf16[1,176,2048]{2,1,0:T(8,128)(2,1)S(1)} %bitcast.360), channel_id=1, source_target_pairs={{0,8},{1,9},{2,10},{3,11},{4,12},{5,13},{6,14},{7,15},{8,0},{9,1},... | collective-permute-start | bytes 2162696 | tf_op jit(solution)/shard_map/ppermute | solution.py:45
  226.2 62.7 %collective-permute-start.9 = (f32[2,128,128]{2,1,0:T(8,128)}, f32[2,128,128]{2,1,0:T(8,128)S(1)}, u32[]{:S(2)}, u32[]{:S(2)}) collective-permute-start(f32[2,128,128]{2,1,0:T(8,128)} %get-tuple-element.51), channel_id=1, source_target_pairs={{0,8},{1,9},{2,10},{3,11},{4,12},{5,13},{6,14},{7,15},{16,24},{17,... | collective-permute-start | bytes 393224 | tf_op jit(solution)/shard_map/ppermute | solution.py:737
  269.3 51.8 %collective-permute-start.22 = (bf16[1,2,8,64,1408]{4,3,2,1,0:T(8,128)(2,1)}, bf16[1,2,8,64,1408]{4,3,2,1,0:T(8,128)(2,1)}, u32[]{:S(2)}, u32[]{:S(2)}) collective-permute-start(bf16[1,2,8,64,1408]{4,3,2,1,0:T(8,128)(2,1)} %maximum_bitcast_fusion), channel_id=1, source_target_pairs={{0,16},{16,0},{1,17},{17,1},{2,18},{18,2},{3,19},{19,3},{4,20},{20... | collective-permute-start | bytes 8650760 | tf_op jit(solution)/shard_map/ppermute | solution.py:45
  275.6 54.1 %collective-permute-start.11 = (bf16[1024,2048]{1,0:T(8,128)(2,1)}, bf16[1024,2048]{1,0:T(8,128)(2,1)}, u32[]{:S(2)}, u32[]{:S(2)}) collective-permute-start(bf16[1024,2048]{1,0:T(8,128)(2,1)} %bitcast.51), channel_id=1, source_target_pairs={{0,16},{16,0},{1,17},{17,1},{2,18},{18,2},{3,19},{19,3},{4,20},{20... | collective-permute-start | bytes 12582920 | tf_op jit(solution)/shard_map/ppermute | solution.py:45
  288.8 30.1 %collective-permute-start.24 = (bf16[2,176,2048]{2,1,0:T(8,128)(2,1)S(1)}, bf16[2,176,2048]{2,1,0:T(8,128)(2,1)S(1)}, u32[]{:S(2)}, u32[]{:S(2)}) collective-permute-start(bf16[2,176,2048]{2,1,0:T(8,128)(2,1)S(1)} %broadcast_select_fusion.7), channel_id=1, source_target_pairs={{0,16},{16,0},{1,17},{17,1},{2,18},{18,2},{3,19},{19,3},{4,20},{20... | collective-permute-start | bytes 4325384 | tf_op jit(solution)/shard_map/ppermute | solution.py:45
  300.8 15.6 %all-to-all-start.2 = ((bf16[8,128,256]{2,1,0:T(8,128)(2,1)}), bf16[8,128,256]{2,1,0:T(8,128)(2,1)S(1)}, u32[]{:S(2)}, u32[]{:S(2)}) async-start(bf16[8,128,256]{2,1,0:T(8,128)(2,1)} %bitcast.369), calls=%async_computation.2 | async-start | bytes 1048576 | tf_op jit(solution)/shard_map/all_to_all | solution.py:121
  334.1 5.4 collective-permute-start.15
  335.4 10.1 %collective-permute-start.18 = (bf16[1,1,1,128,768]{3,4,2,1,0:T(8,128)(2,1)}, bf16[1,1,1,128,768]{3,4,2,1,0:T(8,128)(2,1)}, u32[]{:S(2)}, u32[]{:S(2)}) collective-permute-start(bf16[1,1,1,128,768]{3,4,2,1,0:T(8,128)(2,1)} %get-tuple-element.99), channel_id=1, source_target_pairs={{0,4},{1,5},{2,6},{3,7},{4,0},{5,1},{6,2},{7,3},{8,12},{9,13},{10,... | collective-permute-start | bytes 589832 | tf_op jit(solution)/shard_map/ppermute | solution.py:45
  337.0 5.4 collective-permute-start.12
  339.7 8.6 %collective-permute-start.16 = (bf16[1,2,1,128,640]{4,3,1,2,0:T(8,128)(2,1)S(1)}, bf16[1,2,1,128,640]{4,3,1,2,0:T(8,128)(2,1)S(1)}, u32[]{:S(2)}, u32[]{:S(2)}) collective-permute-start(bf16[1,2,1,128,640]{4,3,1,2,0:T(8,128)(2,1)S(1)} %broadcast_select_fusion.22), channel_id=1, source_target_pairs={{0,4},{1,5},{2,6},{3,7},{4,0},{5,1},{6,2},{7,3},{8,12},{9,13},{10,... | collective-permute-start | bytes 983048 | tf_op jit(solution)/shard_map/ppermute | solution.py:45
  343.2 16.9 %collective-permute-start.13 = (bf16[1,1,2,128,640]{4,3,2,1,0:T(8,128)(2,1)S(1)}, bf16[1,1,2,128,640]{4,3,2,1,0:T(8,128)(2,1)S(1)}, u32[]{:S(2)}, u32[]{:S(2)}) collective-permute-start(bf16[1,1,2,128,640]{4,3,2,1,0:T(8,128)(2,1)S(1)} %broadcast_select_fusion.24), channel_id=1, source_target_pairs={{0,2},{1,3},{2,0},{3,1},{4,6},{5,7},{6,4},{7,5},{8,10},{9,11},{10,... | collective-permute-start | bytes 983048 | tf_op jit(solution)/shard_map/ppermute | solution.py:45
  346.7 12.1 %collective-permute-start.19 = (bf16[2,1,1,128,768]{4,3,0,2,1:T(8,128)(2,1)S(1)}, bf16[2,1,1,128,768]{4,3,0,2,1:T(8,128)(2,1)S(1)}, u32[]{:S(2)}, u32[]{:S(2)}) collective-permute-start(bf16[2,1,1,128,768]{4,3,0,2,1:T(8,128)(2,1)S(1)} %broadcast_select_fusion.20), channel_id=1, source_target_pairs={{0,1},{1,0},{2,3},{3,2},{4,5},{5,4},{6,7},{7,6},{8,9},{9,8},{10,11... | collective-permute-start | bytes 1179656 | tf_op jit(solution)/shard_map/ppermute | solution.py:45
  348.5 20.7 %collective-permute-start.17 = (bf16[2,2,1,128,640]{4,3,1,0,2:T(8,128)(2,1)S(1)}, bf16[2,2,1,128,640]{4,3,1,0,2:T(8,128)(2,1)S(1)}, u32[]{:S(2)}, u32[]{:S(2)}) collective-permute-start(bf16[2,2,1,128,640]{4,3,1,0,2:T(8,128)(2,1)S(1)} %broadcast_select_fusion.16), channel_id=1, source_target_pairs={{0,1},{1,0},{2,3},{3,2},{4,5},{5,4},{6,7},{7,6},{8,9},{9,8},{10,11... | collective-permute-start | bytes 1966088 | tf_op jit(solution)/shard_map/ppermute | solution.py:45
  359.5 12.6 %collective-permute-start.20 = (bf16[2,1,2,128,768]{4,3,2,0,1:T(8,128)(2,1)S(1)}, bf16[2,1,2,128,768]{4,3,2,0,1:T(8,128)(2,1)S(1)}, u32[]{:S(2)}, u32[]{:S(2)}) collective-permute-start(bf16[2,1,2,128,768]{4,3,2,0,1:T(8,128)(2,1)S(1)} %broadcast_select_fusion.14), channel_id=1, source_target_pairs={{0,2},{1,3},{2,0},{3,1},{4,6},{5,7},{6,4},{7,5},{8,10},{9,11},{10,... | collective-permute-start | bytes 2359304 | tf_op jit(solution)/shard_map/ppermute | solution.py:45
  360.3 10.7 %collective-permute-start.14 = (bf16[1,2,2,128,640]{4,3,2,1,0:T(8,128)(2,1)S(1)}, bf16[1,2,2,128,640]{4,3,2,1,0:T(8,128)(2,1)S(1)}, u32[]{:S(2)}, u32[]{:S(2)}) collective-permute-start(bf16[1,2,2,128,640]{4,3,2,1,0:T(8,128)(2,1)S(1)} %broadcast_select_fusion.18), channel_id=1, source_target_pairs={{0,4},{1,5},{2,6},{3,7},{4,0},{5,1},{6,2},{7,3},{8,12},{9,13},{10,... | collective-permute-start | bytes 1966088 | tf_op jit(solution)/shard_map/ppermute | solution.py:45
  384.9 32.2 %copy-start.24 = (bf16[1024,704]{1,0:T(8,128)(2,1)}, bf16[1024,704]{1,0:T(8,128)(2,1)S(1)}, u32[]{:S(2)}) copy-start(bf16[1024,704]{1,0:T(8,128)(2,1)S(1)} %get-tuple-element.83.refs_0_) | copy-start | bytes 4325380
  395.6 50.2 %all-to-all-start.5 = ((bf16[8,128,2048]{2,1,0:T(8,128)(2,1)}), bf16[8,128,2048]{2,1,0:T(8,128)(2,1)}, u32[]{:S(2)}, u32[]{:S(2)}) async-start(bf16[8,128,2048]{2,1,0:T(8,128)(2,1)} %bitcast.356), calls=%async_computation.5 | async-start | bytes 8388608 | tf_op jit(solution)/shard_map/all_to_all | solution.py:121
  417.1 17.0 %collective-permute-start.25 = (bf16[1,2,8,64,1408]{4,3,2,1,0:T(8,128)(2,1)}, bf16[1,2,8,64,1408]{4,3,2,1,0:T(8,128)(2,1)}, u32[]{:S(2)}, u32[]{:S(2)}) collective-permute-start(bf16[1,2,8,64,1408]{4,3,2,1,0:T(8,128)(2,1)} %bitcast.86), channel_id=1, source_target_pairs={{0,16},{16,0},{1,17},{17,1},{2,18},{18,2},{3,19},{19,3},{4,20},{20... | collective-permute-start | bytes 8650760 | tf_op jit(solution)/shard_map/ppermute | solution.py:45
  428.6 3.6 collective-permute-start.26
  479.8 88.0 %all-to-all-start.7 = ((bf16[8,128,2048]{2,1,0:T(8,128)(2,1)}), bf16[8,128,2048]{2,1,0:T(8,128)(2,1)}, u32[]{:S(2)}, u32[]{:S(2)}) async-start(bf16[8,128,2048]{2,1,0:T(8,128)(2,1)} %broadcast_in_dim.548), calls=%async_computation.7 | async-start | bytes 8388608 | tf_op jit(solution)/shard_map/all_to_all | solution.py:121
  497.1 9.9 %collective-permute-start.27 = (f32[2,128,128]{2,1,0:T(8,128)}, f32[2,128,128]{2,1,0:T(8,128)}, u32[]{:S(2)}, u32[]{:S(2)}) collective-permute-start(f32[2,128,128]{2,1,0:T(8,128)} %get-tuple-element.68), channel_id=1, source_target_pairs={{8,0},{9,1},{10,2},{11,3},{12,4},{13,5},{14,6},{15,7},{24,16},{25,... | collective-permute-start | bytes 393224 | tf_op jit(solution)/shard_map/ppermute | solution.py:800
  538.8 100.0 %collective-permute-start.34 = (bf16[8,768]{1,0:T(8,128)(2,1)}, bf16[8,768]{1,0:T(8,128)(2,1)}, u32[]{:S(2)}, u32[]{:S(2)}) collective-permute-start(bf16[8,768]{1,0:T(8,128)(2,1)} %convert_element_type.464), channel_id=1, source_target_pairs={{8,0},{9,1},{10,2},{11,3},{12,4},{13,5},{14,6},{15,7},{24,16},{25,... | collective-permute-start | bytes 36872 | tf_op jit(solution)/shard_map/ppermute | solution.py:811
  546.3 67.7 %collective-permute-start.31 = (bf16[2,1,2,128,1024]{4,3,2,1,0:T(8,128)(2,1)}, bf16[2,1,2,128,1024]{4,3,2,1,0:T(8,128)(2,1)}, u32[]{:S(2)}, u32[]{:S(2)}) collective-permute-start(bf16[2,1,2,128,1024]{4,3,2,1,0:T(8,128)(2,1)} %dynamic-slice_convert_fusion.3), channel_id=1, source_target_pairs={{0,2},{1,3},{2,0},{3,1},{4,6},{5,7},{6,4},{7,5},{8,10},{9,11},{10,... | collective-permute-start | bytes 3145736 | tf_op jit(solution)/shard_map/ppermute | solution.py:45
  553.0 64.6 %collective-permute-start.28 = (bf16[2,2,1,128,1024]{4,3,2,1,0:T(8,128)(2,1)}, bf16[2,2,1,128,1024]{4,3,2,1,0:T(8,128)(2,1)}, u32[]{:S(2)}, u32[]{:S(2)}) collective-permute-start(bf16[2,2,1,128,1024]{4,3,2,1,0:T(8,128)(2,1)} %dynamic-slice_convert_fusion.4), channel_id=1, source_target_pairs={{0,1},{1,0},{2,3},{3,2},{4,5},{5,4},{6,7},{7,6},{8,9},{9,8},{10,11... | collective-permute-start | bytes 3145736 | tf_op jit(solution)/shard_map/ppermute | solution.py:45
  554.5 68.4 %collective-permute-start.42 = (bf16[1,8,64,1408]{3,2,1,0:T(8,128)(2,1)}, bf16[1,8,64,1408]{3,2,1,0:T(8,128)(2,1)S(1)}, u32[]{:S(2)}, u32[]{:S(2)}) collective-permute-start(bf16[1,8,64,1408]{3,2,1,0:T(8,128)(2,1)} %shard_map.245), channel_id=1, source_target_pairs={{0,8},{1,9},{2,10},{3,11},{4,12},{5,13},{6,14},{7,15},{8,0},{9,1},... | collective-permute-start | bytes 4325384 | tf_op jit(solution)/shard_map/ppermute | solution.py:45
  567.8 149.6 %all-to-all-start.9 = ((f32[32,1,768]{2,1,0:T(1,128)}), f32[32,1,768]{2,1,0:T(1,128)}, u32[]{:S(2)}, u32[]{:S(2)}) async-start(f32[32,1,768]{2,1,0:T(1,128)} %all_to_all.52), calls=%async_computation.9 | async-start | bytes 196608 | tf_op jit(solution)/shard_map/all_to_all | solution.py:131
  613.7 26.9 %collective-permute-start.35 = (bf16[1,2,8,64,1152]{4,3,2,1,0:T(8,128)(2,1)S(1)}, bf16[1,2,8,64,1152]{4,3,2,1,0:T(8,128)(2,1)S(1)}, u32[]{:S(2)}, u32[]{:S(2)}) collective-permute-start(bf16[1,2,8,64,1152]{4,3,2,1,0:T(8,128)(2,1)S(1)} %bitcast.366), channel_id=1, source_target_pairs={{0,16},{16,0},{1,17},{17,1},{2,18},{18,2},{3,19},{19,3},{4,20},{20... | collective-permute-start | bytes 7077896 | tf_op jit(solution)/shard_map/ppermute | solution.py:45
  615.9 14.7 %collective-permute-start.32 = (bf16[2,1,1,128,1024]{4,3,2,1,0:T(8,128)(2,1)S(1)}, bf16[2,1,1,128,1024]{4,3,2,1,0:T(8,128)(2,1)S(1)}, u32[]{:S(2)}, u32[]{:S(2)}) collective-permute-start(bf16[2,1,1,128,1024]{4,3,2,1,0:T(8,128)(2,1)S(1)} %dynamic-slice_convert_fusion.9), channel_id=1, source_target_pairs={{0,1},{1,0},{2,3},{3,2},{4,5},{5,4},{6,7},{7,6},{8,9},{9,8},{10,11... | collective-permute-start | bytes 1572872 | tf_op jit(solution)/shard_map/ppermute | solution.py:45
  621.3 99.7 %collective-permute-start.29 = (bf16[1,2,1,128,1024]{4,3,2,1,0:T(8,128)(2,1)}, bf16[1,2,1,128,1024]{4,3,2,1,0:T(8,128)(2,1)}, u32[]{:S(2)}, u32[]{:S(2)}) collective-permute-start(bf16[1,2,1,128,1024]{4,3,2,1,0:T(8,128)(2,1)} %dynamic-slice_convert_fusion.10), channel_id=1, source_target_pairs={{0,4},{1,5},{2,6},{3,7},{4,0},{5,1},{6,2},{7,3},{8,12},{9,13},{10,... | collective-permute-start | bytes 1572872 | tf_op jit(solution)/shard_map/ppermute | solution.py:45
  638.8 20.3 %collective-permute-start.43 = (bf16[1,2,64,2048]{3,2,1,0:T(8,128)(2,1)}, bf16[1,2,64,2048]{3,2,1,0:T(8,128)(2,1)}, u32[]{:S(2)}, u32[]{:S(2)}) collective-permute-start(bf16[1,2,64,2048]{3,2,1,0:T(8,128)(2,1)} %dynamic-slice_convert_fusion.6), channel_id=1, source_target_pairs={{0,16},{16,0},{1,17},{17,1},{2,18},{18,2},{3,19},{19,3},{4,20},{20... | collective-permute-start | bytes 1572872 | tf_op jit(solution)/shard_map/ppermute | solution.py:45
  649.9 25.5 %collective-permute-start.39 = (bf16[2,1,2,128,1024]{4,3,2,1,0:T(8,128)(2,1)}, bf16[2,1,2,128,1024]{4,3,2,1,0:T(8,128)(2,1)}, u32[]{:S(2)}, u32[]{:S(2)}) collective-permute-start(bf16[2,1,2,128,1024]{4,3,2,1,0:T(8,128)(2,1)} %dynamic-slice_convert_fusion.1), channel_id=1, source_target_pairs={{0,2},{1,3},{2,0},{3,1},{4,6},{5,7},{6,4},{7,5},{8,10},{9,11},{10,... | collective-permute-start | bytes 3145736 | tf_op jit(solution)/shard_map/ppermute | solution.py:45
  657.6 26.4 %collective-permute-start.36 = (bf16[2,2,1,128,1024]{4,3,2,1,0:T(8,128)(2,1)}, bf16[2,2,1,128,1024]{4,3,2,1,0:T(8,128)(2,1)}, u32[]{:S(2)}, u32[]{:S(2)}) collective-permute-start(bf16[2,2,1,128,1024]{4,3,2,1,0:T(8,128)(2,1)} %dynamic-slice_convert_fusion.2), channel_id=1, source_target_pairs={{0,1},{1,0},{2,3},{3,2},{4,5},{5,4},{6,7},{7,6},{8,9},{9,8},{10,11... | collective-permute-start | bytes 3145736 | tf_op jit(solution)/shard_map/ppermute | solution.py:45
  662.7 25.0 %collective-permute-start.44 = (bf16[1,1,64,2048]{3,2,1,0:T(8,128)(2,1)}, bf16[1,1,64,2048]{3,2,1,0:T(8,128)(2,1)S(1)}, u32[]{:S(2)}, u32[]{:S(2)}) collective-permute-start(bf16[1,1,64,2048]{3,2,1,0:T(8,128)(2,1)} %shard_map.246), channel_id=1, source_target_pairs={{0,8},{1,9},{2,10},{3,11},{4,12},{5,13},{6,14},{7,15},{8,0},{9,1},... | collective-permute-start | bytes 786440 | tf_op jit(solution)/shard_map/ppermute | solution.py:45
  677.8 16.2 %collective-permute-start.40 = (bf16[2,1,1,128,1024]{4,3,2,1,0:T(8,128)(2,1)S(1)}, bf16[2,1,1,128,1024]{4,3,2,1,0:T(8,128)(2,1)S(1)}, u32[]{:S(2)}, u32[]{:S(2)}) collective-permute-start(bf16[2,1,1,128,1024]{4,3,2,1,0:T(8,128)(2,1)S(1)} %dynamic-slice_convert_fusion.7), channel_id=1, source_target_pairs={{0,1},{1,0},{2,3},{3,2},{4,5},{5,4},{6,7},{7,6},{8,9},{9,8},{10,11... | collective-permute-start | bytes 1572872 | tf_op jit(solution)/shard_map/ppermute | solution.py:45
  685.7 13.4 %collective-permute-start.37 = (bf16[1,2,1,128,1024]{4,3,2,1,0:T(8,128)(2,1)S(1)}, bf16[1,2,1,128,1024]{4,3,2,1,0:T(8,128)(2,1)S(1)}, u32[]{:S(2)}, u32[]{:S(2)}) collective-permute-start(bf16[1,2,1,128,1024]{4,3,2,1,0:T(8,128)(2,1)S(1)} %dynamic-slice_convert_fusion.8), channel_id=1, source_target_pairs={{0,4},{1,5},{2,6},{3,7},{4,0},{5,1},{6,2},{7,3},{8,12},{9,13},{10,... | collective-permute-start | bytes 1572872 | tf_op jit(solution)/shard_map/ppermute | solution.py:45
  694.9 12.0 %collective-permute-start.41 = (bf16[1,1,1,128,1024]{4,3,2,1,0:T(8,128)(2,1)}, bf16[1,1,1,128,1024]{4,3,2,1,0:T(8,128)(2,1)S(1)}, u32[]{:S(2)}, u32[]{:S(2)}) collective-permute-start(bf16[1,1,1,128,1024]{4,3,2,1,0:T(8,128)(2,1)} %dynamic-slice_convert_fusion.12), channel_id=1, source_target_pairs={{0,4},{1,5},{2,6},{3,7},{4,0},{5,1},{6,2},{7,3},{8,12},{9,13},{10,... | collective-permute-start | bytes 786440 | tf_op jit(solution)/shard_map/ppermute | solution.py:45
  701.0 6.7 collective-permute-start.38
  704.7 57.4 %collective-permute-start.45 = (bf16[1,8,64,1152]{3,2,1,0:T(8,128)(2,1)}, bf16[1,8,64,1152]{3,2,1,0:T(8,128)(2,1)}, u32[]{:S(2)}, u32[]{:S(2)}) collective-permute-start(bf16[1,8,64,1152]{3,2,1,0:T(8,128)(2,1)} %shard_map.247), channel_id=1, source_target_pairs={{0,8},{1,9},{2,10},{3,11},{4,12},{5,13},{6,14},{7,15},{8,0},{9,1},... | collective-permute-start | bytes 3538952 | tf_op jit(solution)/shard_map/ppermute | solution.py:45
  715.7 23.6 %collective-permute-start.33 = (bf16[1,1,1,128,1024]{4,3,2,1,0:T(8,128)(2,1)}, bf16[1,1,1,128,1024]{4,3,2,1,0:T(8,128)(2,1)}, u32[]{:S(2)}, u32[]{:S(2)}) collective-permute-start(bf16[1,1,1,128,1024]{4,3,2,1,0:T(8,128)(2,1)} %dynamic-slice_convert_fusion.14), channel_id=1, source_target_pairs={{0,4},{1,5},{2,6},{3,7},{4,0},{5,1},{6,2},{7,3},{8,12},{9,13},{10,... | collective-permute-start | bytes 786440 | tf_op jit(solution)/shard_map/ppermute | solution.py:45
  717.4 58.8 %all-to-all-start.8 = ((bf16[8,64,1408]{2,1,0:T(8,128)(2,1)}), bf16[8,64,1408]{2,1,0:T(8,128)(2,1)S(1)}, u32[]{:S(2)}, u32[]{:S(2)}) async-start(bf16[8,64,1408]{2,1,0:T(8,128)(2,1)} %shard_map.248), calls=%async_computation.8 | async-start | bytes 2883584 | tf_op jit(solution)/shard_map/all_to_all | solution.py:121
  724.2 16.2 %collective-permute-start.30 = (bf16[1,1,1,128,1024]{4,3,2,1,0:T(8,128)(2,1)}, bf16[1,1,1,128,1024]{4,3,2,1,0:T(8,128)(2,1)}, u32[]{:S(2)}, u32[]{:S(2)}) collective-permute-start(bf16[1,1,1,128,1024]{4,3,2,1,0:T(8,128)(2,1)} %dynamic-slice_convert_fusion.15), channel_id=1, source_target_pairs={{0,2},{1,3},{2,0},{3,1},{4,6},{5,7},{6,4},{7,5},{8,10},{9,11},{10,... | collective-permute-start | bytes 786440 | tf_op jit(solution)/shard_map/ppermute | solution.py:45
  741.6 44.3 %collective-permute-start.46 = (bf16[64,2048]{1,0:T(8,128)(2,1)}, bf16[64,2048]{1,0:T(8,128)(2,1)}, u32[]{:S(2)}, u32[]{:S(2)}) collective-permute-start(bf16[64,2048]{1,0:T(8,128)(2,1)} %get-tuple-element.79), channel_id=1, source_target_pairs={{0,0},{1,4},{2,8},{3,12},{4,16},{5,20},{6,24},{7,28},{8,1},{9,5},{... | collective-permute-start | bytes 786440 | tf_op jit(solution)/shard_map/ppermute | solution.py:824
  777.3 41.6 %all-to-all-start.10 = ((bf16[8,64,1152]{2,1,0:T(8,128)(2,1)}), bf16[8,64,1152]{2,1,0:T(8,128)(2,1)}, u32[]{:S(2)}, u32[]{:S(2)}) async-start(bf16[8,64,1152]{2,1,0:T(8,128)(2,1)} %shard_map.249), calls=%async_computation.10 | async-start | bytes 2359296 | tf_op jit(solution)/shard_map/all_to_all | solution.py:121
  784.8 28.8 %collective-permute-start.47 = (bf16[1,1,176,2048]{3,2,1,0:T(8,128)(2,1)}, bf16[1,1,176,2048]{3,2,1,0:T(8,128)(2,1)}, u32[]{:S(2)}, u32[]{:S(2)}) collective-permute-start(bf16[1,1,176,2048]{3,2,1,0:T(8,128)(2,1)} %shard_map.250), channel_id=1, source_target_pairs={{0,8},{1,9},{2,10},{3,11},{4,12},{5,13},{6,14},{7,15},{8,0},{9,1},... | collective-permute-start | bytes 2162696 | tf_op jit(solution)/shard_map/ppermute | solution.py:45
  (112 other events, 784.7 us)

commit v3 on v2

--- a/solution.py
+++ b/solution.py
@@ -255,6 +255,14 @@
         (((1,), (1,)), ((), ())),
         preferred_element_type=FULL,
     )
+
+
+def mul_once(left, right):
+    return jnp.dot(left.astype(LOW), right.astype(LOW), preferred_element_type=FULL)
+
+
+def mul_once_t(left, right):
+    return dot_right_t(left.astype(LOW), right.astype(LOW))
 
 
 def grid_index(dim):
@@ -470,27 +478,25 @@
             key, key_scale = unit_part(jax.nn.silu(mixed[1][0]))
             value = jax.nn.silu(mixed[2][0])
             weight = jax.nn.sigmoid(last[:, head : head + 1])
-            key_s = split(key)
             leave = now_ref[head]
-            leave_s = split(leave)
-            now_ref[head] = mul(split(map_ref[at].T), leave_s) + term_ref[at]
-            ddelta = first_ref[at] + mul(split(key * ending), leave_s)
-            solved = mul(split(inv_ref[at].T), split(ddelta))
-            delta_s = split(delta_ref[at])
+            now_ref[head] = mul(split(map_ref[at].T), split(leave)) + term_ref[at]
+            ddelta = first_ref[at] + mul_once(key * ending, leave)
+            solved = mul_once(inv_ref[at].T, ddelta)
+            delta = delta_ref[at]
             dout = dout_ref[at]
-            ends = split(jnp.concatenate([solved, dout], 0))
-            by_state = mul_t(ends, split(p_ref[at]))
-            by_delta = mul_t(ends, delta_s)
+            ends = jnp.concatenate([solved, dout], 0)
+            by_state = mul_once_t(ends, p_ref[at])
+            by_delta = mul_once_t(ends, delta)
             dright = -by_state[:CHUNK]
             dsystem = -by_delta[:CHUNK] * lower
             datt = by_delta[CHUNK:] * inclusive
-            dquery = carried * by_state[CHUNK:] + mul(split(datt), key_s)
-            gram = mul_t(key_s, key_s)
+            dquery = carried * by_state[CHUNK:] + mul_once(datt, key)
+            gram = mul_once_t(key, key)
             dgram = weight * dsystem
-            left = split(jnp.concatenate([datt.T, dgram + dgram.T], 1))
-            right = tuple(jnp.concatenate([a, b], 0) for a, b in zip(split(query), key_s))
-            dkey = mul(left, right) + (weight * carried) * dright
-            dkey = dkey + ending * mul_t(delta_s, leave_s)
+            left = jnp.concatenate([datt.T, dgram + dgram.T], 1)
+            right = jnp.concatenate([query, key], 0)
+            dkey = mul_once(left, right) + (weight * carried) * dright
+            dkey = dkey + ending * mul_once_t(delta, leave)
             dvalue = weight * solved
             dweight = row_sum(solved * value + carried * dright * key + dsystem * gram)
             dlogit = dweight * weight * (1.0 - weight)

time: 837 us -> 834 us (level)
  no operation moved by 1% of the time
where the time goes in v3:
time: 834 us; the launch traced here: 826 us
  waiting for transfers between devices  221 us (26%)
  local copies, waits for them, and re-layouts  154 us (18%)
  starting transfers between devices  147 us (18%)
  other arithmetic  114 us (14%)
  matrix products  90.6 us (11%)
  Pallas kernels  81.2 us (10%)
  blocking collectives  15.3 us (2%)
    ppermute x43, waiting for transfers between devices, swap(): lax.ppermute(values, axis, [(i, i ^ bit) for i in range(lax.axis_size(axi...  194 us
    pallas_call x4, Pallas kernels, on_chip(): pl.pallas_call(lambda *refs: body(*refs[:used], *refs[used + spare:]), ou...  81.2 us
    ppermute x43, starting transfers between devices, swap(): lax.ppermute(values, axis, [(i, i ^ bit) for i in range(lax.axis_size(axi...  58.3 us
    all_to_all x8, starting transfers between devices, cube_turn(): lax.all_to_all(values, 'seq', 0, 0, axis_index_groups=groups, tiled=True)  37.8 us
    all_to_all x1, starting transfers between devices, sum_all(): lax.all_to_all(values, ('dp', 'seq'), 0, 0, tiled=True)  34.7 us
    dot_general x6, matrix products, dot_right_t(): lax.dot_general(left, right, (((1,), (1,)), ((), ())), preferred_element_...  34.2 us
    unnamed x245, local copies, waits for them, and re-layouts  30.8 us
    dot_general x4, matrix products, dot_left_t(): lax.dot_general(left, right, (((0,), (0,)), ((), ())), preferred_element_...  30.6 us
  transfers between devices with their start and end apart: 58, of which 26 were waited for; matrix products, arithmetic and copies ran while one was open for 32% of the time, Pallas kernels for 10%

profile of v3, /device:TPU:0, one launch (start us, length us, event | category | flops | bytes accessed | tf_op | source)
XLA Modules:
  0.0 826.3 jit_solution(896446194785035905)
XLA Ops:
  13.8 4.9 all-to-all-start
  27.6 4.0 all-to-all-start.1
  46.0 23.5 %collective-permute-done.1 = bf16[1,2,1,2,128,1024]{5,4,1,3,2,0:T(8,128)(2,1)} collective-permute-done((bf16[1,2,1,2,128,1024]{5,4,1,3,2,0:T(8,128)(2,1)}, bf16[1,2,1,2,128,1024]{5,4,1,3,2,0:T(8,128)(2,1)}, u32[]{:S(2)}, u32[]{:S(2)}) %collective-permute-start.1) | collective-permute-done | bytes 1048608 | tf_op jit(solution)/shard_map/ppermute | solution.py:45
  91.9 3.0 copy.273
  94.9 4.5 reshape.605
  105.9 4.9 all-to-all-start.4
  110.8 22.1 %collective-permute-done.7 = bf16[1,8,64,1152]{3,2,1,0:T(8,128)(2,1)} collective-permute-done((bf16[1,8,64,1152]{3,2,1,0:T(8,128)(2,1)S(1)}, bf16[1,8,64,1152]{3,2,1,0:T(8,128)(2,1)}, u32[]{:S(2)}, u32[]{:S(2)}) %collective-permute-start.7) | collective-permute-done | bytes 1179680 | tf_op jit(solution)/shard_map/ppermute | solution.py:45
  148.6 3.8 fusion.4
  153.1 3.1 fusion
  159.1 7.8 fusion.62.refs_0_
  168.2 13.1 %collective-permute-done.10 = bf16[1,64,2048]{2,1,0:T(8,128)(2,1)S(1)} collective-permute-done((bf16[1,64,2048]{2,1,0:T(8,128)(2,1)S(1)}, bf16[1,64,2048]{2,1,0:T(8,128)(2,1)S(1)}, u32[]{:S(2)}, u32[]{:S(2)}) %collective-permute-start.10) | collective-permute-done | bytes 262176 | tf_op jit(solution)/shard_map/ppermute | solution.py:45
  183.9 4.7 all-to-all-start.3
  196.3 29.9 %shard_map.237 = (f32[16,128,128]{2,1,0:T(8,128)}, f32[16,128,128]{2,1,0:T(8,128)}, f32[16,128,128]{2,1,0:T(8,128)}, f32[16,128,128]{2,1,0:T(8,128)}, f32[16,128...) custom-call(f32[1040,1152]{1,0:T(8,128)} %fusion.62.refs_0_, ...), custom_call_target="tpu_custom_call" | custom-call | flops 32212254720 | bytes 20971520 | tf_op jit(solution)/shard_map/pallas_call | solution.py:551
  228.1 37.8 %collective-permute-done.21 = bf16[1,8,64,1408]{3,2,1,0:T(8,128)(2,1)S(1)} collective-permute-done((bf16[1,8,64,1408]{3,2,1,0:T(8,128)(2,1)}, bf16[1,8,64,1408]{3,2,1,0:T(8,128)(2,1)S(1)}, u32[]{:S(2)}, u32[]{:S(2)}) %collective-permute-start.21) | collective-permute-done | bytes 1441824 | tf_op jit(solution)/shard_map/ppermute | solution.py:45
  266.0 3.3 maximum_bitcast_fusion
  269.3 6.4 all-to-all-done.3
  275.7 12.9 %collective-permute-done.23 = bf16[1,176,2048]{2,1,0:T(8,128)(2,1)S(1)} collective-permute-done((bf16[1,176,2048]{2,1,0:T(8,128)(2,1)S(1)}, bf16[1,176,2048]{2,1,0:T(8,128)(2,1)S(1)}, u32[]{:S(2)}, u32[]{:S(2)}) %collective-permute-start.23) | collective-permute-done | bytes 720928 | tf_op jit(solution)/shard_map/ppermute | solution.py:45
  289.7 11.1 %shard_map.238 = (f32[16,128,128]{2,1,0:T(8,128)}, f32[16,128,128]{2,1,0:T(8,128)}, f32[16,128,128]{2,1,0:T(8,128)}, bf16[1024,256]{1,0:T(8,128)(2,1)}) custom-call(f32[1040,1152]{1,0:T(8,128)} %fusion.62.refs_0_, f32[1032,8]{1,0:T(8,128)} %pad.5.refs_2_.refs_1_, f32[1,256]{1,0:T(1,128)} %bitcast.429, f32[16,128,128]{2,1,0:T(8,128)} %get-tuple-element.45.refs_3_.refs_4_, ...), custom_call_target="tpu_custom_call" | custom-call | flops 11811160064 | bytes 20971520 | tf_op jit(solution)/shard_map/pallas_call | solution.py:551
  300.8 7.1 all-to-all-start.2
  310.0 6.4 all-to-all-done.2
  321.1 5.8 pad_maximum_fusion
  329.8 3.0 multiply_reduce_fusion.4
  349.8 9.0 %collective-permute-done.19 = bf16[2,1,1,128,768]{4,3,0,2,1:T(8,128)(2,1)S(1)} collective-permute-done((bf16[2,1,1,128,768]{4,3,0,2,1:T(8,128)(2,1)S(1)}, bf16[2,1,1,128,768]{4,3,0,2,1:T(8,128)(2,1)S(1)}, u32[]{:S(2)}, u32[]{:S(2)}) %collective-permute-start.19) | collective-permute-done | bytes 393248 | tf_op jit(solution)/shard_map/ppermute | solution.py:45
  361.1 8.1 collective-permute-done.17
  372.4 6.7 fusion.16
  379.2 5.7 fusion.11
  384.9 10.7 %convolution_convert_fusion = bf16[1024,2048]{1,0:T(8,128)(2,1)} fusion(bf16[2048,1408]{1,0:T(8,128)(2,1)S(1)} %bitcast.344, bf16[1024,704]{1,0:T(8,128)(2,1)} %get-tuple-element.82, bf16[1024,704]{1,0:T(8,128)(2,1)} %get-tuple-element.81), kind=kOutput, calls=%fused_computation.26 | convolution fusion | flops 5913444352 | bytes 12845056 | tf_op jit(solution)/shard_map/dot_general | solution.py:37
  395.6 4.6 all-to-all-start.5
  400.2 10.7 %fusion.15 = f32[2048,1408]{1,0:T(8,128)S(1)} fusion(bf16[1024,704]{1,0:T(8,128)(2,1)} %get-tuple-element.82, bf16[1024,704]{1,0:T(8,128)(2,1)} %get-tuple-element.81, bf16[1024,768]{1,0:T(8,128)(2,1)} %copy-done.62, bf16[1024,640]{1,0:T(8,128)(2,1)} %copy-done.63, bf16[1024,640]{1,0:T(8,128)(2,1)} %copy-done.64), kind=kOutput, calls=%fused_computation.67 | convolution fusion | flops 5923930112 | bytes 18612224 | tf_op jit(solution)/shard_map/dot_general | solution.py:33
  410.9 4.3 copy-done.6
  419.0 5.8 fusion.5
  429.1 3.1 collective-permute-done.26
  434.1 4.9 add_bitcast_fusion
  439.0 6.9 all-to-all-done.5
  452.5 3.9 convolution_convert_fusion.2
  456.4 3.7 convolution_convert_fusion.1
  461.0 15.3 %all_to_all.64 = bf16[8,128,256]{2,1,0:T(8,128)(2,1)} all-to-all(bf16[8,128,256]{2,1,0:T(8,128)(2,1)S(1)} %bitcast.379), channel_id=1, replica_groups={{0,1,2,3,4,5,6,7},{8,9,10,11,12,13,14,15},{16,17,18,19,20,21,22,23},{24..., dimensions={0} | all-to-all | bytes 1048576 | tf_op jit(solution)/shard_map/all_to_all | solution.py:121
  476.3 3.5 broadcast_in_dim.548
  479.8 4.6 all-to-all-start.7
  484.5 12.6 %shard_map.239 = (f32[16,128,128]{2,1,0:T(8,128)}, f32[16,128,128]{2,1,0:T(8,128)}, f32[16,128,128]{2,1,0:T(8,128)}, bf16[1024,256]{1,0:T(8,128)(2,1)}, f32[2,128,128]{2,1,0:T(8,128)}) custom-call(f32[1040,1152]{1,0:T(8,128)} %fusion.62.refs_0_, f32[1032,8]{1,0:T(8,128)} %pad.5.refs_2_.refs_1_, f32[1,256]{1,0:T(1,128)} %bitcast.430, ...), custom_call_target="tpu_custom_call" | custom-call | flops 12884901888 | bytes 20971520 | tf_op jit(solution)/shard_map/pallas_call | solution.py:551
  500.6 3.3 bitcast_select_fusion
  503.9 3.1 slice.282.refs_0_
  507.0 27.7 %shard_map.240 = (bf16[1040,1152]{1,0:T(8,128)(2,1)}, f32[8,768]{1,0:T(8,128)}, f32[8,768]{1,0:T(8,128)}, f32[8,768]{1,0:T(8,128)}) custom-call(f32[1040,1152]{1,0:T(8,128)} %fusion.62.refs_0_, f32[4,768]{1,0:T(4,128)} %bitcast.426, f32[1032,8]{1,0:T(8,128)} %pad.5.refs_2_.refs_1_, f32[8,1,128]{2,1,0:T(1,128)} %bitcast.419, ...), custom_call_target="tpu_custom_call" | custom-call | flops 32212254720 | bytes 20971520 | tf_op jit(solution)/shard_map/pallas_call | solution.py:551
  537.6 3.6 fusion.18
  551.7 4.7 collective-permute-start.42
  565.0 34.7 %all-to-all-start.9 = ((f32[32,1,768]{2,1,0:T(1,128)}), f32[32,1,768]{2,1,0:T(1,128)}, u32[]{:S(2)}, u32[]{:S(2)}) async-start(f32[32,1,768]{2,1,0:T(1,128)} %all_to_all.52), calls=%async_computation.9 | async-start | bytes 196608 | tf_op jit(solution)/shard_map/all_to_all | solution.py:131
  600.4 10.2 %fusion.60 = f32[2048,1152]{1,0:T(8,128)S(1)} fusion(bf16[1040,1152]{1,0:T(8,128)(2,1)} %shard_map.243, f32[2048]{0:T(1024)S(1)} %bitcast.428, f32[1040]{0:T(1024)} %copy-done.89, bf16[1024,2048]{1,0:T(8,128)(2,1)} %fusion.4, bf16[16,2048]{1,0:T(8,128)(2,1)} %copy-done.70), kind=kOutput, calls=%fused_computation.238 | convolution fusion | flops 4922245120 | bytes 16105536 | tf_op jit(solution)/shard_map/dot_general | solution.py:33
  621.7 6.1 collective-permute-done.32
  628.0 3.9 fusion.73
  640.4 5.4 fusion.72
  648.9 4.7 fusion.71
  662.2 10.5 %collective-permute-done.39 = bf16[2,1,2,128,1024]{4,3,2,1,0:T(8,128)(2,1)} collective-permute-done((bf16[2,1,2,128,1024]{4,3,2,1,0:T(8,128)(2,1)}, bf16[2,1,2,128,1024]{4,3,2,1,0:T(8,128)(2,1)}, u32[]{:S(2)}, u32[]{:S(2)}) %collective-permute-start.39) | collective-permute-done | bytes 1048608 | tf_op jit(solution)/shard_map/ppermute | solution.py:45
  676.7 4.6 collective-permute-done.36
  686.0 5.2 collective-permute-done.40
  714.7 3.6 all-to-all-start.8
  725.8 10.7 %collective-permute-done.33 = bf16[1,1,1,128,1024]{4,3,2,1,0:T(8,128)(2,1)} collective-permute-done((bf16[1,1,1,128,1024]{4,3,2,1,0:T(8,128)(2,1)}, bf16[1,1,1,128,1024]{4,3,2,1,0:T(8,128)(2,1)}, u32[]{:S(2)}, u32[]{:S(2)}) %collective-permute-start.33) | collective-permute-done | bytes 262176 | tf_op jit(solution)/shard_map/ppermute | solution.py:45
  738.9 4.1 collective-permute-start.46
  743.0 16.4 %collective-permute-done.45 = bf16[1,8,64,1152]{3,2,1,0:T(8,128)(2,1)} collective-permute-done((bf16[1,8,64,1152]{3,2,1,0:T(8,128)(2,1)}, bf16[1,8,64,1152]{3,2,1,0:T(8,128)(2,1)}, u32[]{:S(2)}, u32[]{:S(2)}) %collective-permute-start.45) | collective-permute-done | bytes 1179680 | tf_op jit(solution)/shard_map/ppermute | solution.py:45
  765.9 7.5 all-to-all-done.8.refs_1_
  774.5 4.4 all-to-all-start.10
  787.8 4.7 reshape.624
  795.1 3.3 reshape.625.refs_2_
  798.4 4.7 reshape.622
  805.7 3.4 reshape.623.refs_1_
  (586 shorter events, 285.5 us)
Async XLA Ops:
  8.1 32.2 %copy-start.32 = (bf16[2,128,1024]{2,1,0:T(8,128)(2,1)}, bf16[2,128,1024]{2,1,0:T(8,128)(2,1)S(1)}, u32[]{:S(2)}) copy-start(bf16[2,128,1024]{2,1,0:T(8,128)(2,1)S(1)} %get-tuple-element.90) | copy-start | bytes 1572868
  8.1 23.4 %collective-permute-start = (bf16[1,1,1,2,128,1024]{5,4,3,2,1,0:T(8,128)(2,1)}, bf16[1,1,1,2,128,1024]{5,4,3,2,1,0:T(8,128)(2,1)}, u32[]{:S(2)}, u32[]{:S(2)}) collective-permute-start(bf16[1,1,1,2,128,1024]{5,4,3,2,1,0:T(8,128)(2,1)} %get-tuple-element.91), channel_id=1, source_target_pairs={{0,2},{1,3},{2,0},{3,1},{4,6},{5,7},{6,4},{7,5},{8,10},{9,11},{10,... | collective-permute-start | bytes 1572872 | tf_op jit(solution)/shard_map/ppermute | solution.py:45
  13.8 13.1 %all-to-all-start = ((bf16[32,2,544]{2,1,0:T(2,128)(2,1)}), bf16[32,2,544]{2,1,0:T(2,128)(2,1)S(1)}, u32[]{:S(2)}, u32[]{:S(2)}) async-start(bf16[32,2,544]{2,1,0:T(2,128)(2,1)} %reshape.649), calls=%async_computation | async-start | bytes 163840 | tf_op jit(solution)/shard_map/all_to_all | solution.py:127
  18.7 21.7 %collective-permute-start.3 = (bf16[1,1,1,2,128,1024]{5,4,3,2,1,0:T(8,128)(2,1)}, bf16[1,1,1,2,128,1024]{5,4,3,2,1,0:T(8,128)(2,1)}, u32[]{:S(2)}, u32[]{:S(2)}) collective-permute-start(bf16[1,1,1,2,128,1024]{5,4,3,2,1,0:T(8,128)(2,1)} %get-tuple-element.92), channel_id=1, source_target_pairs={{0,4},{1,5},{2,6},{3,7},{4,0},{5,1},{6,2},{7,3},{8,12},{9,13},{10,... | collective-permute-start | bytes 1572872 | tf_op jit(solution)/shard_map/ppermute | solution.py:45
  26.9 49.0 %copy-start.80 = (pred[2]{0:T(512)(128)(4,1)}, pred[2]{0:T(512)(128)(4,1)S(1)}, u32[]{:S(2)}) copy-start(pred[2]{0:T(512)(128)(4,1)S(1)} %iota_compare_fusion.2) | copy-start | bytes 10
  27.6 52.7 %all-to-all-start.1 = ((bf16[8,64,1152]{2,1,0:T(8,128)(2,1)}), bf16[8,64,1152]{2,1,0:T(8,128)(2,1)S(1)}, u32[]{:S(2)}, u32[]{:S(2)}) async-start(bf16[8,64,1152]{2,1,0:T(8,128)(2,1)} %copy.202), calls=%async_computation.1 | async-start | bytes 2359296 | tf_op jit(solution)/shard_map/all_to_all | solution.py:121
  33.8 35.7 %collective-permute-start.1 = (bf16[1,2,1,2,128,1024]{5,4,1,3,2,0:T(8,128)(2,1)}, bf16[1,2,1,2,128,1024]{5,4,1,3,2,0:T(8,128)(2,1)}, u32[]{:S(2)}, u32[]{:S(2)}) collective-permute-start(bf16[1,2,1,2,128,1024]{5,4,1,3,2,0:T(8,128)(2,1)} %broadcast_select_fusion.10), channel_id=1, source_target_pairs={{0,4},{1,5},{2,6},{3,7},{4,0},{5,1},{6,2},{7,3},{8,12},{9,13},{10,... | collective-permute-start | bytes 3145736 | tf_op jit(solution)/shard_map/ppermute | solution.py:45
  38.9 47.0 %copy-start.82 = (pred[2]{0:T(512)(128)(4,1)}, pred[2]{0:T(512)(128)(4,1)S(1)}, u32[]{:S(2)}) copy-start(pred[2]{0:T(512)(128)(4,1)S(1)} %iota_compare_fusion.4) | copy-start | bytes 10
  40.1 42.9 %copy-start.74 = (pred[2]{0:T(512)(128)(4,1)}, pred[2]{0:T(512)(128)(4,1)S(1)}, u32[]{:S(2)}) copy-start(pred[2]{0:T(512)(128)(4,1)S(1)} %iota_compare_fusion.3) | copy-start | bytes 10
  40.3 32.0 %copy-start.66 = (bf16[32,1,1088]{2,0,1:T(8,128)(2,1)}, bf16[32,1,1088]{2,0,1:T(8,128)(2,1)S(1)}, u32[]{:S(2)}) copy-start(bf16[32,1,1088]{2,0,1:T(8,128)(2,1)S(1)} %copy.276) | copy-start | bytes 208900
  42.5 33.4 %collective-permute-start.4 = (bf16[2,1,1,2,128,1024]{5,4,0,3,2,1:T(8,128)(2,1)}, bf16[2,1,1,2,128,1024]{5,4,0,3,2,1:T(8,128)(2,1)}, u32[]{:S(2)}, u32[]{:S(2)}) collective-permute-start(bf16[2,1,1,2,128,1024]{5,4,0,3,2,1:T(8,128)(2,1)} %broadcast_select_fusion.8), channel_id=1, source_target_pairs={{0,1},{1,0},{2,3},{3,2},{4,5},{5,4},{6,7},{7,6},{8,9},{9,8},{10,11... | collective-permute-start | bytes 3145736 | tf_op jit(solution)/shard_map/ppermute | solution.py:45
  72.3 63.6 %collective-permute-start.2 = (bf16[2,2,1,2,128,1024]{5,4,1,0,3,2:T(8,128)(2,1)}, bf16[2,2,1,2,128,1024]{5,4,1,0,3,2:T(8,128)(2,1)}, u32[]{:S(2)}, u32[]{:S(2)}) collective-permute-start(bf16[2,2,1,2,128,1024]{5,4,1,0,3,2:T(8,128)(2,1)} %broadcast_select_fusion.5), channel_id=1, source_target_pairs={{0,1},{1,0},{2,3},{3,2},{4,5},{5,4},{6,7},{7,6},{8,9},{9,8},{10,11... | collective-permute-start | bytes 6291464 | tf_op jit(solution)/shard_map/ppermute | solution.py:45
  78.8 60.4 %collective-permute-start.5 = (bf16[2,1,2,2,128,1024]{5,4,2,0,3,1:T(8,128)(2,1)}, bf16[2,1,2,2,128,1024]{5,4,2,0,3,1:T(8,128)(2,1)}, u32[]{:S(2)}, u32[]{:S(2)}) collective-permute-start(bf16[2,1,2,2,128,1024]{5,4,2,0,3,1:T(8,128)(2,1)} %broadcast_select_fusion.3), channel_id=1, source_target_pairs={{0,2},{1,3},{2,0},{3,1},{4,6},{5,7},{6,4},{7,5},{8,10},{9,11},{10,... | collective-permute-start | bytes 6291464 | tf_op jit(solution)/shard_map/ppermute | solution.py:45
  80.3 52.6 %collective-permute-start.7 = (bf16[1,8,64,1152]{3,2,1,0:T(8,128)(2,1)S(1)}, bf16[1,8,64,1152]{3,2,1,0:T(8,128)(2,1)}, u32[]{:S(2)}, u32[]{:S(2)}) collective-permute-start(bf16[1,8,64,1152]{3,2,1,0:T(8,128)(2,1)S(1)} %bitcast.345), channel_id=1, source_target_pairs={{0,8},{1,9},{2,10},{3,11},{4,12},{5,13},{6,14},{7,15},{8,0},{9,1},... | collective-permute-start | bytes 3538952 | tf_op jit(solution)/shard_map/ppermute | solution.py:45
  105.9 75.4 %all-to-all-start.4 = ((bf16[8,64,1408]{2,1,0:T(8,128)(2,1)}), bf16[8,64,1408]{2,1,0:T(8,128)(2,1)}, u32[]{:S(2)}, u32[]{:S(2)}) async-start(bf16[8,64,1408]{2,1,0:T(8,128)(2,1)} %pad_maximum_fusion.11), calls=%async_computation.4 | async-start | bytes 2883584 | tf_op jit(solution)/shard_map/all_to_all | solution.py:121
  135.9 20.3 %collective-permute-start.8 = (bf16[1,2,8,64,1152]{4,3,2,1,0:T(8,128)(2,1)S(1)}, bf16[1,2,8,64,1152]{4,3,2,1,0:T(8,128)(2,1)}, u32[]{:S(2)}, u32[]{:S(2)}) collective-permute-start(bf16[1,2,8,64,1152]{4,3,2,1,0:T(8,128)(2,1)S(1)} %get-tuple-element.85), channel_id=1, source_target_pairs={{0,16},{16,0},{1,17},{17,1},{2,18},{18,2},{3,19},{19,3},{4,20},{20... | collective-permute-start | bytes 7077896 | tf_op jit(solution)/shard_map/ppermute | solution.py:45
  146.4 5.9 collective-permute-start.6
  166.9 14.4 %collective-permute-start.10 = (bf16[1,64,2048]{2,1,0:T(8,128)(2,1)S(1)}, bf16[1,64,2048]{2,1,0:T(8,128)(2,1)S(1)}, u32[]{:S(2)}, u32[]{:S(2)}) collective-permute-start(bf16[1,64,2048]{2,1,0:T(8,128)(2,1)S(1)} %bitcast.394), channel_id=1, source_target_pairs={{0,8},{1,9},{2,10},{3,11},{4,12},{5,13},{6,14},{7,15},{8,0},{9,1},... | collective-permute-start | bytes 786440 | tf_op jit(solution)/shard_map/ppermute | solution.py:45
  183.9 91.8 %all-to-all-start.3 = ((bf16[8,2,64,2048]{3,2,1,0:T(8,128)(2,1)}), bf16[8,2,64,2048]{3,2,1,0:T(8,128)(2,1)}, u32[]{:S(2)}, u32[]{:S(2)}) async-start(bf16[8,2,64,2048]{3,2,1,0:T(8,128)(2,1)} %broadcast_in_dim.490), calls=%async_computation.3 | async-start | bytes 8388608 | tf_op jit(solution)/shard_map/all_to_all | solution.py:121
  193.4 72.6 %collective-permute-start.21 = (bf16[1,8,64,1408]{3,2,1,0:T(8,128)(2,1)}, bf16[1,8,64,1408]{3,2,1,0:T(8,128)(2,1)S(1)}, u32[]{:S(2)}, u32[]{:S(2)}) collective-permute-start(bf16[1,8,64,1408]{3,2,1,0:T(8,128)(2,1)} %bitcast.75), channel_id=1, source_target_pairs={{0,8},{1,9},{2,10},{3,11},{4,12},{5,13},{6,14},{7,15},{8,0},{9,1},... | collective-permute-start | bytes 4325384 | tf_op jit(solution)/shard_map/ppermute | solution.py:45
  193.4 95.2 %collective-permute-start.23 = (bf16[1,176,2048]{2,1,0:T(8,128)(2,1)S(1)}, bf16[1,176,2048]{2,1,0:T(8,128)(2,1)S(1)}, u32[]{:S(2)}, u32[]{:S(2)}) collective-permute-start(bf16[1,176,2048]{2,1,0:T(8,128)(2,1)S(1)} %bitcast.360), channel_id=1, source_target_pairs={{0,8},{1,9},{2,10},{3,11},{4,12},{5,13},{6,14},{7,15},{8,0},{9,1},... | collective-permute-start | bytes 2162696 | tf_op jit(solution)/shard_map/ppermute | solution.py:45
  226.2 62.7 %collective-permute-start.9 = (f32[2,128,128]{2,1,0:T(8,128)}, f32[2,128,128]{2,1,0:T(8,128)S(1)}, u32[]{:S(2)}, u32[]{:S(2)}) collective-permute-start(f32[2,128,128]{2,1,0:T(8,128)} %get-tuple-element.51), channel_id=1, source_target_pairs={{0,8},{1,9},{2,10},{3,11},{4,12},{5,13},{6,14},{7,15},{16,24},{17,... | collective-permute-start | bytes 393224 | tf_op jit(solution)/shard_map/ppermute | solution.py:743
  269.3 51.8 %collective-permute-start.22 = (bf16[1,2,8,64,1408]{4,3,2,1,0:T(8,128)(2,1)}, bf16[1,2,8,64,1408]{4,3,2,1,0:T(8,128)(2,1)}, u32[]{:S(2)}, u32[]{:S(2)}) collective-permute-start(bf16[1,2,8,64,1408]{4,3,2,1,0:T(8,128)(2,1)} %maximum_bitcast_fusion), channel_id=1, source_target_pairs={{0,16},{16,0},{1,17},{17,1},{2,18},{18,2},{3,19},{19,3},{4,20},{20... | collective-permute-start | bytes 8650760 | tf_op jit(solution)/shard_map/ppermute | solution.py:45
  275.6 54.1 %collective-permute-start.11 = (bf16[1024,2048]{1,0:T(8,128)(2,1)}, bf16[1024,2048]{1,0:T(8,128)(2,1)}, u32[]{:S(2)}, u32[]{:S(2)}) collective-permute-start(bf16[1024,2048]{1,0:T(8,128)(2,1)} %bitcast.51), channel_id=1, source_target_pairs={{0,16},{16,0},{1,17},{17,1},{2,18},{18,2},{3,19},{19,3},{4,20},{20... | collective-permute-start | bytes 12582920 | tf_op jit(solution)/shard_map/ppermute | solution.py:45
  288.8 30.1 %collective-permute-start.24 = (bf16[2,176,2048]{2,1,0:T(8,128)(2,1)S(1)}, bf16[2,176,2048]{2,1,0:T(8,128)(2,1)S(1)}, u32[]{:S(2)}, u32[]{:S(2)}) collective-permute-start(bf16[2,176,2048]{2,1,0:T(8,128)(2,1)S(1)} %broadcast_select_fusion.7), channel_id=1, source_target_pairs={{0,16},{16,0},{1,17},{17,1},{2,18},{18,2},{3,19},{19,3},{4,20},{20... | collective-permute-start | bytes 4325384 | tf_op jit(solution)/shard_map/ppermute | solution.py:45
  300.8 15.6 %all-to-all-start.2 = ((bf16[8,128,256]{2,1,0:T(8,128)(2,1)}), bf16[8,128,256]{2,1,0:T(8,128)(2,1)S(1)}, u32[]{:S(2)}, u32[]{:S(2)}) async-start(bf16[8,128,256]{2,1,0:T(8,128)(2,1)} %bitcast.369), calls=%async_computation.2 | async-start | bytes 1048576 | tf_op jit(solution)/shard_map/all_to_all | solution.py:121
  334.1 5.4 collective-permute-start.15
  335.4 10.1 %collective-permute-start.18 = (bf16[1,1,1,128,768]{3,4,2,1,0:T(8,128)(2,1)}, bf16[1,1,1,128,768]{3,4,2,1,0:T(8,128)(2,1)}, u32[]{:S(2)}, u32[]{:S(2)}) collective-permute-start(bf16[1,1,1,128,768]{3,4,2,1,0:T(8,128)(2,1)} %get-tuple-element.99), channel_id=1, source_target_pairs={{0,4},{1,5},{2,6},{3,7},{4,0},{5,1},{6,2},{7,3},{8,12},{9,13},{10,... | collective-permute-start | bytes 589832 | tf_op jit(solution)/shard_map/ppermute | solution.py:45
  337.0 5.4 collective-permute-start.12
  339.7 8.6 %collective-permute-start.16 = (bf16[1,2,1,128,640]{4,3,1,2,0:T(8,128)(2,1)S(1)}, bf16[1,2,1,128,640]{4,3,1,2,0:T(8,128)(2,1)S(1)}, u32[]{:S(2)}, u32[]{:S(2)}) collective-permute-start(bf16[1,2,1,128,640]{4,3,1,2,0:T(8,128)(2,1)S(1)} %broadcast_select_fusion.22), channel_id=1, source_target_pairs={{0,4},{1,5},{2,6},{3,7},{4,0},{5,1},{6,2},{7,3},{8,12},{9,13},{10,... | collective-permute-start | bytes 983048 | tf_op jit(solution)/shard_map/ppermute | solution.py:45
  343.2 16.9 %collective-permute-start.13 = (bf16[1,1,2,128,640]{4,3,2,1,0:T(8,128)(2,1)S(1)}, bf16[1,1,2,128,640]{4,3,2,1,0:T(8,128)(2,1)S(1)}, u32[]{:S(2)}, u32[]{:S(2)}) collective-permute-start(bf16[1,1,2,128,640]{4,3,2,1,0:T(8,128)(2,1)S(1)} %broadcast_select_fusion.24), channel_id=1, source_target_pairs={{0,2},{1,3},{2,0},{3,1},{4,6},{5,7},{6,4},{7,5},{8,10},{9,11},{10,... | collective-permute-start | bytes 983048 | tf_op jit(solution)/shard_map/ppermute | solution.py:45
  346.7 12.1 %collective-permute-start.19 = (bf16[2,1,1,128,768]{4,3,0,2,1:T(8,128)(2,1)S(1)}, bf16[2,1,1,128,768]{4,3,0,2,1:T(8,128)(2,1)S(1)}, u32[]{:S(2)}, u32[]{:S(2)}) collective-permute-start(bf16[2,1,1,128,768]{4,3,0,2,1:T(8,128)(2,1)S(1)} %broadcast_select_fusion.20), channel_id=1, source_target_pairs={{0,1},{1,0},{2,3},{3,2},{4,5},{5,4},{6,7},{7,6},{8,9},{9,8},{10,11... | collective-permute-start | bytes 1179656 | tf_op jit(solution)/shard_map/ppermute | solution.py:45
  348.5 20.7 %collective-permute-start.17 = (bf16[2,2,1,128,640]{4,3,1,0,2:T(8,128)(2,1)S(1)}, bf16[2,2,1,128,640]{4,3,1,0,2:T(8,128)(2,1)S(1)}, u32[]{:S(2)}, u32[]{:S(2)}) collective-permute-start(bf16[2,2,1,128,640]{4,3,1,0,2:T(8,128)(2,1)S(1)} %broadcast_select_fusion.16), channel_id=1, source_target_pairs={{0,1},{1,0},{2,3},{3,2},{4,5},{5,4},{6,7},{7,6},{8,9},{9,8},{10,11... | collective-permute-start | bytes 1966088 | tf_op jit(solution)/shard_map/ppermute | solution.py:45
  359.5 12.6 %collective-permute-start.20 = (bf16[2,1,2,128,768]{4,3,2,0,1:T(8,128)(2,1)S(1)}, bf16[2,1,2,128,768]{4,3,2,0,1:T(8,128)(2,1)S(1)}, u32[]{:S(2)}, u32[]{:S(2)}) collective-permute-start(bf16[2,1,2,128,768]{4,3,2,0,1:T(8,128)(2,1)S(1)} %broadcast_select_fusion.14), channel_id=1, source_target_pairs={{0,2},{1,3},{2,0},{3,1},{4,6},{5,7},{6,4},{7,5},{8,10},{9,11},{10,... | collective-permute-start | bytes 2359304 | tf_op jit(solution)/shard_map/ppermute | solution.py:45
  360.3 10.7 %collective-permute-start.14 = (bf16[1,2,2,128,640]{4,3,2,1,0:T(8,128)(2,1)S(1)}, bf16[1,2,2,128,640]{4,3,2,1,0:T(8,128)(2,1)S(1)}, u32[]{:S(2)}, u32[]{:S(2)}) collective-permute-start(bf16[1,2,2,128,640]{4,3,2,1,0:T(8,128)(2,1)S(1)} %broadcast_select_fusion.18), channel_id=1, source_target_pairs={{0,4},{1,5},{2,6},{3,7},{4,0},{5,1},{6,2},{7,3},{8,12},{9,13},{10,... | collective-permute-start | bytes 1966088 | tf_op jit(solution)/shard_map/ppermute | solution.py:45
  384.9 32.2 %copy-start.24 = (bf16[1024,704]{1,0:T(8,128)(2,1)}, bf16[1024,704]{1,0:T(8,128)(2,1)S(1)}, u32[]{:S(2)}) copy-start(bf16[1024,704]{1,0:T(8,128)(2,1)S(1)} %get-tuple-element.83.refs_0_) | copy-start | bytes 4325380
  395.6 50.2 %all-to-all-start.5 = ((bf16[8,128,2048]{2,1,0:T(8,128)(2,1)}), bf16[8,128,2048]{2,1,0:T(8,128)(2,1)}, u32[]{:S(2)}, u32[]{:S(2)}) async-start(bf16[8,128,2048]{2,1,0:T(8,128)(2,1)} %bitcast.356), calls=%async_computation.5 | async-start | bytes 8388608 | tf_op jit(solution)/shard_map/all_to_all | solution.py:121
  417.1 17.0 %collective-permute-start.25 = (bf16[1,2,8,64,1408]{4,3,2,1,0:T(8,128)(2,1)}, bf16[1,2,8,64,1408]{4,3,2,1,0:T(8,128)(2,1)}, u32[]{:S(2)}, u32[]{:S(2)}) collective-permute-start(bf16[1,2,8,64,1408]{4,3,2,1,0:T(8,128)(2,1)} %bitcast.86), channel_id=1, source_target_pairs={{0,16},{16,0},{1,17},{17,1},{2,18},{18,2},{3,19},{19,3},{4,20},{20... | collective-permute-start | bytes 8650760 | tf_op jit(solution)/shard_map/ppermute | solution.py:45
  428.6 3.6 collective-permute-start.26
  479.8 85.2 %all-to-all-start.7 = ((bf16[8,128,2048]{2,1,0:T(8,128)(2,1)}), bf16[8,128,2048]{2,1,0:T(8,128)(2,1)}, u32[]{:S(2)}, u32[]{:S(2)}) async-start(bf16[8,128,2048]{2,1,0:T(8,128)(2,1)} %broadcast_in_dim.548), calls=%async_computation.7 | async-start | bytes 8388608 | tf_op jit(solution)/shard_map/all_to_all | solution.py:121
  497.1 9.9 %collective-permute-start.27 = (f32[2,128,128]{2,1,0:T(8,128)}, f32[2,128,128]{2,1,0:T(8,128)}, u32[]{:S(2)}, u32[]{:S(2)}) collective-permute-start(f32[2,128,128]{2,1,0:T(8,128)} %get-tuple-element.68), channel_id=1, source_target_pairs={{8,0},{9,1},{10,2},{11,3},{12,4},{13,5},{14,6},{15,7},{24,16},{25,... | collective-permute-start | bytes 393224 | tf_op jit(solution)/shard_map/ppermute | solution.py:806
  536.0 100.1 %collective-permute-start.34 = (bf16[8,768]{1,0:T(8,128)(2,1)}, bf16[8,768]{1,0:T(8,128)(2,1)}, u32[]{:S(2)}, u32[]{:S(2)}) collective-permute-start(bf16[8,768]{1,0:T(8,128)(2,1)} %convert_element_type.464), channel_id=1, source_target_pairs={{8,0},{9,1},{10,2},{11,3},{12,4},{13,5},{14,6},{15,7},{24,16},{25,... | collective-permute-start | bytes 36872 | tf_op jit(solution)/shard_map/ppermute | solution.py:817
  543.5 67.7 %collective-permute-start.31 = (bf16[2,1,2,128,1024]{4,3,2,1,0:T(8,128)(2,1)}, bf16[2,1,2,128,1024]{4,3,2,1,0:T(8,128)(2,1)}, u32[]{:S(2)}, u32[]{:S(2)}) collective-permute-start(bf16[2,1,2,128,1024]{4,3,2,1,0:T(8,128)(2,1)} %dynamic-slice_convert_fusion.3), channel_id=1, source_target_pairs={{0,2},{1,3},{2,0},{3,1},{4,6},{5,7},{6,4},{7,5},{8,10},{9,11},{10,... | collective-permute-start | bytes 3145736 | tf_op jit(solution)/shard_map/ppermute | solution.py:45
  550.2 64.6 %collective-permute-start.28 = (bf16[2,2,1,128,1024]{4,3,2,1,0:T(8,128)(2,1)}, bf16[2,2,1,128,1024]{4,3,2,1,0:T(8,128)(2,1)}, u32[]{:S(2)}, u32[]{:S(2)}) collective-permute-start(bf16[2,2,1,128,1024]{4,3,2,1,0:T(8,128)(2,1)} %dynamic-slice_convert_fusion.4), channel_id=1, source_target_pairs={{0,1},{1,0},{2,3},{3,2},{4,5},{5,4},{6,7},{7,6},{8,9},{9,8},{10,11... | collective-permute-start | bytes 3145736 | tf_op jit(solution)/shard_map/ppermute | solution.py:45
  551.7 68.5 %collective-permute-start.42 = (bf16[1,8,64,1408]{3,2,1,0:T(8,128)(2,1)}, bf16[1,8,64,1408]{3,2,1,0:T(8,128)(2,1)S(1)}, u32[]{:S(2)}, u32[]{:S(2)}) collective-permute-start(bf16[1,8,64,1408]{3,2,1,0:T(8,128)(2,1)} %shard_map.245), channel_id=1, source_target_pairs={{0,8},{1,9},{2,10},{3,11},{4,12},{5,13},{6,14},{7,15},{8,0},{9,1},... | collective-permute-start | bytes 4325384 | tf_op jit(solution)/shard_map/ppermute | solution.py:45
  565.0 149.7 %all-to-all-start.9 = ((f32[32,1,768]{2,1,0:T(1,128)}), f32[32,1,768]{2,1,0:T(1,128)}, u32[]{:S(2)}, u32[]{:S(2)}) async-start(f32[32,1,768]{2,1,0:T(1,128)} %all_to_all.52), calls=%async_computation.9 | async-start | bytes 196608 | tf_op jit(solution)/shard_map/all_to_all | solution.py:131
  610.9 26.8 %collective-permute-start.35 = (bf16[1,2,8,64,1152]{4,3,2,1,0:T(8,128)(2,1)S(1)}, bf16[1,2,8,64,1152]{4,3,2,1,0:T(8,128)(2,1)S(1)}, u32[]{:S(2)}, u32[]{:S(2)}) collective-permute-start(bf16[1,2,8,64,1152]{4,3,2,1,0:T(8,128)(2,1)S(1)} %bitcast.366), channel_id=1, source_target_pairs={{0,16},{16,0},{1,17},{17,1},{2,18},{18,2},{3,19},{19,3},{4,20},{20... | collective-permute-start | bytes 7077896 | tf_op jit(solution)/shard_map/ppermute | solution.py:45
  613.1 14.7 %collective-permute-start.32 = (bf16[2,1,1,128,1024]{4,3,2,1,0:T(8,128)(2,1)S(1)}, bf16[2,1,1,128,1024]{4,3,2,1,0:T(8,128)(2,1)S(1)}, u32[]{:S(2)}, u32[]{:S(2)}) collective-permute-start(bf16[2,1,1,128,1024]{4,3,2,1,0:T(8,128)(2,1)S(1)} %dynamic-slice_convert_fusion.9), channel_id=1, source_target_pairs={{0,1},{1,0},{2,3},{3,2},{4,5},{5,4},{6,7},{7,6},{8,9},{9,8},{10,11... | collective-permute-start | bytes 1572872 | tf_op jit(solution)/shard_map/ppermute | solution.py:45
  618.6 99.7 %collective-permute-start.29 = (bf16[1,2,1,128,1024]{4,3,2,1,0:T(8,128)(2,1)}, bf16[1,2,1,128,1024]{4,3,2,1,0:T(8,128)(2,1)}, u32[]{:S(2)}, u32[]{:S(2)}) collective-permute-start(bf16[1,2,1,128,1024]{4,3,2,1,0:T(8,128)(2,1)} %dynamic-slice_convert_fusion.10), channel_id=1, source_target_pairs={{0,4},{1,5},{2,6},{3,7},{4,0},{5,1},{6,2},{7,3},{8,12},{9,13},{10,... | collective-permute-start | bytes 1572872 | tf_op jit(solution)/shard_map/ppermute | solution.py:45
  636.0 20.3 %collective-permute-start.43 = (bf16[1,2,64,2048]{3,2,1,0:T(8,128)(2,1)}, bf16[1,2,64,2048]{3,2,1,0:T(8,128)(2,1)}, u32[]{:S(2)}, u32[]{:S(2)}) collective-permute-start(bf16[1,2,64,2048]{3,2,1,0:T(8,128)(2,1)} %dynamic-slice_convert_fusion.6), channel_id=1, source_target_pairs={{0,16},{16,0},{1,17},{17,1},{2,18},{18,2},{3,19},{19,3},{4,20},{20... | collective-permute-start | bytes 1572872 | tf_op jit(solution)/shard_map/ppermute | solution.py:45
  647.1 25.5 %collective-permute-start.39 = (bf16[2,1,2,128,1024]{4,3,2,1,0:T(8,128)(2,1)}, bf16[2,1,2,128,1024]{4,3,2,1,0:T(8,128)(2,1)}, u32[]{:S(2)}, u32[]{:S(2)}) collective-permute-start(bf16[2,1,2,128,1024]{4,3,2,1,0:T(8,128)(2,1)} %dynamic-slice_convert_fusion.1), channel_id=1, source_target_pairs={{0,2},{1,3},{2,0},{3,1},{4,6},{5,7},{6,4},{7,5},{8,10},{9,11},{10,... | collective-permute-start | bytes 3145736 | tf_op jit(solution)/shard_map/ppermute | solution.py:45
  654.9 26.4 %collective-permute-start.36 = (bf16[2,2,1,128,1024]{4,3,2,1,0:T(8,128)(2,1)}, bf16[2,2,1,128,1024]{4,3,2,1,0:T(8,128)(2,1)}, u32[]{:S(2)}, u32[]{:S(2)}) collective-permute-start(bf16[2,2,1,128,1024]{4,3,2,1,0:T(8,128)(2,1)} %dynamic-slice_convert_fusion.2), channel_id=1, source_target_pairs={{0,1},{1,0},{2,3},{3,2},{4,5},{5,4},{6,7},{7,6},{8,9},{9,8},{10,11... | collective-permute-start | bytes 3145736 | tf_op jit(solution)/shard_map/ppermute | solution.py:45
  659.9 25.1 %collective-permute-start.44 = (bf16[1,1,64,2048]{3,2,1,0:T(8,128)(2,1)}, bf16[1,1,64,2048]{3,2,1,0:T(8,128)(2,1)S(1)}, u32[]{:S(2)}, u32[]{:S(2)}) collective-permute-start(bf16[1,1,64,2048]{3,2,1,0:T(8,128)(2,1)} %shard_map.246), channel_id=1, source_target_pairs={{0,8},{1,9},{2,10},{3,11},{4,12},{5,13},{6,14},{7,15},{8,0},{9,1},... | collective-permute-start | bytes 786440 | tf_op jit(solution)/shard_map/ppermute | solution.py:45
  675.0 16.2 %collective-permute-start.40 = (bf16[2,1,1,128,1024]{4,3,2,1,0:T(8,128)(2,1)S(1)}, bf16[2,1,1,128,1024]{4,3,2,1,0:T(8,128)(2,1)S(1)}, u32[]{:S(2)}, u32[]{:S(2)}) collective-permute-start(bf16[2,1,1,128,1024]{4,3,2,1,0:T(8,128)(2,1)S(1)} %dynamic-slice_convert_fusion.7), channel_id=1, source_target_pairs={{0,1},{1,0},{2,3},{3,2},{4,5},{5,4},{6,7},{7,6},{8,9},{9,8},{10,11... | collective-permute-start | bytes 1572872 | tf_op jit(solution)/shard_map/ppermute | solution.py:45
  683.0 13.4 %collective-permute-start.37 = (bf16[1,2,1,128,1024]{4,3,2,1,0:T(8,128)(2,1)S(1)}, bf16[1,2,1,128,1024]{4,3,2,1,0:T(8,128)(2,1)S(1)}, u32[]{:S(2)}, u32[]{:S(2)}) collective-permute-start(bf16[1,2,1,128,1024]{4,3,2,1,0:T(8,128)(2,1)S(1)} %dynamic-slice_convert_fusion.8), channel_id=1, source_target_pairs={{0,4},{1,5},{2,6},{3,7},{4,0},{5,1},{6,2},{7,3},{8,12},{9,13},{10,... | collective-permute-start | bytes 1572872 | tf_op jit(solution)/shard_map/ppermute | solution.py:45
  692.1 12.0 %collective-permute-start.41 = (bf16[1,1,1,128,1024]{4,3,2,1,0:T(8,128)(2,1)}, bf16[1,1,1,128,1024]{4,3,2,1,0:T(8,128)(2,1)S(1)}, u32[]{:S(2)}, u32[]{:S(2)}) collective-permute-start(bf16[1,1,1,128,1024]{4,3,2,1,0:T(8,128)(2,1)} %dynamic-slice_convert_fusion.12), channel_id=1, source_target_pairs={{0,4},{1,5},{2,6},{3,7},{4,0},{5,1},{6,2},{7,3},{8,12},{9,13},{10,... | collective-permute-start | bytes 786440 | tf_op jit(solution)/shard_map/ppermute | solution.py:45
  698.3 6.7 collective-permute-start.38
  702.0 57.4 %collective-permute-start.45 = (bf16[1,8,64,1152]{3,2,1,0:T(8,128)(2,1)}, bf16[1,8,64,1152]{3,2,1,0:T(8,128)(2,1)}, u32[]{:S(2)}, u32[]{:S(2)}) collective-permute-start(bf16[1,8,64,1152]{3,2,1,0:T(8,128)(2,1)} %shard_map.247), channel_id=1, source_target_pairs={{0,8},{1,9},{2,10},{3,11},{4,12},{5,13},{6,14},{7,15},{8,0},{9,1},... | collective-permute-start | bytes 3538952 | tf_op jit(solution)/shard_map/ppermute | solution.py:45
  712.9 23.5 %collective-permute-start.33 = (bf16[1,1,1,128,1024]{4,3,2,1,0:T(8,128)(2,1)}, bf16[1,1,1,128,1024]{4,3,2,1,0:T(8,128)(2,1)}, u32[]{:S(2)}, u32[]{:S(2)}) collective-permute-start(bf16[1,1,1,128,1024]{4,3,2,1,0:T(8,128)(2,1)} %dynamic-slice_convert_fusion.14), channel_id=1, source_target_pairs={{0,4},{1,5},{2,6},{3,7},{4,0},{5,1},{6,2},{7,3},{8,12},{9,13},{10,... | collective-permute-start | bytes 786440 | tf_op jit(solution)/shard_map/ppermute | solution.py:45
  714.7 58.8 %all-to-all-start.8 = ((bf16[8,64,1408]{2,1,0:T(8,128)(2,1)}), bf16[8,64,1408]{2,1,0:T(8,128)(2,1)S(1)}, u32[]{:S(2)}, u32[]{:S(2)}) async-start(bf16[8,64,1408]{2,1,0:T(8,128)(2,1)} %shard_map.248), calls=%async_computation.8 | async-start | bytes 2883584 | tf_op jit(solution)/shard_map/all_to_all | solution.py:121
  721.5 16.2 %collective-permute-start.30 = (bf16[1,1,1,128,1024]{4,3,2,1,0:T(8,128)(2,1)}, bf16[1,1,1,128,1024]{4,3,2,1,0:T(8,128)(2,1)}, u32[]{:S(2)}, u32[]{:S(2)}) collective-permute-start(bf16[1,1,1,128,1024]{4,3,2,1,0:T(8,128)(2,1)} %dynamic-slice_convert_fusion.15), channel_id=1, source_target_pairs={{0,2},{1,3},{2,0},{3,1},{4,6},{5,7},{6,4},{7,5},{8,10},{9,11},{10,... | collective-permute-start | bytes 786440 | tf_op jit(solution)/shard_map/ppermute | solution.py:45
  738.9 44.3 %collective-permute-start.46 = (bf16[64,2048]{1,0:T(8,128)(2,1)}, bf16[64,2048]{1,0:T(8,128)(2,1)}, u32[]{:S(2)}, u32[]{:S(2)}) collective-permute-start(bf16[64,2048]{1,0:T(8,128)(2,1)} %get-tuple-element.79), channel_id=1, source_target_pairs={{0,0},{1,4},{2,8},{3,12},{4,16},{5,20},{6,24},{7,28},{8,1},{9,5},{... | collective-permute-start | bytes 786440 | tf_op jit(solution)/shard_map/ppermute | solution.py:830
  774.5 41.6 %all-to-all-start.10 = ((bf16[8,64,1152]{2,1,0:T(8,128)(2,1)}), bf16[8,64,1152]{2,1,0:T(8,128)(2,1)}, u32[]{:S(2)}, u32[]{:S(2)}) async-start(bf16[8,64,1152]{2,1,0:T(8,128)(2,1)} %shard_map.249), calls=%async_computation.10 | async-start | bytes 2359296 | tf_op jit(solution)/shard_map/all_to_all | solution.py:121
  782.1 28.8 %collective-permute-start.47 = (bf16[1,1,176,2048]{3,2,1,0:T(8,128)(2,1)}, bf16[1,1,176,2048]{3,2,1,0:T(8,128)(2,1)}, u32[]{:S(2)}, u32[]{:S(2)}) collective-permute-start(bf16[1,1,176,2048]{3,2,1,0:T(8,128)(2,1)} %shard_map.250), channel_id=1, source_target_pairs={{0,8},{1,9},{2,10},{3,11},{4,12},{5,13},{6,14},{7,15},{8,0},{9,1},... | collective-permute-start | bytes 2162696 | tf_op jit(solution)/shard_map/ppermute | solution.py:45
  (112 other events, 784.7 us)
